TPU v7x, 128 devices: a whole 4x4x4 slice. The times are simulated.
128 devices in a mesh: dp: 16 (over z_lo, y, core), tensor: 8 (over z_hi, x).
Axes of the slice: x: 4, y: 4, z: 4 (z_hi: 2, z_lo: 2; z = z_hi * 2 + z_lo), core: 2. Of those that a mesh axis runs over, the one named last changes fastest.
Arguments:
- hidden: bfloat16 [32768, 1536], P(('dp', 'tensor')), may hold values from -6 to 6
- doc_ids: int32 [32768], P('dp'), may hold values from 0 to 2, as said below
- norm_gain: float32 [1536], replicated, may hold values from 0.1 to 1.9
- main_proj: bfloat16 [1536, 2, 3072], P('dp', None, 'tensor'), may hold values from -0.15625 to 0.15625
- step_proj: bfloat16 [1536, 48], P('dp', 'tensor'), may hold values from -0.15625 to 0.15625
- state_proj: bfloat16 [1536, 256], P('dp', 'tensor'), may hold values from -0.15625 to 0.15625
- conv_main: float32 [4, 3072], P(None, 'tensor'), may hold values from -3 to 3
- conv_main_bias: float32 [3072], P('tensor'), may hold values from -3 to 3
- conv_state: float32 [4, 256], P(None, 'tensor'), may hold values from -3 to 3
- conv_state_bias: float32 [256], P('tensor'), may hold values from -3 to 3
- step_bias: float32 [48], P('tensor'), may hold values from -6 to -2
- decay_log: float32 [48], P('tensor'), may hold values from 0 to 2.77
- skip_gain: float32 [48], P('tensor'), may hold values from 0.5 to 2
- gate_gain: float32 [3072], P('tensor'), may hold values from 0.1 to 1.9
- out_proj: bfloat16 [1536, 3072], P('dp', 'tensor'), may hold values from -0.109375 to 0.109375
- cotangent: bfloat16 [32768, 1536], P(('dp', 'tensor')), may hold values from -6 to 6
Outputs:
- mixed: bfloat16 [32768, 1536], P(('dp', 'tensor'))
- grad_hidden: float32 [32768, 1536], P(('dp', 'tensor'))
- grad_norm_gain: float32 [1536], replicated
- grad_main_proj: float32 [1536, 2, 3072], P('dp', None, 'tensor')
- grad_step_proj: float32 [1536, 48], P('dp', 'tensor')
- grad_state_proj: float32 [1536, 256], P('dp', 'tensor')
- grad_conv_main: float32 [4, 3072], P(None, 'tensor')
- grad_conv_main_bias: float32 [3072], P('tensor')
- grad_conv_state: float32 [4, 256], P(None, 'tensor')
- grad_conv_state_bias: float32 [256], P('tensor')
- grad_step_bias: float32 [48], P('tensor')
- grad_decay_log: float32 [48], P('tensor')
- grad_skip_gain: float32 [48], P('tensor')
- grad_gate_gain: float32 [3072], P('tensor')
- grad_out_proj: float32 [1536, 3072], P('dp', 'tensor')
Inputs may be any that keep to these rules, and one draw needn't show every extreme that they name: `doc_ids`: in each sequence (the 2048 tokens of one index of dp) the ids run from 0 to 2 in order, never falling, each id on 200 or more consecutive positions.
All inputs are finite; a program needn't handle non-finite values.
Results may differ from a plain program's by a relative error of at most 0.02.
Values may be sent and summed in bfloat16 or wider, within the bound.
A program may use at most 128 MiB of HBM per device.

v0:
```python
import jax
import jax.numpy as jnp
from jax import lax
from jax.sharding import PartitionSpec as P

BLOCK = 256


epsilon = 1e-05


def silu_slope(values):
    sigmoid_val = jax.nn.sigmoid(values)
    return sigmoid_val * (1.0 + values * (1.0 - sigmoid_val))


def causal_conv(values, kernel, bias_row, doc_row):
    length = values.shape[0]
    taps = kernel.shape[0]
    total = bias_row[None, :] + kernel[taps - 1][None, :] * values
    for offset in range(1, taps):
        earlier = jnp.concatenate(
            [jnp.zeros((offset, values.shape[1]), values.dtype), values[: length - offset]], axis=0
        )
        earlier_doc = jnp.concatenate(
            [jnp.full((offset,), -1, jnp.int32), doc_row[: length - offset]]
        )
        linked = (earlier_doc == doc_row).astype(values.dtype)
        total = total + kernel[taps - 1 - offset][None, :] * earlier * linked[:, None]
    return total


def conv_backward(grad_out, values, kernel, doc_row):
    length = values.shape[0]
    taps = kernel.shape[0]
    grad_in = kernel[taps - 1][None, :] * grad_out
    kernel_rows = [None] * taps
    kernel_rows[taps - 1] = jnp.sum(grad_out * values, axis=0)
    for offset in range(1, taps):
        earlier = jnp.concatenate(
            [jnp.zeros((offset, values.shape[1]), values.dtype), values[: length - offset]], axis=0
        )
        earlier_doc = jnp.concatenate(
            [jnp.full((offset,), -1, jnp.int32), doc_row[: length - offset]]
        )
        linked = (earlier_doc == doc_row).astype(values.dtype)
        masked = grad_out * linked[:, None]
        kernel_rows[taps - 1 - offset] = jnp.sum(masked * earlier, axis=0)
        later_rows = jnp.concatenate(
            [masked[offset:], jnp.zeros((offset, values.shape[1]), values.dtype)], axis=0
        )
        grad_in = grad_in + kernel[taps - 1 - offset][None, :] * later_rows
    return (grad_in, jnp.stack(kernel_rows, axis=0), jnp.sum(grad_out, axis=0))


def block_terms(b_block, c_block, step_block, doc_block, doc_prev, decay_rate):
    block_len = doc_block.shape[0]
    cum_decay = jnp.cumsum(step_block * decay_rate[None, :], axis=0)
    scores = lax.dot_general(
        c_block, b_block, (((1,), (1,)), ((), ())), preferred_element_type=jnp.float32
    )
    row_pos = lax.broadcasted_iota(jnp.int32, (block_len, block_len), 0)
    col_pos = lax.broadcasted_iota(jnp.int32, (block_len, block_len), 1)
    linked = (doc_block[:, None] == doc_block[None, :]) & (row_pos >= col_pos)
    cum_heads = cum_decay.T
    spread = jnp.where(linked[None], cum_heads[:, :, None] - cum_heads[:, None, :], -10000.0)
    decay_mat = jnp.exp(spread) * linked[None].astype(jnp.float32)
    decay_step = decay_mat * step_block.T[:, None, :]
    mix_exact = scores[None] * decay_step
    cum_end = cum_decay[block_len - 1]
    end_link = (doc_block == doc_block[block_len - 1]).astype(jnp.float32)
    tail_decay = jnp.exp(cum_end[None, :] - cum_decay) * end_link[:, None]
    weight = tail_decay * step_block
    enter_decay = jnp.exp(cum_decay) * (doc_block == doc_prev).astype(jnp.float32)[:, None]
    keep_decay = jnp.exp(cum_end) * (doc_block[block_len - 1] == doc_prev).astype(jnp.float32)
    return (scores, decay_mat, decay_step, mix_exact, tail_decay, weight, enter_decay, keep_decay)


def block_forward(state_in, block_in, decay_rate, skip_gain):
    x_block, b_block, c_block, step_block, doc_block, doc_prev = block_in
    terms = block_terms(b_block, c_block, step_block, doc_block, doc_prev, decay_rate)
    scores, decay_mat, decay_step, mix_exact, tail_decay, weight, enter_decay, keep_decay = terms
    mixing = mix_exact.astype(jnp.bfloat16)
    y_intra = jnp.einsum("hij,jhp->ihp", mixing, x_block, preferred_element_type=jnp.float32)
    state_low = state_in.astype(jnp.bfloat16)
    carried = jnp.einsum("in,hnp->ihp", c_block, state_low, preferred_element_type=jnp.float32)
    scaled = (weight.T[:, :, None] * b_block.astype(jnp.float32)[None]).astype(jnp.bfloat16)
    update = jnp.einsum("hjn,jhp->hnp", scaled, x_block, preferred_element_type=jnp.float32)
    state_out = keep_decay[:, None, None] * state_in + update
    y_block = (
        y_intra
        + carried * enter_decay[:, :, None]
        + skip_gain[None, :, None] * x_block.astype(jnp.float32)
    )
    return (state_out, (y_block, state_in))


def block_backward(grad_state, block_in, decay_rate, skip_gain):
    x_block, b_block, c_block, step_block, doc_block, doc_prev, state_in, dy_block = block_in
    block_len = doc_block.shape[0]
    terms = block_terms(b_block, c_block, step_block, doc_block, doc_prev, decay_rate)
    scores, decay_mat, decay_step, mix_exact, tail_decay, weight, enter_decay, keep_decay = terms
    mixing = mix_exact.astype(jnp.bfloat16)
    dy_float = dy_block.astype(jnp.float32)
    x_float = x_block.astype(jnp.float32)
    b_float = b_block.astype(jnp.float32)
    grad_mix = jnp.einsum("ihp,jhp->hij", dy_block, x_block, preferred_element_type=jnp.float32)
    grad_x = jnp.einsum("hij,ihp->jhp", mixing, dy_block, preferred_element_type=jnp.float32)
    grad_x = grad_x + skip_gain[None, :, None] * dy_float
    grad_scores = (grad_mix * decay_step).astype(jnp.bfloat16)
    grad_c = jnp.einsum("hij,jn->in", grad_scores, b_block, preferred_element_type=jnp.float32)
    grad_b = jnp.einsum("hij,in->jn", grad_scores, c_block, preferred_element_type=jnp.float32)
    pull_mat = grad_mix * mix_exact
    grad_cum = (jnp.sum(pull_mat, axis=2) - jnp.sum(pull_mat, axis=1)).T
    grad_step = jnp.sum(grad_mix * scores[None] * decay_mat, axis=1).T
    state_low = state_in.astype(jnp.bfloat16)
    carried = jnp.einsum("in,hnp->ihp", c_block, state_low, preferred_element_type=jnp.float32)
    grad_carried = (dy_float * enter_decay[:, :, None]).astype(jnp.bfloat16)
    grad_cum = grad_cum + jnp.sum(dy_float * carried, axis=2) * enter_decay
    grad_c = grad_c + jnp.einsum(
        "ihp,hnp->in", grad_carried, state_low, preferred_element_type=jnp.float32
    )
    grad_before = jnp.einsum(
        "in,ihp->hnp", c_block, grad_carried, preferred_element_type=jnp.float32
    )
    grad_update = grad_state.astype(jnp.bfloat16)
    scaled = (weight.T[:, :, None] * b_float[None]).astype(jnp.bfloat16)
    grad_scaled = jnp.einsum(
        "jhp,hnp->hjn", x_block, grad_update, preferred_element_type=jnp.float32
    )
    grad_x = grad_x + jnp.einsum(
        "hjn,hnp->jhp", scaled, grad_update, preferred_element_type=jnp.float32
    )
    grad_b = grad_b + jnp.sum(grad_scaled * weight.T[:, :, None], axis=0)
    grad_weight = jnp.sum(grad_scaled * b_float[None], axis=2).T
    weight_pull = grad_weight * weight
    grad_keep = jnp.sum(grad_state * state_in, axis=(1, 2))
    grad_end = jnp.sum(weight_pull, axis=0) + grad_keep * keep_decay
    last_row = (lax.broadcasted_iota(jnp.int32, (block_len, 1), 0) == block_len - 1).astype(
        jnp.float32
    )
    grad_cum = grad_cum - weight_pull + last_row * grad_end[None, :]
    grad_step = grad_step + grad_weight * tail_decay
    grad_log = jnp.flip(jnp.cumsum(jnp.flip(grad_cum, 0), axis=0), 0)
    grad_step = grad_step + grad_log * decay_rate[None, :]
    grad_rate = jnp.sum(grad_log * step_block, axis=0)
    grad_skip = jnp.sum(dy_float * x_float, axis=(0, 2))
    carry_out = grad_before + keep_decay[:, None, None] * grad_state
    return (carry_out, (grad_x, grad_b, grad_c, grad_step, grad_rate, grad_skip))


def per_device(
    hidden,
    doc_ids,
    norm_gain,
    main_proj,
    step_proj,
    state_proj,
    conv_main,
    conv_main_bias,
    conv_state,
    conv_state_bias,
    step_bias,
    decay_log,
    skip_gain,
    gate_gain,
    out_proj,
    cotangent,
):
    tensor_count = lax.axis_size("tensor")
    tensor_rank = lax.axis_index("tensor")
    hidden_float = hidden.astype(jnp.float32)
    inv_rms = lax.rsqrt(jnp.mean(hidden_float * hidden_float, axis=1, keepdims=True) + epsilon)
    norm_rows = hidden_float * inv_rms
    normed_own = (norm_rows * norm_gain[None, :]).astype(jnp.bfloat16)
    full_main, full_step, full_state = (
        lax.all_gather(main_proj, "dp", axis=0, tiled=True),
        lax.all_gather(step_proj, "dp", axis=0, tiled=True),
        lax.all_gather(state_proj, "dp", axis=0, tiled=True),
    )
    normed = lax.all_gather(normed_own, "tensor", axis=0, tiled=True)
    length = normed.shape[0]
    main_raw = jnp.einsum("td,dkc->tkc", normed, full_main, preferred_element_type=jnp.float32)
    step_raw = jnp.dot(normed, full_step, preferred_element_type=jnp.float32)
    state_raw = jnp.dot(normed, full_state, preferred_element_type=jnp.float32)
    gate_in = main_raw[:, 0, :]
    x_raw = main_raw[:, 1, :]
    x_pre = causal_conv(x_raw, conv_main, conv_main_bias, doc_ids)
    x_act = jax.nn.silu(x_pre).astype(jnp.bfloat16)
    state_pre = causal_conv(state_raw, conv_state, conv_state_bias, doc_ids)
    state_own = jax.nn.silu(state_pre).astype(jnp.bfloat16)
    state_act = lax.all_gather(state_own, "tensor", axis=1, tiled=True)
    state_width = state_act.shape[1] // 2
    step_in = step_raw + step_bias[None, :]
    step_size = jax.nn.softplus(step_in)
    decay_rate = -jnp.exp(decay_log)
    head_count = step_size.shape[1]
    head_dim = x_act.shape[1] // head_count
    block_count = length // BLOCK
    doc_blocks = doc_ids.reshape(block_count, BLOCK)
    doc_before = jnp.concatenate([jnp.full((1,), -1, jnp.int32), doc_blocks[:-1, -1]])
    x_blocks = x_act.reshape(block_count, BLOCK, head_count, head_dim)
    b_blocks = state_act[:, :state_width].reshape(block_count, BLOCK, state_width)
    c_blocks = state_act[:, state_width:].reshape(block_count, BLOCK, state_width)
    step_blocks = step_size.reshape(block_count, BLOCK, head_count)
    zero_state = jnp.zeros((head_count, state_width, head_dim), jnp.float32)

    def forward_step(state_in, block_in):
        return block_forward(state_in, block_in, decay_rate, skip_gain)

    _, (y_blocks, states_before) = lax.scan(
        forward_step,
        zero_state,
        (x_blocks, b_blocks, c_blocks, step_blocks, doc_blocks, doc_before),
    )
    y_ssd = y_blocks.reshape(length, head_count * head_dim)
    gate_act = jax.nn.silu(gate_in)
    gated = y_ssd * gate_act
    channels = gated.shape[1] * tensor_count
    square_sum = lax.psum(jnp.sum(gated * gated, axis=1), "tensor")
    gate_inv = lax.rsqrt(square_sum / channels + epsilon)[:, None]
    gate_hat = gated * gate_inv
    gate_out = (gate_hat * gate_gain[None, :]).astype(jnp.bfloat16)
    full_out = lax.all_gather(out_proj, "dp", axis=0, tiled=True)
    part_rows = gate_out
    branch_out = lax.psum_scatter(
        lax.dot_general(
            part_rows, full_out, (((1,), (1,)), ((), ())), preferred_element_type=jnp.float32
        ).astype(jnp.bfloat16),
        "tensor",
        scatter_dimension=0,
        tiled=True,
    ).astype(jnp.float32)
    mixed = (hidden_float + branch_out).astype(jnp.bfloat16)
    piece_rows = lax.all_gather(cotangent, "tensor", axis=0, tiled=True)
    part_rows = gate_out
    grad_out_acc = lax.dot_general(
        piece_rows, part_rows, (((0,), (0,)), ((), ())), preferred_element_type=jnp.float32
    )
    grad_gate_acc = jnp.dot(piece_rows, full_out, preferred_element_type=jnp.float32)
    grad_gate_gain = jnp.sum(grad_gate_acc * gate_hat, axis=0)
    gate_dn = grad_gate_acc * gate_gain[None, :]
    inner_sum = lax.psum(jnp.sum(gate_dn * gated, axis=1), "tensor")
    grad_gated = gate_inv * gate_dn - gated * gate_inv**3 * (inner_sum / channels)[:, None]
    grad_y = (grad_gated * gate_act).astype(jnp.bfloat16)
    grad_gate_in = grad_gated * y_ssd * silu_slope(gate_in)
    dy_blocks = grad_y.reshape(block_count, BLOCK, head_count, head_dim)

    def backward_step(grad_state, block_in):
        return block_backward(grad_state, block_in, decay_rate, skip_gain)

    _, block_grads = lax.scan(
        backward_step,
        zero_state,
        (
            x_blocks,
            b_blocks,
            c_blocks,
            step_blocks,
            doc_blocks,
            doc_before,
            states_before,
            dy_blocks,
        ),
        reverse=True,
    )
    dx_blocks, db_blocks, dc_blocks, dstep_blocks, drate_blocks, dskip_blocks = block_grads
    grad_x_act = dx_blocks.reshape(length, head_count * head_dim)
    grad_state_act = jnp.concatenate(
        [db_blocks.reshape(length, state_width), dc_blocks.reshape(length, state_width)], axis=1
    )
    grad_state_own = lax.psum_scatter(grad_state_act, "tensor", scatter_dimension=1, tiled=True)
    grad_step = dstep_blocks.reshape(length, head_count)
    grad_decay_log = jnp.sum(drate_blocks, axis=0) * decay_rate
    grad_skip_gain = jnp.sum(dskip_blocks, axis=0)
    grad_step_in = grad_step * jax.nn.sigmoid(step_in)
    grad_step_bias = jnp.sum(grad_step_in, axis=0)
    grad_step_raw = grad_step_in.astype(jnp.bfloat16)
    grad_x_raw, grad_conv_main, grad_conv_main_bias = conv_backward(
        grad_x_act * silu_slope(x_pre), x_raw, conv_main, doc_ids
    )
    grad_state_pre, grad_conv_state, grad_conv_state_bias = conv_backward(
        grad_state_own * silu_slope(state_pre), state_raw, conv_state, doc_ids
    )
    grad_state_raw = grad_state_pre.astype(jnp.bfloat16)
    grad_main_raw = jnp.stack([grad_gate_in, grad_x_raw], axis=1).astype(jnp.bfloat16)
    grad_main_part = jnp.einsum(
        "td,tkc->dkc", normed, grad_main_raw, preferred_element_type=jnp.float32
    )
    grad_step_part = lax.dot_general(
        normed, grad_step_raw, (((0,), (0,)), ((), ())), preferred_element_type=jnp.float32
    )
    grad_state_part = lax.dot_general(
        normed, grad_state_raw, (((0,), (0,)), ((), ())), preferred_element_type=jnp.float32
    )
    total_rows = jnp.einsum(
        "tkc,dkc->td", grad_main_raw, full_main, preferred_element_type=jnp.float32
    )
    total_rows = total_rows + lax.dot_general(
        grad_step_raw, full_step, (((1,), (1,)), ((), ())), preferred_element_type=jnp.float32
    )
    grad_normed = lax.psum_scatter(
        (
            total_rows
            + lax.dot_general(
                grad_state_raw,
                full_state,
                (((1,), (1,)), ((), ())),
                preferred_element_type=jnp.float32,
            )
        ).astype(jnp.bfloat16),
        "tensor",
        scatter_dimension=0,
        tiled=True,
    ).astype(jnp.float32)
    grad_norm_part = jnp.sum(grad_normed * norm_rows, axis=0)
    norm_dn = grad_normed * norm_gain[None, :]
    grad_hidden = (
        cotangent.astype(jnp.float32)
        + inv_rms * norm_dn
        - norm_rows * inv_rms * jnp.mean(norm_dn * norm_rows, axis=1, keepdims=True)
    )
    grad_main_proj, grad_step_proj, grad_state_proj, grad_out_proj = (
        lax.psum_scatter(
            grad_main_part.astype(jnp.bfloat16), "dp", scatter_dimension=0, tiled=True
        ).astype(jnp.float32),
        lax.psum_scatter(
            grad_step_part.astype(jnp.bfloat16), "dp", scatter_dimension=0, tiled=True
        ).astype(jnp.float32),
        lax.psum_scatter(
            grad_state_part.astype(jnp.bfloat16), "dp", scatter_dimension=0, tiled=True
        ).astype(jnp.float32),
        lax.psum_scatter(
            grad_out_acc.astype(jnp.bfloat16), "dp", scatter_dimension=0, tiled=True
        ).astype(jnp.float32),
    )
    local_small = jnp.concatenate(
        [
            grad_conv_main.reshape(-1),
            grad_conv_main_bias,
            grad_conv_state.reshape(-1),
            grad_conv_state_bias,
            grad_step_bias,
            grad_decay_log,
            grad_skip_gain,
            grad_gate_gain,
        ]
    )
    placed = jnp.where(
        (jnp.arange(tensor_count) == tensor_rank)[:, None], local_small[None, :], 0.0
    )
    summed_small, grad_norm_gain = lax.psum((placed, grad_norm_part), ("dp", "tensor"))
    own_small = lax.dynamic_index_in_dim(summed_small, tensor_rank, 0, keepdims=False)
    extents = [
        conv_main.size,
        conv_main.shape[1],
        conv_state.size,
        conv_state.shape[1],
        step_bias.shape[0],
        step_bias.shape[0],
        step_bias.shape[0],
        gate_gain.shape[0],
    ]
    pieces_out = []
    position = 0
    for extent in extents:
        pieces_out.append(own_small[position : position + extent])
        position = position + extent
    return (
        mixed,
        grad_hidden,
        grad_norm_gain,
        grad_main_proj,
        grad_step_proj,
        grad_state_proj,
        pieces_out[0].reshape(conv_main.shape),
        pieces_out[1],
        pieces_out[2].reshape(conv_state.shape),
        pieces_out[3],
        pieces_out[4],
        pieces_out[5],
        pieces_out[6],
        pieces_out[7],
        grad_out_proj,
    )


def solution(mesh):
    placed = (
        P(("dp", "tensor"), None),
        P("dp"),
        P(),
        P("dp", None, "tensor"),
        P("dp", "tensor"),
        P("dp", "tensor"),
        P(None, "tensor"),
        P("tensor"),
        P(None, "tensor"),
        P("tensor"),
        P("tensor"),
        P("tensor"),
        P("tensor"),
        P("tensor"),
        P("dp", "tensor"),
        P(("dp", "tensor"), None),
    )
    return jax.shard_map(
        per_device,
        mesh=mesh,
        in_specs=placed,
        out_specs=(
            P(("dp", "tensor"), None),
            P(("dp", "tensor"), None),
            P(),
            P("dp", None, "tensor"),
            P("dp", "tensor"),
            P("dp", "tensor"),
            P(None, "tensor"),
            P("tensor"),
            P(None, "tensor"),
            P("tensor"),
            P("tensor"),
            P("tensor"),
            P("tensor"),
            P("tensor"),
            P("dp", "tensor"),
        ),
        check_vma=False,
    )
```

profile of v0, /device:TPU:0, one launch (start us, length us, event | category | flops | bytes accessed | tf_op | source)
XLA Modules:
  0.0 1472.0 jit_solution(11132966270429338952)
XLA Ops:
  8.7 2.3 fusion.139
  11.8 20.9 %all-gather.1 = bf16[16,96,32]{1,2,0:T(8,128)(2,1)S(1)} all-gather(bf16[1,96,32]{1,2,0:T(8,128)(2,1)S(1)} %bitcast.632), channel_id=1, replica_groups=mesh['dp'=16,'tensor'=8] {'dp'}, dimensions={0}, use_global_device_ids=true | all-gather | bytes 104448 | tf_op jit(solution)/shard_map/all_gather | solution.py:179
  33.2 70.1 %all-gather.8.cloned.1.call-done = bf16[2048,1536]{1,0:T(8,128)(2,1)} async-done(((bf16[256,1536]{1,0:T(8,128)(2,1)}), bf16[2048,1536]{1,0:T(8,128)(2,1)}) %all-gather.8.cloned.1.call-update) | async-done | bytes 6291472 | tf_op jit(solution)/shard_map/all_gather | solution.py:181
  103.3 4.7 fusion.162
  111.6 19.4 %all-gather = bf16[16,96,6]{1,2,0:T(8,128)(2,1)S(1)} all-gather(bf16[1,96,6]{1,2,0:T(8,128)(2,1)S(1)} %bitcast.637), channel_id=1, replica_groups=mesh['dp'=16,'tensor'=8] {'dp'}, dimensions={0}, use_global_device_ids=true | all-gather | bytes 19584 | tf_op jit(solution)/shard_map/all_gather | solution.py:178
  133.3 4.5 all-gather.12.cloned.1.call-done
  137.7 7.8 fusion.118
  151.2 4.4 multiply_convert_fusion.10
  160.8 2.4 copy.254
  163.3 5.0 copy.324
  168.3 5.1 compare_select_fusion
  173.4 15.0 %all-gather.10.cloned.1.call-done = bf16[2048,256]{0,1:T(8,128)(2,1)} async-done(((bf16[2048,32]{0,1:T(8,128)(2,1)}), bf16[2048,256]{0,1:T(8,128)(2,1)}) %all-gather.10.cloned.1.call-update) | async-done | bytes 1048592 | tf_op jit(solution)/shard_map/all_gather | solution.py:192
  193.3 184.8 %while.42 = (s32[]{:T(128)}, f32[6,128,64]{1,2,0:T(8,128)S(1)}, f32[8,256,6,64]{1,0,3,2:T(8,128)}, f32[8,6,128,64]{2,3,1,0:T(8,128)}, f32[8,256,6]{1,2,0:T(8,128...) while((s32[]{:T(128)}, f32[6,128,64]{1,2,0:T(8,128)S(1)}, ...), condition=%wide.region_4.5_spmd.clone, body=%wide.region_1.4_spmd.clone.sunk | while | flops 121430560 | bytes 6375891 | solution.py:211
  203.1 9.8 dynamic_update_slice.86
  226.1 9.9 dynamic_update_slice.86
  249.2 9.8 dynamic_update_slice.86
  272.3 9.8 dynamic_update_slice.86
  295.3 9.8 dynamic_update_slice.86
  318.4 9.8 dynamic_update_slice.86
  341.4 9.8 dynamic_update_slice.86
  364.4 9.8 dynamic_update_slice.86
  378.2 4.1 multiply_reduce_fusion.9
  383.7 2.3 copy.253
  386.0 21.4 %psum.28 = f32[2048]{0:T(1024)S(1)} all-reduce(f32[2048]{0:T(1024)S(1)} %bitcast.631), channel_id=1, replica_groups=mesh['dp'=16,'tensor'=8] {'tensor'}, use_global_device_ids=true, to_apply=%region_6.7 | all-reduce | flops 2048 | bytes 16384 | tf_op jit(solution)/shard_map/psum | solution.py:220
  407.5 12.4 multiply_reduce_fusion.3
  419.9 19.2 %psum.29 = f32[2048]{0:T(1024)S(1)} all-reduce(f32[2048]{0:T(1024)S(1)} %get-tuple-element.816), channel_id=1, replica_groups=mesh['dp'=16,'tensor'=8] {'tensor'}, use_global_device_ids=true, to_apply=%region_9.10 | all-reduce | flops 2048 | bytes 16384 | tf_op jit(solution)/shard_map/psum | solution.py:243
  439.2 6.2 fusion.146
  454.9 326.2 %while.43 = (s32[]{:T(128)}, f32[6,128,64]{1,2,0:T(8,128)S(1)}, f32[8,256,6,64]{1,0,3,2:T(8,128)}, f32[8,256,128]{2,1,0:T(8,128)}, f32[8,256,128]{2,1,0:T(8,128)...) while((s32[]{:T(128)}, f32[6,128,64]{1,2,0:T(8,128)S(1)}, ...), condition=%wide.region_26.27_spmd.clone, body=%wide.region_10.26_spmd.clone.sunk | while | flops 288919616 | bytes 11354347 | solution.py:252
  459.0 2.2 fusion.256
  479.0 9.8 dynamic_update_slice.90
  519.8 9.8 dynamic_update_slice.90
  560.6 9.8 dynamic_update_slice.90
  601.4 9.8 dynamic_update_slice.90
  642.1 9.8 dynamic_update_slice.90
  682.9 9.8 dynamic_update_slice.90
  723.6 9.8 dynamic_update_slice.90
  764.4 9.8 dynamic_update_slice.90
  781.0 2.6 copy.272
  783.6 2.5 copy.273
  786.1 3.2 pad_maximum_fusion.1
  789.4 3.0 copy.327
  792.5 3.6 copy.264
  797.1 3.9 convolution_convert_fusion.3
  802.4 7.7 fusion.130
  810.0 3.6 multiply_reduce_fusion.7
  813.6 2.6 copy.279
  816.3 6.3 fusion.157
  822.7 4.0 slice.304
  832.8 5.8 fusion.145
  838.6 26.7 %reduce-scatter.16.cloned.1.call-done = f32[2048,32]{0,1:T(8,128)} async-done(((f32[2048,256]{0,1:T(8,128)}), f32[2048,32]{0,1:T(8,128)}) %reduce-scatter.16.cloned.1.call-update) | async-done | bytes 262160 | tf_op jit(solution)/shard_map/reduce_scatter | solution.py:272
  868.6 4.1 convolution_convert_fusion.2
  873.7 9.4 fusion.120
  886.0 8.2 fusion.135
  894.2 9.0 fusion.115
  905.1 6.7 convolution_convert_fusion
  911.9 15.5 %reduce-scatter.22.cloned.1.call-done = bf16[96,6]{1,0:T(8,128)(2,1)} async-done(((bf16[1536,6]{1,0:T(8,128)(2,1)}), bf16[96,6]{1,0:T(8,128)(2,1)}) %reduce-scatter.22.cloned.1.call-update) | async-done | bytes 1168
  928.8 61.4 %reduce-scatter.26.cloned.1.call-done = bf16[96,384]{1,0:T(8,128)(2,1)} async-done(((bf16[1536,384]{1,0:T(8,128)(2,1)}), bf16[96,384]{1,0:T(8,128)(2,1)}) %reduce-scatter.26.cloned.1.call-update) | async-done | bytes 73744
  991.9 138.9 %all-reduce.16.cloned.1.call-done = f32[8,2482]{1,0:T(8,128)} async-done(((f32[8,2482]{1,0:T(8,128)}), f32[8,2482]{1,0:T(8,128)}) %all-reduce.16.cloned.1.call-update) | async-done | bytes 79440 | tf_op jit(solution)/shard_map/psum | solution.py:352
  1137.7 54.4 %reduce-scatter.24.cloned.1.call-done = bf16[96,32]{1,0:T(8,128)(2,1)} async-done(((bf16[1536,32]{1,0:T(8,128)(2,1)}), bf16[96,32]{1,0:T(8,128)(2,1)}) %reduce-scatter.24.cloned.1.call-update) | async-done | bytes 6160
  1193.5 63.5 %reduce-scatter.20.cloned.1.call-done = bf16[96,2,384]{2,0,1:T(8,128)(2,1)} async-done(((bf16[1536,2,384]{2,0,1:T(8,128)(2,1)}), bf16[96,2,384]{2,0,1:T(8,128)(2,1)}) %reduce-scatter.20.cloned.1.call-update) | async-done | bytes 147472 | tf_op jit(solution)/shard_map/reduce_scatter | solution.py:324
  1258.7 100.0 %reduce-scatter.18.cloned.1.call-done = bf16[256,1536]{1,0:T(8,128)(2,1)} async-done(((bf16[2048,1536]{1,0:T(8,128)(2,1)}), bf16[256,1536]{1,0:T(8,128)(2,1)}) %reduce-scatter.18.cloned.1.call-update) | async-done | bytes 786448 | tf_op jit(solution)/shard_map/reduce_scatter | solution.py:302
  1360.5 74.9 %psum.30 = f32[1536]{0:T(1024)} all-reduce(f32[1536]{0:T(1024)S(1)} %get-tuple-element.819), channel_id=1, replica_groups=mesh['dp'=16,'tensor'=8] {'dp','tensor'}, use_global_device_ids=true, to_apply=%region_31.32 | all-reduce | flops 1536 | bytes 12288 | tf_op jit(solution)/shard_map/psum | solution.py:352
  1435.4 26.3 %reduce-scatter.14.cloned.1.call-done = bf16[256,1536]{1,0:T(8,128)(2,1)} async-done(((bf16[2048,1536]{1,0:T(8,128)(2,1)}), bf16[256,1536]{1,0:T(8,128)(2,1)}) %reduce-scatter.14.cloned.1.call-update) | async-done | bytes 786448 | tf_op jit(solution)/shard_map/reduce_scatter | solution.py:226
  1461.7 3.5 fusion.138
  (936 shorter events, 395.9 us)
Async XLA Ops:
  7.2 25.7 %copy-start.70 = (f32[4,32]{1,0:T(4,128)S(1)}, f32[4,32]{1,0:T(4,128)}, u32[]{:S(2)}) copy-start(f32[4,32]{1,0:T(4,128)} %param.28) | copy-start | bytes 1540
  7.2 25.8 %copy-start.38 = (s32[2048]{0:T(1024)S(1)}, s32[2048]{0:T(1024)}, u32[]{:S(2)}) copy-start(s32[2048]{0:T(1024)} %param.21) | copy-start | bytes 24580
  7.2 96.0 %all-gather.8.cloned.1.call-start = ((), (), s32[]{:S(2)}) async-start(), calls=%async_computation.7 | async-start | bytes 7077888 | tf_op jit(solution)/shard_map/all_gather | solution.py:181
  11.0 126.8 %all-gather.12.cloned.1.call-start = ((), (), s32[]{:S(2)}) async-start(), calls=%async_computation.9 | async-start | bytes 2506752 | tf_op jit(solution)/shard_map/all_gather | solution.py:177
  11.7 176.6 %all-gather.10.cloned.1.call-start = ((), (), s32[]{:S(2)}) async-start(), calls=%async_computation.8 | async-start | bytes 1179648 | tf_op jit(solution)/shard_map/all_gather | solution.py:192
  33.0 75.0 %copy-start.29 = (bf16[1536,32]{0,1:T(8,128)(2,1)}, bf16[1536,32]{0,1:T(8,128)(2,1)S(1)}, u32[]{:S(2)}) copy-start(bf16[1536,32]{0,1:T(8,128)(2,1)S(1)} %reshape.534) | copy-start | bytes 294916
  33.0 75.0 %copy-start.57 = (f32[32]{0:T(128)}, f32[32]{0:T(128)S(1)}, u32[]{:S(2)}) copy-start(f32[32]{0:T(128)S(1)} %get-tuple-element.949) | copy-start | bytes 388
  33.0 75.0 %copy-start.59 = (f32[32]{0:T(128)}, f32[32]{0:T(128)S(1)}, u32[]{:S(2)}) copy-start(f32[32]{0:T(128)S(1)} %get-tuple-element.950) | copy-start | bytes 388
  33.0 75.0 %copy-start.61 = (f32[32]{0:T(128)}, f32[32]{0:T(128)S(1)}, u32[]{:S(2)}) copy-start(f32[32]{0:T(128)S(1)} %get-tuple-element.951) | copy-start | bytes 388
  33.0 75.0 %copy-start.63 = (f32[32]{0:T(128)}, f32[32]{0:T(128)S(1)}, u32[]{:S(2)}) copy-start(f32[32]{0:T(128)S(1)} %get-tuple-element.952) | copy-start | bytes 388
  33.1 113.2 %copy-start.34 = (f32[2048]{0:T(1024)}, f32[2048]{0:T(1024)S(1)}, u32[]{:S(2)}) copy-start(f32[2048]{0:T(1024)S(1)} %get-tuple-element.947) | copy-start | bytes 24580
  33.1 113.2 %copy-start.36 = (f32[2048]{0:T(1024)}, f32[2048]{0:T(1024)S(1)}, u32[]{:S(2)}) copy-start(f32[2048]{0:T(1024)S(1)} %get-tuple-element.948) | copy-start | bytes 24580
  33.1 75.5 %copy-start.72 = (f32[32]{0:T(128)S(1)}, f32[32]{0:T(128)}, u32[]{:S(2)}) copy-start(f32[32]{0:T(128)} %param.29) | copy-start | bytes 388
  33.1 78.4 %copy-start.56 = (f32[4,384]{1,0:T(4,128)S(1)}, f32[4,384]{1,0:T(4,128)}, u32[]{:S(2)}) copy-start(f32[4,384]{1,0:T(4,128)} %param.26) | copy-start | bytes 18436
  33.1 78.5 %copy-start.69 = (bf16[96,6]{0,1:T(8,128)(2,1)S(1)}, bf16[96,6]{0,1:T(8,128)(2,1)}, u32[]{:S(2)}) copy-start(bf16[96,6]{0,1:T(8,128)(2,1)} %param.24) | copy-start | bytes 3460
  33.2 100.1 %copy-start.74 = (f32[6]{0:T(128)S(1)}, f32[6]{0:T(128)}, u32[]{:S(2)}) copy-start(f32[6]{0:T(128)} %param.31) | copy-start | bytes 76
  109.7 297.7 %all-gather.14.cloned.1.call-start = ((), (), s32[]{:S(2)}) async-start(), calls=%async_computation.10 | async-start | bytes 1253376 | tf_op jit(solution)/shard_map/all_gather | solution.py:224
  110.3 297.2 %all-gather.16.cloned.1.call-start = ((), (), s32[]{:S(2)}) async-start(), calls=%async_computation.12 | async-start | bytes 7077888 | tf_op jit(solution)/shard_map/all_gather | solution.py:235
  110.9 754.5 %reduce-scatter.16.cloned.1.call-start = ((), (), s32[]{:S(2)}) async-start(), calls=%async_computation.13 | async-start | bytes 2359296 | tf_op jit(solution)/shard_map/reduce_scatter | solution.py:272
  111.6 34.7 %copy-start.44 = (f32[384]{0:T(512)}, f32[384]{0:T(512)S(1)}, u32[]{:S(2)}) copy-start(f32[384]{0:T(512)S(1)} %get-tuple-element.825) | copy-start | bytes 4612
  111.6 34.7 %copy-start.46 = (f32[384]{0:T(512)}, f32[384]{0:T(512)S(1)}, u32[]{:S(2)}) copy-start(f32[384]{0:T(512)S(1)} %get-tuple-element.826) | copy-start | bytes 4612
  111.6 34.7 %copy-start.48 = (f32[384]{0:T(512)}, f32[384]{0:T(512)S(1)}, u32[]{:S(2)}) copy-start(f32[384]{0:T(512)S(1)} %get-tuple-element.827) | copy-start | bytes 4612
  111.6 34.7 %copy-start.50 = (f32[384]{0:T(512)}, f32[384]{0:T(512)S(1)}, u32[]{:S(2)}) copy-start(f32[384]{0:T(512)S(1)} %get-tuple-element.828) | copy-start | bytes 4612
  163.3 5.0 copy-start.68
  383.7 23.8 %copy-start.66 = (f32[384]{0:T(512)S(1)}, f32[384]{0:T(512)}, u32[]{:S(2)}) copy-start(f32[384]{0:T(512)} %param.33) | copy-start | bytes 4612
  407.4 31.7 %copy-start.42 = (f32[2048]{0:T(1024)}, f32[2048]{0:T(1024)S(1)}, u32[]{:S(2)}) copy-start(f32[2048]{0:T(1024)S(1)} %get-tuple-element.945) | copy-start | bytes 24580
  407.5 31.7 %copy-start.13 = (f32[2048,384]{1,0:T(8,128)S(1)}, f32[2048,384]{1,0:T(8,128)}, u32[]{:S(2)}) copy-start(f32[2048,384]{1,0:T(8,128)} %copy.253) | copy-start | bytes 9437188
  448.1 6.7 copy-start.18
  448.1 6.7 copy-start.24
  478.4 15.9 %copy-start.41 = (f32[6]{0:T(128)S(1)}, f32[6]{0:T(128)}, u32[]{:S(2)}) copy-start(f32[6]{0:T(128)} %get-tuple-element.1185) | copy-start | bytes 76 | tf_op jit(solution)/shard_map/while
  519.2 15.9 %copy-start.41 = (f32[6]{0:T(128)S(1)}, f32[6]{0:T(128)}, u32[]{:S(2)}) copy-start(f32[6]{0:T(128)} %get-tuple-element.1185) | copy-start | bytes 76 | tf_op jit(solution)/shard_map/while
  560.0 15.9 %copy-start.41 = (f32[6]{0:T(128)S(1)}, f32[6]{0:T(128)}, u32[]{:S(2)}) copy-start(f32[6]{0:T(128)} %get-tuple-element.1185) | copy-start | bytes 76 | tf_op jit(solution)/shard_map/while
  600.7 15.9 %copy-start.41 = (f32[6]{0:T(128)S(1)}, f32[6]{0:T(128)}, u32[]{:S(2)}) copy-start(f32[6]{0:T(128)} %get-tuple-element.1185) | copy-start | bytes 76 | tf_op jit(solution)/shard_map/while
  641.5 15.9 %copy-start.41 = (f32[6]{0:T(128)S(1)}, f32[6]{0:T(128)}, u32[]{:S(2)}) copy-start(f32[6]{0:T(128)} %get-tuple-element.1185) | copy-start | bytes 76 | tf_op jit(solution)/shard_map/while
  682.3 15.9 %copy-start.41 = (f32[6]{0:T(128)S(1)}, f32[6]{0:T(128)}, u32[]{:S(2)}) copy-start(f32[6]{0:T(128)} %get-tuple-element.1185) | copy-start | bytes 76 | tf_op jit(solution)/shard_map/while
  723.0 15.9 %copy-start.41 = (f32[6]{0:T(128)S(1)}, f32[6]{0:T(128)}, u32[]{:S(2)}) copy-start(f32[6]{0:T(128)} %get-tuple-element.1185) | copy-start | bytes 76 | tf_op jit(solution)/shard_map/while
  763.8 15.9 %copy-start.41 = (f32[6]{0:T(128)S(1)}, f32[6]{0:T(128)}, u32[]{:S(2)}) copy-start(f32[6]{0:T(128)} %get-tuple-element.1185) | copy-start | bytes 76 | tf_op jit(solution)/shard_map/while
  789.4 138.0 %reduce-scatter.22.cloned.1.call-start = ((), (), s32[]{:S(2)}) async-start(), calls=%async_computation.17 | async-start | bytes 417792
  797.1 5.2 copy-start.43
  797.1 5.2 copy-start.67
  802.0 8.0 copy-start.6
  802.0 8.0 copy-start.37
  802.1 188.1 %reduce-scatter.26.cloned.1.call-start = ((), (), s32[]{:S(2)}) async-start(), calls=%async_computation.19 | async-start | bytes 1253376
  802.3 7.7 copy-start.14
  802.3 7.7 copy-start.16
  816.2 314.6 %all-reduce.16.cloned.1.call-start = ((), (), s32[]{:S(2)}) async-start(), calls=%async_computation.16 | async-start | bytes 163840 | tf_op jit(solution)/shard_map/psum | solution.py:352
  832.8 32.6 %copy-start.9 = (f32[2048,32]{0,1:T(8,128)S(1)}, f32[2048,32]{0,1:T(8,128)}, u32[]{:S(2)}) copy-start(f32[2048,32]{0,1:T(8,128)} %copy-done.8) | copy-start | bytes 786436
  838.6 28.9 %copy-start.71 = (f32[384]{0:T(512)S(1)}, f32[384]{0:T(512)}, u32[]{:S(2)}) copy-start(f32[384]{0:T(512)} %get-tuple-element.815) | copy-start | bytes 4612
  838.6 29.7 %copy-start.58 = (f32[32]{0:T(128)S(1)}, f32[32]{0:T(128)}, u32[]{:S(2)}) copy-start(f32[32]{0:T(128)} %copy-done.57) | copy-start | bytes 388
  838.6 29.7 %copy-start.60 = (f32[32]{0:T(128)S(1)}, f32[32]{0:T(128)}, u32[]{:S(2)}) copy-start(f32[32]{0:T(128)} %copy-done.59) | copy-start | bytes 388
  838.6 29.7 %copy-start.62 = (f32[32]{0:T(128)S(1)}, f32[32]{0:T(128)}, u32[]{:S(2)}) copy-start(f32[32]{0:T(128)} %copy-done.61) | copy-start | bytes 388
  838.6 29.7 %copy-start.64 = (f32[32]{0:T(128)S(1)}, f32[32]{0:T(128)}, u32[]{:S(2)}) copy-start(f32[32]{0:T(128)} %copy-done.63) | copy-start | bytes 388
  868.3 323.8 %reduce-scatter.24.cloned.1.call-start = ((), (), s32[]{:S(2)}) async-start(), calls=%async_computation.18 | async-start | bytes 417792
  868.5 5.1 copy-start.25
  868.5 5.1 copy-start.27
  873.6 383.4 %reduce-scatter.20.cloned.1.call-start = ((), (), s32[]{:S(2)}) async-start(), calls=%async_computation.15 | async-start | bytes 2506752 | tf_op jit(solution)/shard_map/reduce_scatter | solution.py:324
  873.7 9.7 copy-start.33
  883.1 475.7 %reduce-scatter.18.cloned.1.call-start = ((), (), s32[]{:S(2)}) async-start(), calls=%async_computation.14 | async-start | bytes 7077888 | tf_op jit(solution)/shard_map/reduce_scatter | solution.py:302
  886.0 8.2 copy-start.30
  903.3 558.5 %reduce-scatter.14.cloned.1.call-start = ((), (), s32[]{:S(2)}) async-start(), calls=%async_computation.11 | async-start | bytes 7077888 | tf_op jit(solution)/shard_map/reduce_scatter | solution.py:226
  911.8 446.9 %copy-start.12 = (bf16[256,1536]{1,0:T(8,128)(2,1)S(1)}, bf16[256,1536]{1,0:T(8,128)(2,1)}, u32[]{:S(2)}) copy-start(bf16[256,1536]{1,0:T(8,128)(2,1)} %param.20) | copy-start | bytes 2359300
  911.8 446.9 %copy-start.40 = (f32[1536]{0:T(1024)S(1)}, f32[1536]{0:T(1024)}, u32[]{:S(2)}) copy-start(f32[1536]{0:T(1024)} %param.22) | copy-start | bytes 18436
  911.8 446.9 %copy-start.54 = (f32[256]{0:T(256)S(1)}, f32[256]{0:T(256)}, u32[]{:S(2)}) copy-start(f32[256]{0:T(256)} %copy-done.53) | copy-start | bytes 3076
  911.8 549.9 %copy-start.21 = (bf16[256,1536]{1,0:T(8,128)(2,1)S(1)}, bf16[256,1536]{1,0:T(8,128)(2,1)}, u32[]{:S(2)}) copy-start(bf16[256,1536]{1,0:T(8,128)(2,1)} %param.35) | copy-start | bytes 2359300
  (33 other events, 103.8 us)
Sparse Core Ops, SparseCore 0:
  11.1 92.1 all-gather.7
  105.5 32.1 all-gather.11
  140.6 47.6 all-gather.9
  189.9 31.4 all-gather.13
  223.6 89.6 all-gather.15
  789.5 75.8 reduce-scatter.15
  868.4 58.8 reduce-scatter.21
  929.7 60.4 reduce-scatter.25
  995.5 135.2 all-reduce.15
  1133.1 58.9 reduce-scatter.23
  1194.5 62.4 reduce-scatter.19
  1260.7 97.9 reduce-scatter.17
  1363.1 98.5 reduce-scatter.13
where the time goes:
time: 1480 us; the launch traced here: 1470 us
  waiting for transfers between devices  577 us (39%)
  local copies, waits for them, and re-layouts  346 us (23%)
  matrix products  188 us (13%)
  other arithmetic  165 us (11%)
  blocking collectives  156 us (11%)
  loops' own time  23.2 us (2%)
  between operations  15.2 us (1%)
    dynamic_update_slice x32, local copies, waits for them, and re-layouts, per_device(): lax.scan(forward_step, zero_state, (x_blocks, b_blocks, c_blocks, step_bl...  164 us
    psum x1, waiting for transfers between devices, per_device(): lax.psum((placed, grad_norm_part), ('dp', 'tensor'))  139 us
    unnamed x16, waiting for transfers between devices  132 us
    reduce_scatter x1, waiting for transfers between devices, per_device(): lax.psum_scatter((total_rows + lax.dot_general(grad_state_raw, full_state...  100 us
    psum x1, blocking collectives, per_device(): lax.psum((placed, grad_norm_part), ('dp', 'tensor'))  74.9 us
    all_gather x1, waiting for transfers between devices, per_device(): normed = lax.all_gather(normed_own, 'tensor', axis=0, tiled=True)  70.1 us
    reduce_scatter x1, waiting for transfers between devices, per_device(): lax.psum_scatter(grad_main_part.astype(jnp.bfloat16), 'dp', scatter_dimen...  63.5 us
    another operation x56, other arithmetic  44.8 us
  transfers between devices with their start and end apart: 13, of which 11 were waited for; matrix products, arithmetic and copies ran while one was open for 22% of the time, Pallas kernels for 0%

commit v1 on v0

v1 whole, which is shorter than its diff:
```python
import functools

import jax
import jax.numpy as jnp
from jax import lax
from jax.experimental import pallas as pl
from jax.experimental.pallas import tpu as pltpu
from jax.sharding import PartitionSpec as P

BLOCK = 256
epsilon = 1e-05

MESH = pl.DeviceIdType.MESH
AXES = (0, 1, 2)
SIDE = 4


def coordinates():
    dp = lax.axis_index("dp")
    t = lax.axis_index("tensor")
    z = lax.div(t, 4) * 2 + lax.div(dp, 8)
    return (lax.rem(t, 4), lax.rem(lax.div(dp, 2), 4), z), lax.rem(dp, 2)


def device(at, core):
    x, y, z = at
    return (lax.rem(z, 2) * 8 + y * 2 + core, lax.div(z, 2) * 4 + x)


def moved(at, axis, by):
    return tuple(lax.rem(v + by + SIDE, SIDE) if i == axis else v for i, v in enumerate(at))


def pieces(at, whole, width):
    x, y, z = at
    lo = pl.ds(0, 2) if 2 in whole else pl.ds(lax.rem(z, 2), 1)
    row = pl.ds(0, 4) if 1 in whole else pl.ds(y, 1)
    hi = lax.div(z, 2)
    if 0 in whole and 2 in whole:
        cols = [pl.ds(0, 8 * width)]
    elif 0 in whole:
        cols = [pl.ds(pl.multiple_of(hi * 4 * width, 128), 4 * width)]
    elif 2 in whole:
        cols = [
            pl.ds(pl.multiple_of(x * width, 128), width),
            pl.ds(pl.multiple_of((4 + x) * width, 128), width),
        ]
    else:
        cols = [pl.ds(pl.multiple_of((hi * 4 + x) * width, 128), width)]
    return [(lo, row, c) for c in cols]


def greet(at, core, group):
    barrier = pltpu.get_barrier_semaphore()
    others = [device(moved(at, axis, by), core) for axis in AXES for by in (1, -1)]
    others.append(device(at, 1 - core))
    others += group
    for other in others:
        pl.semaphore_signal(barrier, inc=1, device_id=other, device_id_type=MESH)
    pl.semaphore_wait(barrier, len(others))


def tensor_peer(by):
    return (lax.axis_index("dp"), lax.rem(lax.axis_index("tensor") + by, 8))


ROWS, WIDTH, SMALL_ROWS, SMALL_WIDTH = 96, 384, 32, 128
UNITS = [(0, q * 32, q) for q in range(3)] + [(1, 0, 0)]
WIDTHS = [WIDTH, SMALL_WIDTH]
STACK = [3, 1]


def axes_of(u):
    return [(UNITS[u][2] + j) % 3 for j in range(3)]


def region(ref, u, core, mats, where, whole, half=None):
    which, first, rows = UNITS[u][0], UNITS[u][1], 32
    if half is not None:
        first, rows = first + half * 16, 16
    return [
        ref.at[mats, lo, row, core, pl.ds(first, rows), cols]
        for lo, row, cols in pieces(where, whole, WIDTHS[which])
    ]


def sized(ref, u, mats, blocks, halves=2):
    width = WIDTHS[UNITS[u][0]]
    cols = min(blocks, 8)
    rest = blocks // cols
    return ref.at[mats, pl.ds(0, max(rest // 4, 1)), pl.ds(0, min(rest, 4)), 0, pl.ds(0, 16 * halves), pl.ds(0, cols * width)]


def gather_kernel(*refs):
    shards, small, tail, params = refs[0], refs[1], refs[2], refs[3]
    full, halo, params_all = refs[4:6], refs[6], refs[7]
    own_sem, halo_sem, param_send, param_recv, send, recv, core_send, core_recv = refs[8:]
    at, core = coordinates()
    t = lax.axis_index("tensor")
    own = []
    for w, source in enumerate((shards, small)):
        for lo, row, cols in pieces(at, (), WIDTHS[w]):
            own.append(
                pltpu.make_async_copy(source, full[w].at[:, lo.start, row.start, core, :, cols], own_sem.at[w])
            )
    own.append(pltpu.make_async_copy(params, params_all.at[t], own_sem.at[2]))
    for c in own:
        c.start()
    greet(at, core, [tensor_peer(by) for by in range(1, 8)])
    last = []

    def go(copy, wait=True):
        copy.start()
        if wait:
            last.append(copy)

    def tail_copy():
        return pltpu.make_async_remote_copy(
            src_ref=tail, dst_ref=halo, send_sem=halo_sem.at[0], recv_sem=halo_sem.at[1],
            device_id=tensor_peer(1), device_id_type=MESH,
        )

    def param_copy(by, of):
        return pltpu.make_async_remote_copy(
            src_ref=params, dst_ref=params_all.at[of], send_sem=param_send.at[by - 1],
            recv_sem=param_recv.at[by - 1], device_id=tensor_peer(by), device_id_type=MESH,
        )

    go(tail_copy())
    for by in range(1, 8):
        go(param_copy(by, t))
    for c in own:
        c.wait()

    def slot(u, phase, m):
        return (phase if phase < 2 else 2 + m), [u]

    def mats_of(u, phase, m):
        return pl.ds(0, STACK[UNITS[u][0]]) if phase < 2 else pl.ds(m, 1)

    def sends(u, phase, m, step):
        axes = axes_of(u)
        whole, axis = axes[:phase], axes[phase]
        index = phase if phase < 2 else 2 + m
        ref = full[UNITS[u][0]]
        for kind, by in ((0, 1), (1, -1)):
            where = at if step == 0 else moved(at, axis, -by)
            for part in region(ref, u, core, mats_of(u, phase, m), where, whole, kind if step else None):
                pltpu.make_async_remote_copy(
                    src_ref=part, dst_ref=part, send_sem=send.at[u, index, step],
                    recv_sem=recv.at[u, index, step],
                    device_id=device(moved(at, axis, by), core), device_id_type=MESH,
                ).start()

    def await_step(u, phase, m, step, sem):
        index = phase if phase < 2 else 2 + m
        part = sized(full[UNITS[u][0]], u, mats_of(u, phase, m), 2 * 4**phase // (1 + step))
        pltpu.make_async_copy(part, part, sem.at[u, index, step]).wait()

    def to_partner(u, m, where, whole):
        for part in region(full[UNITS[u][0]], u, core, mats_of(u, 2, m), where, whole):
            pltpu.make_async_remote_copy(
                src_ref=part, dst_ref=part, send_sem=core_send.at[u, m],
                recv_sem=core_recv.at[u, m], device_id=device(at, 1 - core), device_id_type=MESH,
            ).start()

    everything = range(len(UNITS))
    late = [(u, m) for m in range(3) for u in everything if m < STACK[UNITS[u][0]]]
    for phase in (0, 1):
        for u in everything:
            sends(u, phase, 0, 0)
        for u in everything:
            await_step(u, phase, 0, 0, recv)
            sends(u, phase, 0, 1)
        for u in everything:
            await_step(u, phase, 0, 1, recv)
    for u, m in late:
        sends(u, 2, m, 0)
    for u, m in late:
        to_partner(u, m, at, axes_of(u)[:2])
    for u, m in late:
        await_step(u, 2, m, 0, recv)
        sends(u, 2, m, 1)
        whole, axis = axes_of(u)[:2], axes_of(u)[2]
        for by in (-1, 1):
            to_partner(u, m, moved(at, axis, by), whole)
    for u, m in late:
        await_step(u, 2, m, 1, recv)
        whole, axis = axes_of(u)[:2], axes_of(u)[2]
        to_partner(u, m, moved(at, axis, 2), whole)
    for u, m in late:
        part = sized(full[UNITS[u][0]], u, mats_of(u, 2, m), 64)
        pltpu.make_async_copy(part, part, core_recv.at[u, m]).wait()
        pltpu.make_async_copy(part, part, core_send.at[u, m]).wait()
    tail_copy().wait_recv()
    for by in range(1, 8):
        param_copy(by, lax.rem(t + 8 - by, 8)).wait_recv()
    for u in everything:
        for phase in (0, 1):
            for step in (0, 1):
                await_step(u, phase, 0, step, send)
    for u, m in late:
        for step in (0, 1):
            await_step(u, 2, m, step, send)
    for c in last:
        c.wait_send()


def gather_weights(shards, small, tail, params):
    units = len(UNITS)
    return pl.pallas_call(
        gather_kernel,
        name="gather_weights",
        out_shape=[
            jax.ShapeDtypeStruct((3, 2, 4, 2, ROWS, 8 * WIDTH), jnp.bfloat16),
            jax.ShapeDtypeStruct((1, 2, 4, 2, SMALL_ROWS, 8 * SMALL_WIDTH), jnp.bfloat16),
            jax.ShapeDtypeStruct(tail.shape, tail.dtype),
            jax.ShapeDtypeStruct((8,) + params.shape, params.dtype),
        ],
        in_specs=[pl.BlockSpec(memory_space=pl.ANY)] * 4,
        out_specs=[pl.BlockSpec(memory_space=pl.ANY)] * 4,
        scratch_shapes=[
            pltpu.SemaphoreType.DMA((3,)),
            pltpu.SemaphoreType.DMA((2,)),
            pltpu.SemaphoreType.DMA((7,)),
            pltpu.SemaphoreType.DMA((7,)),
            pltpu.SemaphoreType.DMA((units, 5, 2)),
            pltpu.SemaphoreType.DMA((units, 5, 2)),
            pltpu.SemaphoreType.DMA((units, 3)),
            pltpu.SemaphoreType.DMA((units, 3)),
        ],
        compiler_params=pltpu.CompilerParams(collective_id=0, has_side_effects=True),
    )(shards, small, tail, params)


VEC_ROWS = 168


def spread(whole):
    return (2 if 2 in whole else 1, 4 if 1 in whole else 1, (4 if 0 in whole else 1) * (2 if 2 in whole else 1))


def half_shape(u, phase, rows):
    lo, y, cols = spread(axes_of(u)[:phase])
    which = UNITS[u][0]
    return (2, STACK[which], lo, y, rows, cols * WIDTHS[which])


def scatter_kernel(*refs):
    grads, vec = refs[0:2], refs[2]
    outs, vec_out = refs[3:5], refs[5]
    own, other = refs[6:8], refs[8:10]
    units = len(UNITS)
    half_buf = [[refs[10 + 3 * u + p] for p in range(3)] for u in range(units)]
    full_buf = [[refs[10 + 3 * (units + u) + p] for p in range(3)] for u in range(units)]
    rest = refs[10 + 6 * units :]
    vec_acc, vec_in, own_sem, vec_send, vec_recv, send, recv, core_send, core_recv = rest
    at, core = coordinates()
    loads = [
        [pltpu.make_async_copy(grads[w].at[m, :, :, core], own[w].at[m], own_sem.at[w, m]) for m in range(STACK[w])]
        for w in range(2)
    ]
    for w in range(2):
        for c in loads[w]:
            c.start()
    greet(at, core, [device(moved(at, axis, 2), core) for axis in AXES])

    everything = range(units)
    late = [(u, m) for m in range(3) for u in everything if m < STACK[UNITS[u][0]]]

    def part_of(ref, u, mats, where, whole, half=None):
        which, first, rows = UNITS[u][0], UNITS[u][1], 32
        if half is not None:
            first, rows = first + half * 16, 16
        return [ref.at[mats, lo, y, pl.ds(first, rows), cols] for lo, y, cols in pieces(where, whole, WIDTHS[which])]

    groups = [[2], [1, -1], [0]]

    for u, m in late:
        axes = axes_of(u)
        which = UNITS[u][0]
        for g, group in enumerate(groups):
            for by in group:
                where = moved(at, axes[2], by) if by else at
                for src, dst in zip(
                    region(grads[which], u, 1 - core, pl.ds(m, 1), where, axes[:2]),
                    part_of(other[which], u, pl.ds(m, 1), where, axes[:2]),
                ):
                    pltpu.make_async_remote_copy(
                        src_ref=src, dst_ref=dst, send_sem=core_send.at[u, m], recv_sem=core_recv.at[u, m, g],
                        device_id=device(at, 1 - core), device_id_type=MESH,
                    ).start()

    def await_partner(u, m, g):
        which = UNITS[u][0]
        rows = 2 * len(groups[g])
        part = other[which].at[pl.ds(m, 1), pl.ds(0, 1), pl.ds(0, rows), pl.ds(0, 32)]
        pltpu.make_async_copy(part, part, core_recv.at[u, m, g]).wait()

    def add(u, phase, m, where, half, terms, result=None):
        which, first, rows = UNITS[u][0], UNITS[u][1], 32
        if half is not None:
            first, rows = first + half * 16, 16
        whole = axes_of(u)[:phase]
        n_lo, n_y, _ = spread(whole)
        mats = STACK[which] if m is None else 1
        for i, (lo, y, cols) in enumerate(pieces(where, whole, WIDTHS[which])):

            @pl.loop(0, mats * n_lo * n_y)
            def _(k, i=i, lo=lo, y=y, cols=cols):
                mat = lax.div(k, n_lo * n_y) if m is None else m
                a, b = lax.rem(lax.div(k, n_y), n_lo), lax.rem(k, n_y)
                here = (mat, lo.start + a, y.start + b, pl.ds(first, rows), cols)
                total = own[which][here].astype(jnp.float32)
                for term in terms:
                    total = total + term(mat, i, a, b, here).astype(jnp.float32)
                if result is None:
                    own[which][here] = total.astype(jnp.bfloat16)
                else:
                    result[mat, pl.ds(first, rows), :] = total

    def from_other(u):
        return lambda mat, i, a, b, here: other[UNITS[u][0]][here]

    def from_buf(ref, side, u, phase):
        which = UNITS[u][0]
        whole = axes_of(u)[:phase]
        width = spread(whole)[2] * WIDTHS[which] // (2 if 2 in whole and 0 not in whole else 1)
        return lambda mat, i, a, b, here: ref[side, mat, a, b, :, pl.ds(i * width, width)]

    def send_step(u, phase, m, step):
        axes = axes_of(u)
        whole, axis = axes[:phase], axes[phase]
        which = UNITS[u][0]
        mats = pl.ds(0, STACK[which]) if m is None else pl.ds(m, 1)
        index = phase if m is None else 2 + m
        buf = half_buf[u][phase] if step == 0 else full_buf[u][phase]
        for side, by in ((0, 1), (1, -1)):
            where = moved(at, axis, 2 if step == 0 else by)
            sources = part_of(own[which], u, mats, where, whole, side if step == 0 else None)
            width = buf.shape[-1] // len(sources)
            for i, src in enumerate(sources):
                pltpu.make_async_remote_copy(
                    src_ref=src, dst_ref=buf.at[side, mats, :, :, :, pl.ds(i * width, width)],
                    send_sem=send.at[u, index, step], recv_sem=recv.at[u, index, step],
                    device_id=device(moved(at, axis, by), core), device_id_type=MESH,
                ).start()

    def await_step(u, phase, m, step, sem):
        index = phase if m is None else 2 + m
        buf = half_buf[u][phase] if step == 0 else full_buf[u][phase]
        part = buf if m is None else buf.at[:, pl.ds(m, 1)]
        pltpu.make_async_copy(part, part, sem.at[u, index, step]).wait()

    def vec_copy(k):
        (x, y, z) = at
        flip = lambda v: v + 1 - 2 * lax.rem(v, 2)
        to = [
            device(at, 1 - core),
            device((flip(x), y, z), core),
            device((x, flip(y), z), core),
            device((x, y, flip(z)), core),
            device(moved(at, 0, 2), core),
            device(moved(at, 1, 2), core),
            device(moved(at, 2, 2), core),
        ][k]
        return pltpu.make_async_remote_copy(
            src_ref=vec_acc.at[k], dst_ref=vec_in.at[k], send_sem=vec_send.at[k], recv_sem=vec_recv.at[k],
            device_id=to, device_id_type=MESH,
        )

    def vec_step(k):
        if k == 0:
            vec_acc[0] = vec[...]
        else:
            vec_copy(k - 1).wait_recv()
            vec_acc[k] = vec_acc[k - 1] + vec_in[k - 1]
        if k < 7:
            vec_copy(k).start()
        else:
            vec_out[...] = vec_acc[7]

    def stage_a(m):
        for u, n in late:
            if n == m:
                axis = axes_of(u)[2]
                loads[UNITS[u][0]][m].wait() if u == 0 or u == 3 else None
                await_partner(u, m, 0)
                add(u, 2, m, moved(at, axis, 2), None, [from_other(u)])
                send_step(u, 2, m, 0)

    def stage_b(m):
        for u, n in late:
            if n == m:
                axis = axes_of(u)[2]
                await_partner(u, m, 1)
                await_step(u, 2, m, 0, recv)
                for side, by in ((0, 1), (1, -1)):
                    where = moved(at, axis, by)
                    add(u, 2, m, where, side, [from_other(u), from_buf(half_buf[u][2], side, u, 2)])
                    add(u, 2, m, where, 1 - side, [from_other(u)])
                send_step(u, 2, m, 1)

    def stage_c(m):
        for u, n in late:
            if n == m:
                await_partner(u, m, 2)
                await_step(u, 2, m, 1, recv)
                add(u, 2, m, at, None, [from_other(u)] + [from_buf(full_buf[u][2], side, u, 2) for side in (0, 1)])

    vec_step(0)
    stage_a(0)
    stage_a(1)
    vec_step(1)
    stage_b(0)
    stage_a(2)
    vec_step(2)
    stage_b(1)
    vec_step(3)
    stage_c(0)
    vec_step(4)
    stage_b(2)
    vec_step(5)
    stage_c(1)
    vec_step(6)
    stage_c(2)
    vec_step(7)
    for phase in (1, 0):
        for u in everything:
            send_step(u, phase, None, 0)
        for u in everything:
            axis = axes_of(u)[phase]
            await_step(u, phase, None, 0, recv)
            for side, by in ((0, 1), (1, -1)):
                add(u, phase, None, moved(at, axis, by), side, [from_buf(half_buf[u][phase], side, u, phase)])
            send_step(u, phase, None, 1)
        for u in everything:
            await_step(u, phase, None, 1, recv)
            add(
                u, phase, None, at, None, [from_buf(full_buf[u][phase], side, u, phase) for side in (0, 1)],
                None if phase else outs[UNITS[u][0]],
            )
    for u, m in late:
        part = other[UNITS[u][0]].at[pl.ds(m, 1), :, :, pl.ds(0, 32)]
        pltpu.make_async_copy(part, part, core_send.at[u, m]).wait()
        for step in (0, 1):
            await_step(u, 2, m, step, send)
    for u in everything:
        for phase in (0, 1):
            for step in (0, 1):
                await_step(u, phase, None, step, send)
    for k in range(7):
        vec_copy(k).wait_send()


def scatter_grads(main, small, vec):
    units = range(len(UNITS))
    n = len(UNITS)
    held = [(3, 2, 4, ROWS, 8 * WIDTH), (1, 2, 4, SMALL_ROWS, 8 * SMALL_WIDTH)]
    return pl.pallas_call(
        scatter_kernel,
        name="scatter_grads",
        out_shape=[
            jax.ShapeDtypeStruct((3, ROWS, WIDTH), jnp.float32),
            jax.ShapeDtypeStruct((1, SMALL_ROWS, SMALL_WIDTH), jnp.float32),
            jax.ShapeDtypeStruct((VEC_ROWS, 128), jnp.float32),
        ],
        in_specs=[pl.BlockSpec(memory_space=pl.ANY)] * 2 + [pl.BlockSpec(memory_space=pltpu.VMEM)],
        out_specs=[pl.BlockSpec(memory_space=pltpu.VMEM)] * 3,
        scratch_shapes=[pltpu.VMEM(s, jnp.bfloat16) for s in held + held]
        + [pltpu.VMEM(half_shape(u, p, 16), jnp.bfloat16) for u in units for p in range(3)]
        + [pltpu.VMEM(half_shape(u, p, 32), jnp.bfloat16) for u in units for p in range(3)]
        + [
            pltpu.VMEM((8, VEC_ROWS, 128), jnp.float32),
            pltpu.VMEM((7, VEC_ROWS, 128), jnp.float32),
            pltpu.SemaphoreType.DMA((2, 3)),
            pltpu.SemaphoreType.DMA((7,)),
            pltpu.SemaphoreType.DMA((7,)),
            pltpu.SemaphoreType.DMA((n, 5, 2)),
            pltpu.SemaphoreType.DMA((n, 5, 2)),
            pltpu.SemaphoreType.DMA((n, 3)),
            pltpu.SemaphoreType.DMA((n, 3, 3)),
        ],
        compiler_params=pltpu.CompilerParams(
            collective_id=3, has_side_effects=True, vmem_limit_bytes=58 * 2**20
        ),
    )(main, small, vec)


CHUNK = 256


def chain_kernel(forward, add_ref, keep_ref, out_ref, sending, arriving, send, recv):
    t = lax.axis_index("tensor")
    by = 1 if forward else 7
    is_first = t == (0 if forward else 7)
    is_last = t == (7 if forward else 0)
    barrier = pltpu.get_barrier_semaphore()
    for other in (tensor_peer(1), tensor_peer(7)):
        pl.semaphore_signal(barrier, inc=1, device_id=other, device_id_type=MESH)
    pl.semaphore_wait(barrier, 2)

    def copy(cols, g):
        return pltpu.make_async_remote_copy(
            src_ref=sending.at[:, cols], dst_ref=arriving.at[:, cols], send_sem=send.at[g], recv_sem=recv.at[g],
            device_id=tensor_peer(by), device_id_type=MESH,
        )

    chunks = add_ref.shape[1] // CHUNK

    @pl.loop(0, chunks)
    def _(g):
        cols = pl.ds(pl.multiple_of(g * CHUNK, CHUNK), CHUNK)

        @pl.when(is_first)
        def _():
            out_ref[:, cols] = jnp.zeros((add_ref.shape[0], CHUNK), jnp.float32)

        @pl.when(jnp.logical_not(is_first))
        def _():
            copy(cols, g).wait_recv()
            out_ref[:, cols] = arriving[:, cols].astype(jnp.float32)

        @pl.when(jnp.logical_not(is_last))
        def _():
            sending[:, cols] = (keep_ref[:, cols] * out_ref[:, cols] + add_ref[:, cols]).astype(jnp.bfloat16)
            copy(cols, g).start()

    @pl.when(jnp.logical_not(is_last))
    def _():
        @pl.loop(0, chunks)
        def _(g):
            cols = pl.ds(pl.multiple_of(g * CHUNK, CHUNK), CHUNK)
            copy(cols, g).wait_send()


def chain(add, keep, forward):
    chunks = add.shape[1] // CHUNK
    return pl.pallas_call(
        functools.partial(chain_kernel, forward),
        name="state_chain" if forward else "state_grad_chain",
        out_shape=jax.ShapeDtypeStruct(add.shape, jnp.float32),
        in_specs=[pl.BlockSpec(memory_space=pltpu.VMEM)] * 2,
        out_specs=pl.BlockSpec(memory_space=pltpu.VMEM),
        scratch_shapes=[
            pltpu.VMEM(add.shape, jnp.bfloat16),
            pltpu.VMEM(add.shape, jnp.bfloat16),
            pltpu.SemaphoreType.DMA((chunks,)),
            pltpu.SemaphoreType.DMA((chunks,)),
        ],
        compiler_params=pltpu.CompilerParams(
            collective_id=1 if forward else 2, has_side_effects=True, vmem_limit_bytes=32 * 2**20
        ),
    )(add, keep)


D, DI, HEADS, HEAD_DIM, STATE, TAPS, HALO = 1536, 3072, 48, 64, 128, 4, 16
BF16, F32 = jnp.bfloat16, jnp.float32


def silu_slope(values):
    sigmoid_val = jax.nn.sigmoid(values)
    return sigmoid_val * (1.0 + values * (1.0 - sigmoid_val))


def dot(a, b, dims):
    return lax.dot_general(a, b, ((dims[:1], dims[1:]), ((), ())), preferred_element_type=F32)


def conv(ext, kernel, bias_row, link):
    total = bias_row[None, :] + kernel[TAPS - 1][None, :] * ext[HALO:]
    for offset in range(1, TAPS):
        total = total + kernel[TAPS - 1 - offset][None, :] * ext[HALO - offset : -offset] * link[offset]
    return total


def conv_backward(grad_ext, ext, kernel, link_ext):
    grad_out = grad_ext[:BLOCK]
    grad_in = kernel[TAPS - 1][None, :] * grad_out
    rows = [None] * TAPS
    rows[TAPS - 1] = jnp.sum(grad_out * ext[HALO:], axis=0)
    for offset in range(1, TAPS):
        masked = grad_ext * link_ext[offset]
        rows[TAPS - 1 - offset] = jnp.sum(masked[:BLOCK] * ext[HALO - offset : -offset], axis=0)
        grad_in = grad_in + kernel[TAPS - 1 - offset][None, :] * masked[offset : offset + BLOCK]
    return grad_in, jnp.stack(rows, axis=0), jnp.sum(grad_out, axis=0)


def per_device(
    hidden,
    doc_ids,
    norm_gain,
    main_proj,
    step_proj,
    state_proj,
    conv_main,
    conv_main_bias,
    conv_state,
    conv_state_bias,
    step_bias,
    decay_log,
    skip_gain,
    gate_gain,
    out_proj,
    cotangent,
):
    t = lax.axis_index("tensor")
    shards = jnp.stack([main_proj[:, 1], main_proj[:, 0], out_proj])
    small = jnp.concatenate([state_proj, step_proj], axis=1).reshape(3, SMALL_ROWS, 38)
    small = jnp.pad(small.transpose(1, 0, 2).reshape(SMALL_ROWS, 114), ((0, 0), (0, 14)))[None]
    own_params = [conv_main, conv_main_bias, conv_state, conv_state_bias, step_bias, decay_log, skip_gain, gate_gain]
    params = jnp.concatenate([v.reshape(-1) for v in own_params])
    params = jnp.pad(params, (0, 20 * 128 - params.size)).reshape(20, 128)
    full, small_full, halo, params_all = gather_weights(shards, small, hidden[BLOCK - HALO :], params)
    w_x, w_gate, w_out = (full[i].reshape(D, DI) for i in range(3))
    w_small = small_full.reshape(16, SMALL_ROWS, 8, 128)[..., :114].reshape(16, SMALL_ROWS, 8, 3, 38)
    w_small = w_small.transpose(0, 3, 1, 2, 4).reshape(D, 8, 38)
    w_state, w_step = w_small[..., :32].reshape(D, 256), w_small[..., 32:].reshape(D, HEADS)
    flat = params_all.reshape(8, 20 * 128)
    position, full_params = 0, []
    for v in own_params:
        part = flat[:, position : position + v.size].reshape((8,) + v.shape)
        position += v.size
        full_params.append(jnp.moveaxis(part, 0, -2).reshape(v.shape[:-1] + (8 * v.shape[-1],)))
    conv_main, conv_main_bias, conv_state, conv_state_bias, step_bias, decay_log, skip_gain, gate_gain = full_params

    docs_all = jnp.concatenate([jnp.full((HALO,), -1, jnp.int32), doc_ids, jnp.full((8,), -2, jnp.int32)])
    docs = lax.dynamic_slice(docs_all, (t * BLOCK,), (HALO + BLOCK + 8,))
    doc_block = docs[HALO : HALO + BLOCK]
    doc_prev = docs[HALO - 1]
    link_ext = [None] + [
        (docs[HALO : HALO + BLOCK + 8] == docs[HALO - o : BLOCK + 8 + HALO - o]).astype(F32)[:, None]
        for o in range(1, TAPS)
    ]
    link = [None] + [v[:BLOCK] for v in link_ext[1:]]

    hidden_ext = jnp.concatenate([halo, hidden]).astype(F32)
    inv_ext = lax.rsqrt(jnp.mean(hidden_ext * hidden_ext, axis=1, keepdims=True) + epsilon)
    rows_ext = hidden_ext * inv_ext
    normed_ext = (rows_ext * norm_gain[None, :]).astype(BF16)
    normed, norm_rows, inv_rms = normed_ext[HALO:], rows_ext[HALO:], inv_ext[HALO:]
    hidden_float = hidden_ext[HALO:]

    x_ext = dot(normed_ext, w_x, (1, 0))
    state_ext = dot(normed_ext, w_state, (1, 0))
    gate_in = dot(normed, w_gate, (1, 0))
    step_in = dot(normed, w_step, (1, 0)) + step_bias[None, :]
    x_pre = conv(x_ext, conv_main, conv_main_bias, link)
    x_act = jax.nn.silu(x_pre).astype(BF16)
    state_pre = conv(state_ext, conv_state, conv_state_bias, link)
    state_act = jax.nn.silu(state_pre).astype(BF16)
    b_rows, c_rows = state_act[:, :STATE], state_act[:, STATE:]
    step = jax.nn.softplus(step_in)
    decay_rate = -jnp.exp(decay_log)

    x_heads = x_act.reshape(BLOCK, HEADS, HEAD_DIM)
    cum = jnp.cumsum(step * decay_rate[None, :], axis=0)
    cum_heads, step_heads = cum.T, step.T
    scores = dot(c_rows, b_rows, (1, 1))
    row_pos = lax.broadcasted_iota(jnp.int32, (BLOCK, BLOCK), 0)
    col_pos = lax.broadcasted_iota(jnp.int32, (BLOCK, BLOCK), 1)
    linked = (doc_block[:, None] == doc_block[None, :]) & (row_pos >= col_pos)
    spread_ = jnp.where(linked[None], cum_heads[:, :, None] - cum_heads[:, None, :], -10000.0)
    decay_mat = jnp.exp(spread_) * linked[None].astype(F32)
    decay_step = decay_mat * step_heads[:, None, :]
    mix_exact = scores[None] * decay_step
    mixing = mix_exact.astype(BF16)
    cum_end = cum[BLOCK - 1]
    end_link = (doc_block == doc_block[BLOCK - 1]).astype(F32)
    tail_decay = jnp.exp(cum_end[None, :] - cum) * end_link[:, None]
    weight = tail_decay * step
    enter = jnp.exp(cum) * (doc_block == doc_prev).astype(F32)[:, None]
    keep = jnp.exp(cum_end) * (doc_block[BLOCK - 1] == doc_prev).astype(F32)
    keep_row = jnp.repeat(keep, HEAD_DIM)[None, :]
    scaled = (weight.T[:, :, None] * b_rows.astype(F32)[None]).astype(BF16)
    update = jnp.einsum("hjn,jhp->nhp", scaled, x_heads, preferred_element_type=F32).reshape(STATE, DI)
    state_in = chain(update, keep_row, True)
    state_low = state_in.astype(BF16)
    carried = dot(c_rows, state_low, (1, 0))
    y_intra = jnp.einsum("hij,jhp->ihp", mixing, x_heads, preferred_element_type=F32).reshape(BLOCK, DI)
    enter_wide = jnp.repeat(enter, HEAD_DIM, axis=1)
    skip_wide = jnp.repeat(skip_gain, HEAD_DIM)[None, :]
    x_float = x_act.astype(F32)
    y_ssd = y_intra + carried * enter_wide + skip_wide * x_float

    gate_act = jax.nn.silu(gate_in)
    gated = y_ssd * gate_act
    gate_inv = lax.rsqrt(jnp.mean(gated * gated, axis=1, keepdims=True) + epsilon)
    gate_hat = gated * gate_inv
    gate_out = (gate_hat * gate_gain[None, :]).astype(BF16)
    mixed = (hidden_float + dot(gate_out, w_out, (1, 1))).astype(BF16)

    grad_out = dot(cotangent, gate_out, (0, 0)).astype(BF16)
    grad_gate = dot(cotangent, w_out, (1, 0))
    grad_gate_gain = jnp.sum(grad_gate * gate_hat, axis=0)
    gate_dn = grad_gate * gate_gain[None, :]
    inner = jnp.mean(gate_dn * gated, axis=1, keepdims=True)
    grad_gated = gate_inv * gate_dn - gated * gate_inv**3 * inner
    grad_y = (grad_gated * gate_act).astype(BF16)
    grad_gate_in = grad_gated * y_ssd * silu_slope(gate_in)

    dy_float = grad_y.astype(F32)
    dy_heads = grad_y.reshape(BLOCK, HEADS, HEAD_DIM)
    grad_carried = (dy_float * enter_wide).astype(BF16)
    grad_state = chain(dot(c_rows, grad_carried, (0, 0)), keep_row, False)

    grad_mix = jnp.einsum("ihp,jhp->hij", dy_heads, x_heads, preferred_element_type=F32)
    grad_x = jnp.einsum("hij,ihp->jhp", mixing, dy_heads, preferred_element_type=F32).reshape(BLOCK, DI)
    grad_x = grad_x + skip_wide * dy_float
    grad_scores = (grad_mix * decay_step).astype(BF16)
    grad_c = jnp.einsum("hij,jn->in", grad_scores, b_rows, preferred_element_type=F32)
    grad_b = jnp.einsum("hij,in->jn", grad_scores, c_rows, preferred_element_type=F32)
    pull = grad_mix * mix_exact
    grad_cum = (jnp.sum(pull, axis=2) - jnp.sum(pull, axis=1)).T
    grad_step = jnp.sum(grad_mix * scores[None] * decay_mat, axis=1).T
    by_head = lambda v: jnp.sum(v.reshape(-1, HEADS, HEAD_DIM), axis=2)
    grad_cum = grad_cum + by_head(dy_float * carried) * enter
    grad_c = grad_c + dot(grad_carried, state_low, (1, 1))
    grad_update = grad_state.astype(BF16)
    update_heads = grad_update.reshape(STATE, HEADS, HEAD_DIM)
    grad_scaled = jnp.einsum("jhp,nhp->hjn", x_heads, update_heads, preferred_element_type=F32)
    grad_x = grad_x + jnp.einsum("hjn,nhp->jhp", scaled, update_heads, preferred_element_type=F32).reshape(BLOCK, DI)
    grad_b = grad_b + jnp.sum(grad_scaled * weight.T[:, :, None], axis=0)
    grad_weight = jnp.sum(grad_scaled * b_rows.astype(F32)[None], axis=2).T
    weight_pull = grad_weight * weight
    grad_keep = jnp.sum(by_head(grad_state * state_in), axis=0)
    grad_end = jnp.sum(weight_pull, axis=0) + grad_keep * keep
    last_row = (lax.broadcasted_iota(jnp.int32, (BLOCK, 1), 0) == BLOCK - 1).astype(F32)
    grad_cum = grad_cum - weight_pull + last_row * grad_end[None, :]
    grad_step = grad_step + grad_weight * tail_decay
    grad_log = jnp.flip(jnp.cumsum(jnp.flip(grad_cum, 0), axis=0), 0)
    grad_step = grad_step + grad_log * decay_rate[None, :]
    grad_decay_log = jnp.sum(grad_log * step, axis=0) * decay_rate
    grad_skip = jnp.sum(by_head(dy_float * x_float), axis=0)
    grad_step_in = grad_step * jax.nn.sigmoid(step_in)
    grad_step_bias = jnp.sum(grad_step_in, axis=0)

    grad_pre = jnp.concatenate(
        [grad_x * silu_slope(x_pre), jnp.concatenate([grad_b, grad_c], axis=1) * silu_slope(state_pre)], axis=1
    )
    after = lax.ppermute(grad_pre[:8], "tensor", [(i, i - 1) for i in range(1, 8)])
    grad_pre = jnp.concatenate([grad_pre, after])
    grad_x_raw, grad_conv_main, grad_conv_main_bias = conv_backward(grad_pre[:, :DI], x_ext, conv_main, link_ext)
    grad_state_raw, grad_conv_state, grad_conv_state_bias = conv_backward(
        grad_pre[:, DI:], state_ext, conv_state, link_ext
    )
    grad_x_raw, grad_gate_in, grad_state_raw, grad_step_raw = (
        v.astype(BF16) for v in (grad_x_raw, grad_gate_in, grad_state_raw, grad_step_in)
    )
    grad_main = [dot(normed, v, (0, 0)).astype(BF16) for v in (grad_x_raw, grad_gate_in)]
    small_raw = jnp.concatenate([grad_state_raw.reshape(BLOCK, 8, 32), grad_step_raw.reshape(BLOCK, 8, 6)], axis=2)
    grad_small = dot(normed, small_raw.reshape(BLOCK, 8 * 38), (0, 0)).astype(BF16)
    grad_small = grad_small.reshape(16, 3, SMALL_ROWS, 8, 38).transpose(0, 2, 3, 1, 4).reshape(16, SMALL_ROWS, 8, 114)
    grad_small = jnp.pad(grad_small, ((0, 0), (0, 0), (0, 0), (0, 14)))
    grad_normed = (
        dot(grad_x_raw, w_x, (1, 1))
        + dot(grad_gate_in, w_gate, (1, 1))
        + dot(grad_step_raw, w_step, (1, 1))
        + dot(grad_state_raw, w_state, (1, 1))
    )
    grad_norm_gain = jnp.sum(grad_normed * norm_rows, axis=0)
    norm_dn = grad_normed * norm_gain[None, :]
    grad_hidden = (
        cotangent.astype(F32)
        + inv_rms * norm_dn
        - norm_rows * inv_rms * jnp.mean(norm_dn * norm_rows, axis=1, keepdims=True)
    )

    local = [
        grad_conv_main, grad_conv_main_bias, grad_conv_state, grad_conv_state_bias,
        grad_step_bias, grad_decay_log, grad_skip, grad_gate_gain, grad_norm_gain,
    ]
    by_tensor = [jnp.moveaxis(v.reshape(v.shape[:-1] + (8, -1)), -2, 0).reshape(8, -1) for v in local]
    vec = jnp.concatenate(by_tensor, axis=1)
    vec = jnp.pad(vec, ((0, 0), (0, VEC_ROWS * 16 - vec.shape[1]))).reshape(VEC_ROWS, 128)
    main_grads = jnp.stack(grad_main + [grad_out]).reshape(3, 2, 4, 2, ROWS, DI)
    own_main, own_small, vec = scatter_grads(main_grads, grad_small.reshape(1, 2, 4, 2, SMALL_ROWS, 1024), vec)
    vec = vec.reshape(8, VEC_ROWS * 16)
    own = lax.dynamic_index_in_dim(vec, t, 0, keepdims=False)
    results, position = [], 0
    for v in own_params:
        results.append(own[position : position + v.size].reshape(v.shape))
        position += v.size
    grad_norm_gain = vec[:, position : position + D // 8].reshape(D)
    own_small = own_small[0, :, :114].reshape(SMALL_ROWS, 3, 38).transpose(1, 0, 2).reshape(ROWS, 38)
    return (
        mixed,
        grad_hidden,
        grad_norm_gain,
        jnp.stack([own_main[1], own_main[0]], axis=1),
        own_small[:, 32:],
        own_small[:, :32],
        *results,
        own_main[2],
    )


def solution(mesh):
    placed = (
        P(("dp", "tensor"), None),
        P("dp"),
        P(),
        P("dp", None, "tensor"),
        P("dp", "tensor"),
        P("dp", "tensor"),
        P(None, "tensor"),
        P("tensor"),
        P(None, "tensor"),
        P("tensor"),
        P("tensor"),
        P("tensor"),
        P("tensor"),
        P("tensor"),
        P("dp", "tensor"),
        P(("dp", "tensor"), None),
    )
    return jax.shard_map(
        per_device,
        mesh=mesh,
        in_specs=placed,
        out_specs=(
            P(("dp", "tensor"), None),
            P(("dp", "tensor"), None),
            P(),
            P("dp", None, "tensor"),
            P("dp", "tensor"),
            P("dp", "tensor"),
            P(None, "tensor"),
            P("tensor"),
            P(None, "tensor"),
            P("tensor"),
            P("tensor"),
            P("tensor"),
            P("tensor"),
            P("tensor"),
            P("dp", "tensor"),
        ),
        check_vma=False,
    )
```

time: 1480 us -> 586 us (0.40)
  waiting for transfers between devices: 577 us -> 0.01 us
  Pallas kernels: 0 us -> 250 us
  local copies, waits for them, and re-layouts: 346 us -> 140 us
  blocking collectives: 156 us -> 0 us
  matrix products: 188 us -> 104 us
  other arithmetic: 165 us -> 81.2 us
  loops' own time: 23.2 us -> 0 us
    pallas_call x0 -> x4, Pallas kernels: none -> 250 us  [the longest x1 88.1 us: scatter_grads(): pl.pallas_call(scatter_kernel, name='scatter_grads', out_shape=[jax.Shape...]
    reduce_scatter x4 -> x0, waiting for transfers between devices: 217 us -> none  [the longest x1 100 us: per_device(): lax.psum_scatter((total_rows + lax.dot_general(grad_state_raw, full_state...]
    dynamic_update_slice x48 -> x0, local copies, waits for them, and re-layouts: 184 us -> none  [the longest x32 164 us: per_device(): lax.scan(forward_step, zero_state, (x_blocks, b_blocks, c_blocks, step_bl...]
    psum x1 -> x0, waiting for transfers between devices: 139 us -> none  [per_device(): lax.psum((placed, grad_norm_part), ('dp', 'tensor'))]
    unnamed x16 -> x0, waiting for transfers between devices: 132 us -> none
    psum x3 -> x0, blocking collectives: 115 us -> none  [the longest x1 74.9 us: per_device(): lax.psum((placed, grad_norm_part), ('dp', 'tensor'))]
    all_gather x5 -> x0, waiting for transfers between devices: 89.6 us -> none  [the longest x1 70.1 us: per_device(): normed = lax.all_gather(normed_own, 'tensor', axis=0, tiled=True)]
    dot_general x108 -> x26, matrix products: 184 us -> 104 us  [the longest x18 70.5 us: dot(): lax.dot_general(a, b, ((dims[:1], dims[1:]), ((), ())), preferred_element...]
  transfers between devices with their start and end apart: 13 -> 1, of which waited for: 11 -> 0; matrix products, arithmetic and copies ran while one was open for 22% -> 12% of each run, Pallas kernels for 0% -> 0%
where the time goes in v1:
time: 586 us; the launch traced here: 580 us
  Pallas kernels  250 us (43%)
  local copies, waits for them, and re-layouts  140 us (24%)
  matrix products  104 us (18%)
  other arithmetic  81.2 us (14%)
    pallas_call x1, Pallas kernels, scatter_grads(): pl.pallas_call(scatter_kernel, name='scatter_grads', out_shape=[jax.Shape...  88.1 us
    pallas_call x2, Pallas kernels, chain(): pl.pallas_call(functools.partial(chain_kernel, forward), name='state_chai...  81.8 us
    pallas_call x1, Pallas kernels, gather_weights(): pl.pallas_call(gather_kernel, name='gather_weights', out_shape=[jax.Shape...  79.8 us
    dot_general x18, matrix products, dot(): lax.dot_general(a, b, ((dims[:1], dims[1:]), ((), ())), preferred_element...  70.5 us
    another operation x1, other arithmetic, per_device(): main_grads = jnp.stack(grad_main + [grad_out]).reshape(3, 2, 4, 2, ROWS, DI)  19.3 us
    slice x1, local copies, waits for them, and re-layouts, per_device(): w_x, w_gate, w_out = (full[i].reshape(D, DI) for i in range(3))  17.8 us
    reshape x2, local copies, waits for them, and re-layouts, per_device(): grad_small.reshape(16, 3, SMALL_ROWS, 8, 38).transpose(0, 2, 3, 1, 4)  12.2 us
  transfers between devices with their start and end apart: 1, of which 0 were waited for; matrix products, arithmetic and copies ran while one was open for 12% of the time, Pallas kernels for 0%

profile of v1, /device:TPU:0, one launch (start us, length us, event | category | flops | bytes accessed | tf_op | source)
XLA Modules:
  0.0 580.3 jit_solution(16241787387421792375)
XLA Ops:
  7.8 1.6 pad_maximum_fusion.4.refs_0_
  9.4 79.8 %gather_weights.1 = (bf16[3,2,4,2,96,3072]{5,4,3,2,1,0:T(8,128)(2,1)}, bf16[1,2,4,2,32,1024]{5,4,3,2,1,0:T(8,128)(2,1)}, bf16[16,1536]{1,0:T(8,128)(2,1)}, f32[8,20,128]{2,1,0:T(8,128)}) custom-call(bf16[3,96,384]{2,1,0:T(8,128)(2,1)} %pad_maximum_fusion.4.refs_0_, bf16[1,32,128]{2,1,0:T(8,128)(2,1)} %pad_bitcast_fusion.1.refs_1_, ...), custom_call_target="tpu_custom_call" | custom-call | tf_op jit(solution)/shard_map/gather_weights/pallas_call | solution.py:211
  95.5 4.5 reshape.416
  99.9 3.1 copy.226
  103.0 2.2 slice.426
  105.2 2.9 copy.227
  108.6 2.6 broadcast_multiply_fusion
  118.4 17.8 %fusion.85 = (bf16[1,2,4,2,96,3072]{5,4,3,2,1,0:T(8,128)(2,1)S(1)}, bf16[1,2,4,2,96,3072]{5,4,3,2,1,0:T(8,128)(2,1)}, bf16[1,2,4,2,96,3072]{5,4,3,2,1,0:T(8,128)(2,1)}) fusion(bf16[3,2,4,2,96,3072]{5,4,3,2,1,0:T(8,128)(2,1)} %get-tuple-element.24), kind=kLoop, calls=%fused_computation.207 | loop fusion | bytes 56623104 | tf_op jit(solution)/shard_map/slice | solution.py:615
  136.2 2.7 fusion.90
  141.0 3.9 multiply_convert_fusion.7
  145.0 2.7 copy.225
  147.9 4.0 copy.228
  155.1 5.2 fusion.8
  160.4 2.7 copy.241
  163.3 2.6 fusion.11
  166.6 21.0 %state_chain.1 = f32[128,3072]{1,0:T(8,128)S(1)} custom-call(f32[128,3072]{1,0:T(8,128)S(1)} %copy.238.add_ref, f32[1,3072]{1,0:T(1,128)S(1)} %broadcast_in_dim_reshape.2.keep_ref), custom_call_target="tpu_custom_call" | custom-call | tf_op jit(solution)/shard_map/state_chain/pallas_call | solution.py:539
  187.6 2.3 fusion.40
  190.1 1.9 broadcast_in_dim.24
  192.1 3.7 copy.240
  195.7 10.7 %multiply_reduce_fusion.6 = (f32[256]{0:T(256)S(1)}, f32[256,3072]{1,0:T(8,128)S(1)}, f32[256,3072]{1,0:T(8,128)S(1)}, f32[256,3072]{1,0:T(8,128)S(1)}) fusion(bf16[256,3072]{1,0:T(8,128)(2,1)} %get-tuple-element.158, f32[3072]{0:T(1024)} %mul.659, f32[256,3072]{1,0:T(8,128)} %copy.241, f32[256,3072]{1,0:T(8,128)} %fusion.40, f32[256,3072]{1,0:T(8,128)} %copy.240, ...), kind=kOutput, calls=%fused_computation.54 | convolution fusion | flops 2425356032 | bytes 30684160 | tf_op jit(solution)/shard_map/dot_general | solution.py:567
  206.5 7.3 %multiply_reduce_fusion.3 = (f32[3072]{0:T(1024)}, f32[256]{0:T(256)S(1)}, f32[256,3072]{1,0:T(8,128)S(1)}) fusion(f32[256,3072]{1,0:T(8,128)S(1)} %get-tuple-element.154, f32[256]{0:T(256)S(1)} %get-tuple-element.205, f32[3072]{0:T(1024)S(1)} %mul.667, bf16[256,1536]{1,0:T(8,128)(2,1)S(1)} %copy-done.23, bf16[1536,3072]{1,0:T(8,128)(2,1)} %bitcast.209), kind=kOutput, calls=%fused_computation.47 | convolution fusion | flops 2420634368 | bytes 16541696 | tf_op jit(solution)/shard_map/dot_general | solution.py:567
  213.9 4.4 fusion.17
  218.7 60.8 %state_grad_chain.1 = f32[128,3072]{1,0:T(8,128)S(1)} custom-call(f32[128,3072]{1,0:T(8,128)S(1)} %fusion.64.add_ref, f32[1,3072]{1,0:T(1,128)S(1)} %broadcast_in_dim_reshape.2.keep_ref), custom_call_target="tpu_custom_call" | custom-call | tf_op jit(solution)/shard_map/state_grad_chain/pallas_call | solution.py:539
  279.6 1.7 multiply_reduce_fusion.10
  281.2 2.3 copy.246
  283.5 3.7 multiply_reduce_fusion.2
  287.3 2.3 fusion.10
  289.6 1.6 copy.243
  291.2 6.5 %fusion.6 = f32[48,64,256]{2,1,0:T(8,128)} fusion(bf16[256,48,64]{0,2,1:T(8,128)(2,1)} %bitcast.230, f32[48,256]{1,0:T(8,128)S(1)} %copy-done.66, f32[256,256]{1,0:T(8,128)} %get-tuple-element.207, f32[48,256]{1,0:T(8,128)} %copy-done.67, f32[256,256]{1,0:T(8,128)} %fusion.61, pred[256,256]{1,0:T(8,128)(4,1)S(1)} %copy-done.57), kind=kOutput, calls=%fused_computation.21 | convolution fusion | flops 421527552 | bytes 5406720 | tf_op jit(solution)/shard_map/hij,ihp->jhp/dot_general | solution.py:708
  297.8 10.7 %fusion.4 = (f32[48,256]{1,0:T(8,128)}, f32[48,256]{1,0:T(8,128)}, f32[48,256]{1,0:T(8,128)}, bf16[256,256]{1,0:T(8,128)(2,1)}) fusion(f32[48,256]{1,0:T(8,128)S(1)} %copy-done.66, f32[256,256]{1,0:T(8,128)S(1)} %copy-done.43, f32[48,256]{1,0:T(8,128)S(1)} %copy-done.68, f32[256,256]{1,0:T(8,128)S(1)} %copy-done.44, pred[256,256]{1,0:T(8,128)(4,1)S(1)} %copy-done.57, ...), kind=kOutput, calls=%fused_computation.12 | convolution fusion | flops 449736704 | bytes 4112384 | tf_op jit(solution)/shard_map/ihp,jhp->hij/dot_general | solution.py:707
  308.5 3.5 copy.248
  312.0 3.6 copy.244
  316.7 3.2 convolution_add_fusion.3
  322.0 8.7 %fusion.15 = (f32[256,3072]{1,0:T(8,128)S(1)}, f32[256,3072]{1,0:T(8,128)}) fusion(f32[256,3072]{1,0:T(8,128)} %copy.248, f32[256,3072]{1,0:T(8,128)} %copy.244, bf16[256,3072]{1,0:T(8,128)(2,1)} %copy-done.2, f32[256,3072]{1,0:T(8,128)} %get-tuple-element.159, f32[3072]{0:T(1024)S(1)} %copy-done.69, f32[256,3072]{1,0:T(8,128)} %fusion.40), kind=kLoop, calls=%fused_computation.31 | loop fusion | flops 10223616 | bytes 20459520 | tf_op jit(solution)/shard_map/mul | solution.py:739
  333.7 5.5 convolution_convert_fusion
  339.3 7.6 %fusion.92 = f32[256,1536]{1,0:T(8,128)} fusion(bf16[256,3072]{1,0:T(8,128)(2,1)S(1)} %copy-done.21, bf16[1536,3072]{1,0:T(8,128)(2,1)} %bitcast.214), kind=kOutput, calls=%fused_computation.214 | convolution fusion | flops 2415919104 | bytes 12582912 | tf_op jit(solution)/shard_map/dot_general | solution.py:567
  346.9 5.1 convolution_convert_fusion.1
  352.0 3.6 fusion.31
  355.6 1.6 copy.254
  357.1 2.2 fusion.82
  359.4 3.5 copy.257
  362.9 2.9 reduce_sum.293
  365.7 1.6 copy.258
  367.3 1.6 copy.255
  368.9 1.6 copy.256
  373.8 1.9 fusion.51
  377.2 1.6 copy.259
  378.9 1.9 reduce-window.16
  385.8 1.6 copy.260
  388.8 1.6 copy.253
  390.4 1.8 fusion.80
  392.8 2.4 fusion.93
  407.5 4.9 fusion.20
  412.4 6.5 %convolution_convert_fusion.2 = bf16[1536,3072]{1,0:T(8,128)(2,1)} fusion(bf16[256,3072]{1,0:T(8,128)(2,1)} %get-tuple-element.163, bf16[272,1536]{1,0:T(8,128)(2,1)S(1)} %copy-done.9), kind=kOutput, calls=%fused_computation.11 | convolution fusion | flops 2420637696 | bytes 11796480 | tf_op jit(solution)/shard_map/dot_general | solution.py:567
  420.0 7.8 %fusion.30 = f32[256,1536]{1,0:T(8,128)S(1)} fusion(f32[256,1536]{1,0:T(8,128)} %fusion.93, f32[256,1536]{1,0:T(8,128)} %fusion.92, bf16[256,3072]{1,0:T(8,128)(2,1)} %get-tuple-element.163, bf16[1536,3072]{1,0:T(8,128)(2,1)} %bitcast.208), kind=kOutput, calls=%fused_computation.70 | convolution fusion | flops 2416705536 | bytes 15728640 | tf_op jit(solution)/shard_map/dot_general | solution.py:567
  427.8 2.3 multiply_reduce_fusion.8
  434.1 5.5 reshape.436
  439.6 8.2 %copy.264 = bf16[16,32,8,3,38]{4,3,2,1,0:T(4,128)(2,1)} copy(bf16[16,32,8,3,38]{4,2,1,3,0:T(8,128)(2,1)} %bitcast.206) | data formatting | bytes 1867776 | tf_op jit(solution)/shard_map/transpose | solution.py:753
  447.8 6.6 %reshape.437 = bf16[16,32,8,114]{3,2,1,0:T(8,128)(2,1)S(1)} reshape(bf16[16,32,8,3,38]{4,3,2,1,0:T(4,128)(2,1)} %copy.264) | data formatting | bytes 1867776 | tf_op jit(solution)/shard_map/reshape | solution.py:753
  455.9 2.3 reshape.438.refs_1_
  459.7 19.3 %pad_maximum_fusion.refs_0_ = bf16[3,2,4,2,96,3072]{5,4,3,2,1,0:T(8,128)(2,1)} fusion(bf16[1,2,4,2,96,3072]{5,4,3,2,1,0:T(8,128)(2,1)} %bitcast.197, bf16[1,2,4,2,96,3072]{5,4,3,2,1,0:T(8,128)(2,1)} %bitcast.198, bf16[1,2,4,2,96,3072]{5,4,3,2,1,0:T(8,128)(2,1)} %bitcast.199), kind=kLoop, calls=%fused_computation | loop fusion | flops 28311552 | bytes 56623104 | tf_op jit(solution)/shard_map/stack | solution.py:776
  479.0 88.1 %scatter_grads.1 = (f32[3,96,384]{2,1,0:T(8,128)}, f32[1,32,128]{2,1,0:T(8,128)}, f32[168,128]{1,0:T(8,128)}) custom-call(bf16[3,2,4,2,96,3072]{5,4,3,2,1,0:T(8,128)(2,1)} %pad_maximum_fusion.refs_0_, bf16[1,2,4,2,32,1024]{5,4,3,2,1,0:T(8,128)(2,1)} %reshape.438.refs_1_, f32[168,128]{1,0:T(8,128)} %reshape.447.refs_2_), custom_call_target="tpu_custom_call" | custom-call | tf_op jit(solution)/shard_map/scatter_grads/pallas_call | solution.py:460
  568.8 1.7 slice_bitcast_fusion
  576.5 3.0 multiply_subtract_fusion.1
  (363 shorter events, 72.8 us)
Async XLA Ops:
  91.8 8.1 %copy-start.71 = (f32[264]{0:T(512)}, f32[264]{0:T(512)S(1)}, u32[]{:S(2)}) copy-start(f32[264]{0:T(512)S(1)} %get-tuple-element.201) | copy-start | bytes 3172
  91.8 8.1 %copy-start.73 = (f32[264]{0:T(512)}, f32[264]{0:T(512)S(1)}, u32[]{:S(2)}) copy-start(f32[264]{0:T(512)S(1)} %get-tuple-element.202) | copy-start | bytes 3172
  91.8 8.1 %copy-start.75 = (f32[264]{0:T(512)}, f32[264]{0:T(512)S(1)}, u32[]{:S(2)}) copy-start(f32[264]{0:T(512)S(1)} %get-tuple-element.203) | copy-start | bytes 3172
  93.9 14.7 %copy-start.82 = (f32[272]{0:T(512)}, f32[272]{0:T(512)S(1)}, u32[]{:S(2)}) copy-start(f32[272]{0:T(512)S(1)} %add_rsqrt_fusion) | copy-start | bytes 3268
  108.1 4.0 copy-start.19
  108.3 5.9 %copy-start.84 = (f32[256]{0:T(256)}, f32[256]{0:T(256)S(1)}, u32[]{:S(2)}) copy-start(f32[256]{0:T(256)S(1)} %mul.634) | copy-start | bytes 3076
  108.4 5.8 copy-start.86
  108.5 5.7 copy-start.88
  108.6 5.6 copy-start.90
  117.1 72.8 %copy-start.83 = (f32[256]{0:T(256)}, f32[256]{0:T(256)S(1)}, u32[]{:S(2)}) copy-start(f32[256]{0:T(256)S(1)} %get-tuple-element.197) | copy-start | bytes 3076
  118.4 17.8 %copy-start.5 = (bf16[272,1536]{1,0:T(8,128)(2,1)S(1)}, bf16[272,1536]{1,0:T(8,128)(2,1)}, u32[]{:S(2)}) copy-start(bf16[272,1536]{1,0:T(8,128)(2,1)} %copy-done.4) | copy-start | bytes 2506756
  139.8 5.2 copy-start
  139.8 5.1 copy-start.45
  139.9 5.1 copy-start.47
  139.9 5.1 copy-start.49
  139.9 5.1 copy-start.51
  145.0 6.9 %copy-start.6 = (bf16[272,1536]{1,0:T(8,128)(2,1)S(1)}, bf16[272,1536]{1,0:T(8,128)(2,1)}, u32[]{:S(2)}) copy-start(bf16[272,1536]{1,0:T(8,128)(2,1)} %copy-done.4) | copy-start | bytes 2506756
  147.8 5.2 copy-start.100
  153.4 6.9 %copy-start.92 = (f32[48]{0:T(128)}, f32[48]{0:T(128)S(1)}, u32[]{:S(2)}) copy-start(f32[48]{0:T(128)S(1)} %slice_bitcast_fusion.3) | copy-start | bytes 580
  155.0 5.3 copy-start.56
  155.1 5.2 copy-start.67
  165.9 21.7 %copy-start.27 = (bf16[256,256]{1,0:T(8,128)(2,1)S(1)}, bf16[256,256]{1,0:T(8,128)(2,1)}, u32[]{:S(2)}) copy-start(bf16[256,256]{1,0:T(8,128)(2,1)} %copy-done.26) | copy-start | bytes 393220
  195.7 10.8 %copy-start.23 = (bf16[256,1536]{1,0:T(8,128)(2,1)S(1)}, bf16[256,1536]{1,0:T(8,128)(2,1)}, u32[]{:S(2)}) copy-start(bf16[256,1536]{1,0:T(8,128)(2,1)} %param.31) | copy-start | bytes 2359300
  206.5 7.4 %copy-start.13 = (f32[256,3072]{1,0:T(8,128)}, f32[256,3072]{1,0:T(8,128)S(1)}, u32[]{:S(2)}) copy-start(f32[256,3072]{1,0:T(8,128)S(1)} %get-tuple-element.154) | copy-start | bytes 9437188
  206.5 7.4 %copy-start.80 = (f32[256]{0:T(256)}, f32[256]{0:T(256)S(1)}, u32[]{:S(2)}) copy-start(f32[256]{0:T(256)S(1)} %get-tuple-element.205) | copy-start | bytes 3076
  206.5 7.4 %copy-start.15 = (bf16[256,3072]{1,0:T(8,128)(2,1)S(1)}, bf16[256,3072]{1,0:T(8,128)(2,1)}, u32[]{:S(2)}) copy-start(bf16[256,3072]{1,0:T(8,128)(2,1)} %get-tuple-element.158) | copy-start | bytes 4718596
  213.9 4.4 copy-start.3
  218.3 98.4 %copy-start.2 = (bf16[256,3072]{1,0:T(8,128)(2,1)}, bf16[256,3072]{1,0:T(8,128)(2,1)S(1)}, u32[]{:S(2)}) copy-start(bf16[256,3072]{1,0:T(8,128)(2,1)S(1)} %get-tuple-element.146) | copy-start | bytes 4718596
  291.1 6.6 %copy-start.30 = (bf16[256,3072]{0,1:T(8,128)(2,1)S(1)}, bf16[256,3072]{0,1:T(8,128)(2,1)}, u32[]{:S(2)}) copy-start(bf16[256,3072]{0,1:T(8,128)(2,1)} %copy.225) | copy-start | bytes 4718596
  291.1 6.6 %copy-start.31 = (bf16[256,3072]{0,1:T(8,128)(2,1)S(1)}, bf16[256,3072]{0,1:T(8,128)(2,1)}, u32[]{:S(2)}) copy-start(bf16[256,3072]{0,1:T(8,128)(2,1)} %copy.243) | copy-start | bytes 4718596
  291.2 6.6 %copy-start.43 = (f32[256,256]{1,0:T(8,128)S(1)}, f32[256,256]{1,0:T(8,128)}, u32[]{:S(2)}) copy-start(f32[256,256]{1,0:T(8,128)} %get-tuple-element.207) | copy-start | bytes 786436
  291.2 6.6 %copy-start.44 = (f32[256,256]{1,0:T(8,128)S(1)}, f32[256,256]{1,0:T(8,128)}, u32[]{:S(2)}) copy-start(f32[256,256]{1,0:T(8,128)} %fusion.61) | copy-start | bytes 786436
  291.2 6.6 %copy-start.68 = (f32[48,256]{1,0:T(8,128)S(1)}, f32[48,256]{1,0:T(8,128)}, u32[]{:S(2)}) copy-start(f32[48,256]{1,0:T(8,128)} %copy-done.67) | copy-start | bytes 147460
  316.7 5.3 copy-start.69
  322.0 8.7 %copy-start.33 = (f32[256,256]{1,0:T(8,128)S(1)}, f32[256,256]{1,0:T(8,128)}, u32[]{:S(2)}) copy-start(f32[256,256]{1,0:T(8,128)} %get-tuple-element.157) | copy-start | bytes 786436
  322.0 8.7 %copy-start.39 = (f32[256,128]{1,0:T(8,128)S(1)}, f32[256,128]{1,0:T(8,128)}, u32[]{:S(2)}) copy-start(f32[256,128]{1,0:T(8,128)} %convolution_add_fusion.3) | copy-start | bytes 393220
  331.5 71.6 %collective-permute-start = (f32[8,3328]{1,0:T(8,128)}, f32[8,3328]{1,0:T(8,128)}, u32[]{:S(2)}, u32[]{:S(2)}) collective-permute-start(f32[8,3328]{1,0:T(8,128)} %pad_maximum_fusion.6), channel_id=1, source_target_pairs={{1,0},{2,1},{3,2},{4,3},{5,4},{6,5},{7,6},{9,8},{10,9},{11,10},{12... | collective-permute-start | bytes 319496 | tf_op jit(solution)/shard_map/ppermute | solution.py:741
  333.7 5.6 copy-start.21
  339.2 7.6 %copy-start.8 = (bf16[272,1536]{1,0:T(8,128)(2,1)S(1)}, bf16[272,1536]{1,0:T(8,128)(2,1)}, u32[]{:S(2)}) copy-start(bf16[272,1536]{1,0:T(8,128)(2,1)} %copy-done.4) | copy-start | bytes 2506756
  339.2 12.8 %slice-start = ((s8[9437184]{0:T(1024)(128)(4,1)}), s8[4194304]{0:T(1024)(128)(4,1)S(1)}, s32[]{:S(2)}) async-start(s8[9437184]{0:T(1024)(128)(4,1)} %bitcast.210), calls=%async_computation | async-start | bytes 8388608
  339.2 12.8 %slice-start.1 = ((s8[9437184]{0:T(1024)(128)(4,1)}), s8[4194304]{0:T(1024)(128)(4,1)S(1)}, s32[]{:S(2)}) async-start(s8[9437184]{0:T(1024)(128)(4,1)} %bitcast.210), calls=%async_computation.1 | async-start | bytes 8388608
  346.9 5.1 slice-start.2
  365.7 35.2 %copy-start.63 = (f32[3072]{0:T(1024)S(1)}, f32[3072]{0:T(1024)}, u32[]{:S(2)}) copy-start(f32[3072]{0:T(1024)} %get-tuple-element.145) | copy-start | bytes 36868
  407.5 4.9 copy-start.9
  412.4 6.5 %copy-start.12 = (f32[272,256]{1,0:T(8,128)S(1)}, f32[272,256]{1,0:T(8,128)}, u32[]{:S(2)}) copy-start(f32[272,256]{1,0:T(8,128)} %copy-done.11) | copy-start | bytes 835588
  412.4 6.5 %copy-start.28 = (f32[264,256]{1,0:T(8,128)S(1)}, f32[264,256]{1,0:T(8,128)}, u32[]{:S(2)}) copy-start(f32[264,256]{1,0:T(8,128)} %get-tuple-element.178) | copy-start | bytes 811012
  412.4 6.5 %copy-start.29 = (f32[264,256]{1,0:T(8,128)S(1)}, f32[264,256]{1,0:T(8,128)}, u32[]{:S(2)}) copy-start(f32[264,256]{1,0:T(8,128)} %get-tuple-element.179) | copy-start | bytes 811012
  412.4 6.5 %copy-start.85 = (f32[256]{0:T(256)S(1)}, f32[256]{0:T(256)}, u32[]{:S(2)}) copy-start(f32[256]{0:T(256)} %copy-done.84) | copy-start | bytes 3076
  412.4 6.5 %copy-start.87 = (f32[256]{0:T(256)S(1)}, f32[256]{0:T(256)}, u32[]{:S(2)}) copy-start(f32[256]{0:T(256)} %copy-done.86) | copy-start | bytes 3076
  412.4 6.5 %copy-start.89 = (f32[256]{0:T(256)S(1)}, f32[256]{0:T(256)}, u32[]{:S(2)}) copy-start(f32[256]{0:T(256)} %copy-done.88) | copy-start | bytes 3076
  412.4 6.5 %copy-start.91 = (f32[256]{0:T(256)S(1)}, f32[256]{0:T(256)}, u32[]{:S(2)}) copy-start(f32[256]{0:T(256)} %copy-done.90) | copy-start | bytes 3076
  419.9 7.8 %copy-start.16 = (f32[272,1536]{1,0:T(8,128)S(1)}, f32[272,1536]{1,0:T(8,128)}, u32[]{:S(2)}) copy-start(f32[272,1536]{1,0:T(8,128)} %get-tuple-element.173) | copy-start | bytes 5013508
  419.9 7.8 %copy-start.20 = (bf16[1536,8,32]{0,2,1:T(8,128)(2,1)S(1)}, bf16[1536,8,32]{0,2,1:T(8,128)(2,1)}, u32[]{:S(2)}) copy-start(bf16[1536,8,32]{0,2,1:T(8,128)(2,1)} %copy.227) | copy-start | bytes 2359300
  419.9 7.8 %copy-start.54 = (f32[1536]{0:T(1024)S(1)}, f32[1536]{0:T(1024)}, u32[]{:S(2)}) copy-start(f32[1536]{0:T(1024)} %param.18) | copy-start | bytes 18436
  454.6 4.2 copy-start.93
  454.6 4.2 copy-start.70
  454.6 4.3 copy-start.64
  454.6 4.3 copy-start.77
  454.6 4.3 copy-start.78
  454.6 4.3 copy-start.79
  479.0 97.5 %copy-start.55 = (f32[1536]{0:T(1024)S(1)}, f32[1536]{0:T(1024)}, u32[]{:S(2)}) copy-start(f32[1536]{0:T(1024)} %param.18) | copy-start | bytes 18436
  479.0 97.5 %copy-start.98 = (f32[256]{0:T(256)S(1)}, f32[256]{0:T(256)}, u32[]{:S(2)}) copy-start(f32[256]{0:T(256)} %slice.360) | copy-start | bytes 3076
  479.0 97.5 %copy-start.99 = (f32[256]{0:T(256)S(1)}, f32[256]{0:T(256)}, u32[]{:S(2)}) copy-start(f32[256]{0:T(256)} %broadcast_multiply_fusion.5) | copy-start | bytes 3076
  567.1 9.4 %copy-start.25 = (bf16[256,1536]{1,0:T(8,128)(2,1)S(1)}, bf16[256,1536]{1,0:T(8,128)(2,1)}, u32[]{:S(2)}) copy-start(bf16[256,1536]{1,0:T(8,128)(2,1)} %param.31) | copy-start | bytes 2359300
  (41 other events, 113.4 us)

commit v2 on v1

v2 whole, which is shorter than its diff:
```python
import functools

import jax
import jax.numpy as jnp
from jax import lax
from jax.experimental import pallas as pl
from jax.experimental.pallas import tpu as pltpu
from jax.sharding import PartitionSpec as P

BLOCK = 256
epsilon = 1e-05

MESH = pl.DeviceIdType.MESH
AXES = (0, 1, 2)
SIDE = 4


def coordinates():
    dp = lax.axis_index("dp")
    t = lax.axis_index("tensor")
    z = lax.div(t, 4) * 2 + lax.div(dp, 8)
    return (lax.rem(t, 4), lax.rem(lax.div(dp, 2), 4), z), lax.rem(dp, 2)


def device(at, core):
    x, y, z = at
    return (lax.rem(z, 2) * 8 + y * 2 + core, lax.div(z, 2) * 4 + x)


def moved(at, axis, by):
    return tuple(lax.rem(v + by + SIDE, SIDE) if i == axis else v for i, v in enumerate(at))


def pieces(at, whole, width):
    x, y, z = at
    lo = pl.ds(0, 2) if 2 in whole else pl.ds(lax.rem(z, 2), 1)
    row = pl.ds(0, 4) if 1 in whole else pl.ds(y, 1)
    hi = lax.div(z, 2)
    if 0 in whole and 2 in whole:
        cols = [pl.ds(0, 8 * width)]
    elif 0 in whole:
        cols = [pl.ds(pl.multiple_of(hi * 4 * width, 128), 4 * width)]
    elif 2 in whole:
        cols = [
            pl.ds(pl.multiple_of(x * width, 128), width),
            pl.ds(pl.multiple_of((4 + x) * width, 128), width),
        ]
    else:
        cols = [pl.ds(pl.multiple_of((hi * 4 + x) * width, 128), width)]
    return [(lo, row, c) for c in cols]


def greet(at, core, group):
    barrier = pltpu.get_barrier_semaphore()
    others = [device(moved(at, axis, by), core) for axis in AXES for by in (1, -1)]
    others.append(device(at, 1 - core))
    others += group
    for other in others:
        pl.semaphore_signal(barrier, inc=1, device_id=other, device_id_type=MESH)
    pl.semaphore_wait(barrier, len(others))


def tensor_peer(by):
    return (lax.axis_index("dp"), lax.rem(lax.axis_index("tensor") + by, 8))


ROWS, WIDTH, SMALL_ROWS, SMALL_WIDTH = 96, 384, 32, 128
UNITS = [(0, q * 32, q) for q in range(3)] + [(1, 0, 0)]
WIDTHS = [WIDTH, SMALL_WIDTH]
STACK = [3, 1]


def axes_of(u):
    return [(UNITS[u][2] + j) % 3 for j in range(3)]


def region(ref, u, core, mats, where, whole, half=None):
    which, first, rows = UNITS[u][0], UNITS[u][1], 32
    if half is not None:
        first, rows = first + half * 16, 16
    return [
        ref.at[mats, lo, row, core, pl.ds(first, rows), cols]
        for lo, row, cols in pieces(where, whole, WIDTHS[which])
    ]


def sized(ref, u, mats, blocks, halves=2):
    width = WIDTHS[UNITS[u][0]]
    cols = min(blocks, 8)
    rest = blocks // cols
    return ref.at[mats, pl.ds(0, max(rest // 4, 1)), pl.ds(0, min(rest, 4)), 0, pl.ds(0, 16 * halves), pl.ds(0, cols * width)]


def gather_kernel(*refs):
    shards, small, tail, params = refs[0], refs[1], refs[2], refs[3:5]
    full, halo, params_all = refs[5:7], refs[7], refs[8:10]
    own_sem, halo_sem, param_send, param_recv, send, recv, core_send, core_recv = refs[10:]
    at, core = coordinates()
    t = lax.axis_index("tensor")
    own = []
    for w, source in enumerate((shards, small)):
        for lo, row, cols in pieces(at, (), WIDTHS[w]):
            own.append(
                pltpu.make_async_copy(source, full[w].at[:, lo.start, row.start, core, :, cols], own_sem.at[w])
            )
    def columns(i, of):
        width = params[i].shape[-1]
        return params_all[i].at[:, pl.ds(pl.multiple_of(of * width, 128), width)]

    for i in range(2):
        own.append(pltpu.make_async_copy(params[i], columns(i, t), own_sem.at[2 + i]))
    for c in own:
        c.start()
    greet(at, core, [tensor_peer(by) for by in range(1, 8)])
    last = []

    def go(copy, wait=True):
        copy.start()
        if wait:
            last.append(copy)

    def tail_copy():
        return pltpu.make_async_remote_copy(
            src_ref=tail, dst_ref=halo, send_sem=halo_sem.at[0], recv_sem=halo_sem.at[1],
            device_id=tensor_peer(1), device_id_type=MESH,
        )

    def param_copy(by, i, of):
        return pltpu.make_async_remote_copy(
            src_ref=params[i], dst_ref=columns(i, of), send_sem=param_send.at[i, by - 1],
            recv_sem=param_recv.at[i, by - 1], device_id=tensor_peer(by), device_id_type=MESH,
        )

    go(tail_copy())
    for by in range(1, 8):
        for i in range(2):
            go(param_copy(by, i, t))
    for c in own:
        c.wait()

    def slot(u, phase, m):
        return (phase if phase < 2 else 2 + m), [u]

    def mats_of(u, phase, m):
        return pl.ds(0, STACK[UNITS[u][0]]) if phase < 2 else pl.ds(m, 1)

    def sends(u, phase, m, step):
        axes = axes_of(u)
        whole, axis = axes[:phase], axes[phase]
        index = phase if phase < 2 else 2 + m
        ref = full[UNITS[u][0]]
        for kind, by in ((0, 1), (1, -1)):
            where = at if step == 0 else moved(at, axis, -by)
            for part in region(ref, u, core, mats_of(u, phase, m), where, whole, kind if step else None):
                pltpu.make_async_remote_copy(
                    src_ref=part, dst_ref=part, send_sem=send.at[u, index, step],
                    recv_sem=recv.at[u, index, step],
                    device_id=device(moved(at, axis, by), core), device_id_type=MESH,
                ).start()

    def await_step(u, phase, m, step, sem):
        index = phase if phase < 2 else 2 + m
        part = sized(full[UNITS[u][0]], u, mats_of(u, phase, m), 2 * 4**phase // (1 + step))
        pltpu.make_async_copy(part, part, sem.at[u, index, step]).wait()

    def to_partner(u, m, where, whole):
        for part in region(full[UNITS[u][0]], u, core, mats_of(u, 2, m), where, whole):
            pltpu.make_async_remote_copy(
                src_ref=part, dst_ref=part, send_sem=core_send.at[u, m],
                recv_sem=core_recv.at[u, m], device_id=device(at, 1 - core), device_id_type=MESH,
            ).start()

    everything = range(len(UNITS))
    late = [(u, m) for m in range(3) for u in everything if m < STACK[UNITS[u][0]]]
    for phase in (0, 1):
        for u in everything:
            sends(u, phase, 0, 0)
        for u in everything:
            await_step(u, phase, 0, 0, recv)
            sends(u, phase, 0, 1)
        for u in everything:
            await_step(u, phase, 0, 1, recv)
    for u, m in late:
        sends(u, 2, m, 0)
    for u, m in late:
        to_partner(u, m, at, axes_of(u)[:2])
    for u, m in late:
        await_step(u, 2, m, 0, recv)
        sends(u, 2, m, 1)
        whole, axis = axes_of(u)[:2], axes_of(u)[2]
        for by in (-1, 1):
            to_partner(u, m, moved(at, axis, by), whole)
    for u, m in late:
        await_step(u, 2, m, 1, recv)
        whole, axis = axes_of(u)[:2], axes_of(u)[2]
        to_partner(u, m, moved(at, axis, 2), whole)
    for u, m in late:
        part = sized(full[UNITS[u][0]], u, mats_of(u, 2, m), 64)
        pltpu.make_async_copy(part, part, core_recv.at[u, m]).wait()
        pltpu.make_async_copy(part, part, core_send.at[u, m]).wait()
    tail_copy().wait_recv()
    for by in range(1, 8):
        for i in range(2):
            param_copy(by, i, lax.rem(t + 8 - by, 8)).wait_recv()
    for u in everything:
        for phase in (0, 1):
            for step in (0, 1):
                await_step(u, phase, 0, step, send)
    for u, m in late:
        for step in (0, 1):
            await_step(u, 2, m, step, send)
    for c in last:
        c.wait_send()


def gather_weights(shards, small, tail, params):
    units = len(UNITS)
    return pl.pallas_call(
        gather_kernel,
        name="gather_weights",
        out_shape=[
            jax.ShapeDtypeStruct((3, 2, 4, 2, ROWS, 8 * WIDTH), jnp.bfloat16),
            jax.ShapeDtypeStruct((1, 2, 4, 2, SMALL_ROWS, 8 * SMALL_WIDTH), jnp.bfloat16),
            jax.ShapeDtypeStruct(tail.shape, tail.dtype),
        ]
        + [jax.ShapeDtypeStruct((8, 8 * p.shape[1]), p.dtype) for p in params],
        in_specs=[pl.BlockSpec(memory_space=pl.ANY)] * 5,
        out_specs=[pl.BlockSpec(memory_space=pl.ANY)] * 5,
        scratch_shapes=[
            pltpu.SemaphoreType.DMA((4,)),
            pltpu.SemaphoreType.DMA((2,)),
            pltpu.SemaphoreType.DMA((2, 7)),
            pltpu.SemaphoreType.DMA((2, 7)),
            pltpu.SemaphoreType.DMA((units, 5, 2)),
            pltpu.SemaphoreType.DMA((units, 5, 2)),
            pltpu.SemaphoreType.DMA((units, 3)),
            pltpu.SemaphoreType.DMA((units, 3)),
        ],
        compiler_params=pltpu.CompilerParams(collective_id=0, has_side_effects=True),
    )(shards, small, tail, *params)


VEC = (8, 8 * WIDTH + 384)


def spread(whole):
    return (2 if 2 in whole else 1, 4 if 1 in whole else 1, (4 if 0 in whole else 1) * (2 if 2 in whole else 1))


def half_shape(u, phase, rows):
    lo, y, cols = spread(axes_of(u)[:phase])
    which = UNITS[u][0]
    return (2, STACK[which], lo, y, rows, cols * WIDTHS[which])


def scatter_kernel(*refs):
    grads, vec = refs[0:3], refs[3]
    outs, vec_out = refs[4:6], refs[6]
    refs = refs[1:]
    own, other = refs[6:8], refs[8:10]

    def grad_of(which, m):
        return (grads[2], 0) if which else (grads[1], 0) if m == 2 else (grads[0], m)

    def load(w, m):
        ref, i = grad_of(w, m)
        return pltpu.make_async_copy(ref.at[i, :, :, core], own[w].at[m], own_sem.at[w, m])

    units = len(UNITS)
    half_buf = [[refs[10 + 3 * u + p] for p in range(3)] for u in range(units)]
    full_buf = [[refs[10 + 3 * (units + u) + p] for p in range(3)] for u in range(units)]
    rest = refs[10 + 6 * units :]
    vec_acc, vec_in, own_sem, vec_send, vec_recv, send, recv, core_send, core_recv = rest
    at, core = coordinates()
    loads = [
        [load(w, m) for m in range(STACK[w])]
        for w in range(2)
    ]
    for w in range(2):
        for c in loads[w]:
            c.start()
    greet(at, core, [device(moved(at, axis, 2), core) for axis in AXES])

    everything = range(units)
    late = [(u, m) for m in range(3) for u in everything if m < STACK[UNITS[u][0]]]

    def part_of(ref, u, mats, where, whole, half=None):
        which, first, rows = UNITS[u][0], UNITS[u][1], 32
        if half is not None:
            first, rows = first + half * 16, 16
        return [ref.at[mats, lo, y, pl.ds(first, rows), cols] for lo, y, cols in pieces(where, whole, WIDTHS[which])]

    groups = [[2], [1, -1], [0]]

    for u, m in late:
        axes = axes_of(u)
        which = UNITS[u][0]
        source, index = grad_of(which, m)
        for g, group in enumerate(groups):
            for by in group:
                where = moved(at, axes[2], by) if by else at
                for src, dst in zip(
                    region(source, u, 1 - core, pl.ds(index, 1), where, axes[:2]),
                    part_of(other[which], u, pl.ds(m, 1), where, axes[:2]),
                ):
                    pltpu.make_async_remote_copy(
                        src_ref=src, dst_ref=dst, send_sem=core_send.at[u, m], recv_sem=core_recv.at[u, m, g],
                        device_id=device(at, 1 - core), device_id_type=MESH,
                    ).start()

    def await_partner(u, m, g):
        which = UNITS[u][0]
        rows = 2 * len(groups[g])
        part = other[which].at[pl.ds(m, 1), pl.ds(0, 1), pl.ds(0, rows), pl.ds(0, 32)]
        pltpu.make_async_copy(part, part, core_recv.at[u, m, g]).wait()

    def add(u, phase, m, where, half, terms, result=None):
        which, first, rows = UNITS[u][0], UNITS[u][1], 32
        if half is not None:
            first, rows = first + half * 16, 16
        whole = axes_of(u)[:phase]
        n_lo, n_y, _ = spread(whole)
        mats = STACK[which] if m is None else 1
        for i, (lo, y, cols) in enumerate(pieces(where, whole, WIDTHS[which])):

            @pl.loop(0, mats * n_lo * n_y)
            def _(k, i=i, lo=lo, y=y, cols=cols):
                mat = lax.div(k, n_lo * n_y) if m is None else m
                a, b = lax.rem(lax.div(k, n_y), n_lo), lax.rem(k, n_y)
                here = (mat, lo.start + a, y.start + b, pl.ds(first, rows), cols)
                total = own[which][here].astype(jnp.float32)
                for term in terms:
                    total = total + term(mat, i, a, b, here).astype(jnp.float32)
                if result is None:
                    own[which][here] = total.astype(jnp.bfloat16)
                else:
                    result[mat, pl.ds(first, rows), :] = total

    def from_other(u):
        return lambda mat, i, a, b, here: other[UNITS[u][0]][here]

    def from_buf(ref, side, u, phase):
        which = UNITS[u][0]
        whole = axes_of(u)[:phase]
        width = spread(whole)[2] * WIDTHS[which] // (2 if 2 in whole and 0 not in whole else 1)
        return lambda mat, i, a, b, here: ref[side, mat, a, b, :, pl.ds(i * width, width)]

    def send_step(u, phase, m, step):
        axes = axes_of(u)
        whole, axis = axes[:phase], axes[phase]
        which = UNITS[u][0]
        mats = pl.ds(0, STACK[which]) if m is None else pl.ds(m, 1)
        index = phase if m is None else 2 + m
        buf = half_buf[u][phase] if step == 0 else full_buf[u][phase]
        for side, by in ((0, 1), (1, -1)):
            where = moved(at, axis, 2 if step == 0 else by)
            sources = part_of(own[which], u, mats, where, whole, side if step == 0 else None)
            width = buf.shape[-1] // len(sources)
            for i, src in enumerate(sources):
                pltpu.make_async_remote_copy(
                    src_ref=src, dst_ref=buf.at[side, mats, :, :, :, pl.ds(i * width, width)],
                    send_sem=send.at[u, index, step], recv_sem=recv.at[u, index, step],
                    device_id=device(moved(at, axis, by), core), device_id_type=MESH,
                ).start()

    def await_step(u, phase, m, step, sem):
        index = phase if m is None else 2 + m
        buf = half_buf[u][phase] if step == 0 else full_buf[u][phase]
        part = buf if m is None else buf.at[:, pl.ds(m, 1)]
        pltpu.make_async_copy(part, part, sem.at[u, index, step]).wait()

    def vec_copy(k):
        (x, y, z) = at
        flip = lambda v: v + 1 - 2 * lax.rem(v, 2)
        to = [
            device(at, 1 - core),
            device((flip(x), y, z), core),
            device((x, flip(y), z), core),
            device((x, y, flip(z)), core),
            device(moved(at, 0, 2), core),
            device(moved(at, 1, 2), core),
            device(moved(at, 2, 2), core),
        ][k]
        return pltpu.make_async_remote_copy(
            src_ref=vec_acc.at[k], dst_ref=vec_in.at[k], send_sem=vec_send.at[k], recv_sem=vec_recv.at[k],
            device_id=to, device_id_type=MESH,
        )

    def vec_step(k):
        if k == 0:
            vec_acc[0] = vec[...]
        else:
            vec_copy(k - 1).wait_recv()
            vec_acc[k] = vec_acc[k - 1] + vec_in[k - 1]
        if k < 7:
            vec_copy(k).start()
        else:
            vec_out[...] = vec_acc[7]

    def stage_a(m):
        for u, n in late:
            if n == m:
                axis = axes_of(u)[2]
                loads[UNITS[u][0]][m].wait() if u == 0 or u == 3 else None
                await_partner(u, m, 0)
                add(u, 2, m, moved(at, axis, 2), None, [from_other(u)])
                send_step(u, 2, m, 0)

    def stage_b(m):
        for u, n in late:
            if n == m:
                axis = axes_of(u)[2]
                await_partner(u, m, 1)
                await_step(u, 2, m, 0, recv)
                for side, by in ((0, 1), (1, -1)):
                    where = moved(at, axis, by)
                    add(u, 2, m, where, side, [from_other(u), from_buf(half_buf[u][2], side, u, 2)])
                    add(u, 2, m, where, 1 - side, [from_other(u)])
                send_step(u, 2, m, 1)

    def stage_c(m):
        for u, n in late:
            if n == m:
                await_partner(u, m, 2)
                await_step(u, 2, m, 1, recv)
                add(u, 2, m, at, None, [from_other(u)] + [from_buf(full_buf[u][2], side, u, 2) for side in (0, 1)])

    vec_step(0)
    stage_a(0)
    stage_a(1)
    vec_step(1)
    stage_b(0)
    stage_a(2)
    vec_step(2)
    stage_b(1)
    vec_step(3)
    stage_c(0)
    vec_step(4)
    stage_b(2)
    vec_step(5)
    stage_c(1)
    vec_step(6)
    stage_c(2)
    vec_step(7)
    for phase in (1, 0):
        for u in everything:
            send_step(u, phase, None, 0)
        for u in everything:
            axis = axes_of(u)[phase]
            await_step(u, phase, None, 0, recv)
            for side, by in ((0, 1), (1, -1)):
                add(u, phase, None, moved(at, axis, by), side, [from_buf(half_buf[u][phase], side, u, phase)])
            send_step(u, phase, None, 1)
        for u in everything:
            await_step(u, phase, None, 1, recv)
            add(
                u, phase, None, at, None, [from_buf(full_buf[u][phase], side, u, phase) for side in (0, 1)],
                None if phase else outs[UNITS[u][0]],
            )
    for u, m in late:
        part = other[UNITS[u][0]].at[pl.ds(m, 1), :, :, pl.ds(0, 32)]
        pltpu.make_async_copy(part, part, core_send.at[u, m]).wait()
        for step in (0, 1):
            await_step(u, 2, m, step, send)
    for u in everything:
        for phase in (0, 1):
            for step in (0, 1):
                await_step(u, phase, None, step, send)
    for k in range(7):
        vec_copy(k).wait_send()


def scatter_grads(main, out, small, vec):
    units = range(len(UNITS))
    n = len(UNITS)
    held = [(3, 2, 4, ROWS, 8 * WIDTH), (1, 2, 4, SMALL_ROWS, 8 * SMALL_WIDTH)]
    return pl.pallas_call(
        scatter_kernel,
        name="scatter_grads",
        out_shape=[
            jax.ShapeDtypeStruct((3, ROWS, WIDTH), jnp.float32),
            jax.ShapeDtypeStruct((1, SMALL_ROWS, SMALL_WIDTH), jnp.float32),
            jax.ShapeDtypeStruct(VEC, jnp.float32),
        ],
        in_specs=[pl.BlockSpec(memory_space=pl.ANY)] * 3 + [pl.BlockSpec(memory_space=pltpu.VMEM)],
        out_specs=[pl.BlockSpec(memory_space=pltpu.VMEM)] * 3,
        scratch_shapes=[pltpu.VMEM(s, jnp.bfloat16) for s in held + held]
        + [pltpu.VMEM(half_shape(u, p, 16), jnp.bfloat16) for u in units for p in range(3)]
        + [pltpu.VMEM(half_shape(u, p, 32), jnp.bfloat16) for u in units for p in range(3)]
        + [
            pltpu.VMEM((8,) + VEC, jnp.float32),
            pltpu.VMEM((7,) + VEC, jnp.float32),
            pltpu.SemaphoreType.DMA((2, 3)),
            pltpu.SemaphoreType.DMA((7,)),
            pltpu.SemaphoreType.DMA((7,)),
            pltpu.SemaphoreType.DMA((n, 5, 2)),
            pltpu.SemaphoreType.DMA((n, 5, 2)),
            pltpu.SemaphoreType.DMA((n, 3)),
            pltpu.SemaphoreType.DMA((n, 3, 3)),
        ],
        compiler_params=pltpu.CompilerParams(
            collective_id=3, has_side_effects=True, vmem_limit_bytes=58 * 2**20
        ),
    )(main, out, small, vec)


D, DI, HEADS, HEAD_DIM, STATE, TAPS, HALO = 1536, 3072, 48, 64, 128, 4, 16
BF16, F32 = jnp.bfloat16, jnp.float32
TILE, LANES, SMALL = 512, 128, 384
TILES = DI // TILE
LOG2E = 1.4426950408889634
EXT = HALO + BLOCK
VMEM = pltpu.VMEM


def dot(a, b, dims=(1, 0), precision=None):
    return lax.dot_general(
        a, b, ((dims[:1], dims[1:]), ((), ())), precision=precision, preferred_element_type=F32
    )


def iota(shape, dim):
    return lax.broadcasted_iota(jnp.int32, shape, dim)


def sigmoid(v):
    return 1.0 / (1.0 + jnp.exp(-v))


def silu(v):
    return v * sigmoid(v)


def silu_slope(v):
    s = sigmoid(v)
    return s * (1.0 + v * (1.0 - s))


def softplus(v):
    return jnp.maximum(v, 0.0) + jnp.log1p(jnp.exp(-jnp.abs(v)))


def split(v):
    high = v.astype(BF16)
    return high, (v - high.astype(F32)).astype(BF16)


def head_map(j):
    return (iota((LANES, TILE), 0) == j * (TILE // HEAD_DIM) + iota((LANES, TILE), 1) // HEAD_DIM).astype(BF16)


def widen(v, j):
    high, low = split(v)
    return dot(high, head_map(j)) + dot(low, head_map(j))


def by_head(v, j):
    high, low = split(v)
    return dot(high, head_map(j), (1, 1)) + dot(low, head_map(j), (1, 1))


def small_map(r):
    row, col = iota((8 * LANES, SMALL), 0), iota((8 * LANES, SMALL), 1)
    t, lane = row // LANES, row % LANES - 38 * r
    state = (lane >= 0) & (lane < 32) & (col == t * 32 + lane)
    step = (lane >= 32) & (lane < 38) & (col == 256 + t * 6 + lane - 32)
    return (state | step).astype(BF16)


def tile_of(j):
    return pl.ds(pl.multiple_of(j * TILE, TILE), TILE)


def conv_links(doc_col, offset, rows):
    return (doc_col[HALO : HALO + rows] == doc_col[HALO - offset : HALO - offset + rows]).astype(F32)


def conv(ext, taps, bias, links):
    total = bias + taps[TAPS - 1 : TAPS] * ext[HALO:]
    for offset in range(1, TAPS):
        total = total + taps[TAPS - 1 - offset : TAPS - offset] * ext[HALO - offset : EXT - offset] * links[offset]
    return total


def small_params(phead):
    return dot(phead, small_map(0).astype(F32), precision=lax.Precision.HIGHEST)


def decay_terms(step, cum, doc_col, doc_prev):
    block = doc_col[HALO:EXT]
    end = cum[BLOCK - 1 : BLOCK]
    tail = jnp.exp(end - cum) * (block == block[BLOCK - 1 : BLOCK]).astype(F32)
    enter = jnp.exp(cum) * (block == doc_prev).astype(F32)
    keep = jnp.exp(end) * (block[BLOCK - 1 : BLOCK] == doc_prev).astype(F32)
    return enter, tail, tail * step, keep


def front_kernel(
    hidden, halo, gain, full, packed, pmain, phead, doc_col,
    normed_out, x_ext, x_pre, x_act, gate_in, update, raw_out, state_pre, bc, steps, scores,
    w_small, w_x, w_gate, normed, weight_ref, sems,
):
    loads = []
    for m, w in ((0, w_x), (1, w_gate)):
        for j in range(TILES):
            cols = pl.ds(j * TILE, TILE)
            loads.append(pltpu.make_async_copy(full.at[m, :, cols], w.at[:, cols], sems.at[m, j]))
    for c in loads:
        c.start()
    for rows, part in ((pl.ds(0, HALO), halo), (pl.ds(HALO, BLOCK), hidden)):
        value = part[...].astype(F32)
        inv = lax.rsqrt(jnp.mean(value * value, axis=1, keepdims=True) + epsilon)
        normed[rows] = (value * inv * gain[...]).astype(BF16)
    normed_out[...] = normed[pl.ds(HALO, BLOCK)]
    for r in range(3):
        rows = dot(packed[...], small_map(r)).astype(BF16)
        for d in range(16):
            w_small[pl.ds(d * 96 + r * 32, 32)] = rows[d * 32 : d * 32 + 32]
    raw = dot(normed[...], w_small[...])
    raw_out[...] = raw
    params = small_params(phead[...])
    docs = doc_col[...]
    links = [None] + [conv_links(docs, o, BLOCK) for o in range(1, TAPS)]
    pre = conv(raw[:, :256], params[:TAPS, :256], params[TAPS : TAPS + 1, :256], links)
    state_pre[...] = pre
    act = silu(pre).astype(BF16)
    bc[...] = act
    b_rows, c_rows = act[:, :STATE], act[:, STATE:]
    scores[...] = dot(c_rows, b_rows, (1, 1))
    step_in = raw[HALO:, 256:] + params[5:6, 256:]
    step = softplus(step_in)
    log_step = step * -jnp.exp(params[6:7, 256:])
    lower = (iota((BLOCK, BLOCK), 0) >= iota((BLOCK, BLOCK), 1)).astype(F32)
    cum = dot(lower, log_step, precision=lax.Precision.HIGHEST)
    steps[0] = step_in
    steps[1] = step
    steps[2] = cum
    weight_ref[...] = decay_terms(step, cum, docs, docs[HALO - 1 : HALO])[2]

    @pl.loop(0, TILES)
    def _(j):
        cols = tile_of(j)
        pltpu.make_async_copy(full.at[0, :, cols], w_x.at[:, cols], sems.at[0, j]).wait()
        ext = dot(normed[...], w_x[:, cols])
        x_ext[:, cols] = ext
        pre = conv(ext, pmain[0:TAPS, cols], pmain[TAPS : TAPS + 1, cols], links)
        x_pre[:, cols] = pre
        act = silu(pre).astype(BF16)
        x_act[:, cols] = act
        heavy = (act.astype(F32) * widen(weight_ref[...], j)).astype(BF16)
        update[:, cols] = dot(bc[:, :STATE], heavy, (0, 0))

    @pl.loop(0, TILES)
    def _(j):
        cols = tile_of(j)
        pltpu.make_async_copy(full.at[1, :, cols], w_gate.at[:, cols], sems.at[1, j]).wait()
        gate_in[:, cols] = dot(normed[pl.ds(HALO, BLOCK)], w_gate[:, cols])


def front(hidden, halo, gain, full, packed, pmain, phead, doc_col):
    shapes = [
        ((BLOCK, D), BF16), ((EXT, DI), F32), ((BLOCK, DI), F32), ((BLOCK, DI), BF16), ((BLOCK, DI), F32),
        ((STATE, DI), F32), ((EXT, SMALL), F32), ((BLOCK, 256), F32), ((BLOCK, 256), BF16),
        ((3, BLOCK, LANES), F32), ((BLOCK, BLOCK), F32), ((D, SMALL), BF16),
    ]
    vmem = pl.BlockSpec(memory_space=VMEM)
    return pl.pallas_call(
        front_kernel,
        name="front",
        out_shape=[jax.ShapeDtypeStruct(*s) for s in shapes],
        in_specs=[vmem] * 3 + [pl.BlockSpec(memory_space=pl.ANY)] + [vmem] * 4,
        out_specs=[vmem] * len(shapes),
        scratch_shapes=[
            VMEM((D, DI), BF16), VMEM((D, DI), BF16), VMEM((EXT, D), BF16),
            VMEM((BLOCK, LANES), F32), pltpu.SemaphoreType.DMA((2, TILES)),
        ],
        compiler_params=pltpu.CompilerParams(vmem_limit_bytes=58 * 2**20),
    )(hidden, halo, gain, full, packed, pmain, phead, doc_col)


def pack_params(conv_main, conv_main_bias, conv_state, conv_state_bias, step_bias, decay_log, skip_gain, gate_gain):
    main = jnp.concatenate(
        [conv_main, conv_main_bias[None], gate_gain[None], jnp.repeat(skip_gain, HEAD_DIM)[None],
         jnp.zeros((1, WIDTH), F32)]
    )
    state = jnp.pad(jnp.concatenate([conv_state, conv_state_bias[None]]), ((0, 3), (0, 96)))
    heads = jnp.pad(jnp.stack([step_bias, decay_log, skip_gain]), ((5, 0), (32, 90)))
    return main, state + heads


PAIR = 2 * HEAD_DIM
PAIRS = DI // PAIR
HALF = BLOCK // 2
FORWARD_LAG, BACKWARD_LAG = 4, 2


def pair_of(p):
    return pl.ds(pl.multiple_of(p * PAIR, PAIR), PAIR)


def only(value, first):
    lane = iota(value.shape, 1)
    return jnp.where((lane < HEAD_DIM) == first, value, jnp.zeros_like(value))


def head_column(ref, h):
    return pltpu.roll(ref[...], lax.rem(LANES - h, LANES), axis=1)[:, :1]


def mid_kernel(
    x_act, gate_in, update, bc, steps, scores, doc_col, doc_row, pmain, phead, hidden, cot, full,
    mixed, grad_out, grad_gate_in, grad_x, grad_bc, grad_step_in, vec_gate, vec_heads,
    w_out, cot_t, grad_add, y, work, gate_out, dy, state, state_low, grad_state, keep_row, f_out, f_in, b_out, b_in,
    barred, cum2, cum_t, step_t, enter_ref, weight_ref, rows_acc, q_t, gs, acc_c, acc_heads, row_acc,
    w_sem, f_send, f_recv, b_send, b_recv,
):
    t = lax.axis_index("tensor")
    load = pltpu.make_async_copy(full.at[2], w_out, w_sem.at[0])
    load.start()
    barrier = pltpu.get_barrier_semaphore()
    for other in (tensor_peer(1), tensor_peer(7)):
        pl.semaphore_signal(barrier, inc=1, device_id=other, device_id_type=MESH)
    pl.semaphore_wait(barrier, 2)

    docs = doc_col[...]
    params = small_params(phead[...])
    rate = -jnp.exp(params[6:7, 256:])
    step, cum = steps[1], steps[2]
    enter, tail, weight, keep = decay_terms(step, cum, docs, docs[HALO - 1 : HALO])
    enter_ref[...] = enter
    weight_ref[...] = weight
    cum2[...] = cum * LOG2E
    for ref, turned in ((cum_t, (cum * LOG2E).T), (step_t, step.T)):
        for h in range(HEADS):
            ref[h] = turned[h : h + 1]
    linked = (docs[HALO:EXT] == doc_row[...]) & (iota((BLOCK, BLOCK), 0) >= iota((BLOCK, BLOCK), 1))
    barred[...] = jnp.where(linked, 0.0, -1e30)
    keep8 = jnp.broadcast_to(keep, (8, LANES))
    cot_t[...] = cot[...].T

    @pl.loop(0, TILES)
    def _(j):
        keep_row[:, tile_of(j)] = widen(keep8, j)

    def chain(forward, c, add, into, outgoing, incoming, send, recv):
        cols = pair_of(c)
        by = 1 if forward else 7
        is_first = t == (0 if forward else 7)
        is_last = t == (7 if forward else 0)

        def copy():
            return pltpu.make_async_remote_copy(
                src_ref=outgoing.at[:, cols], dst_ref=incoming.at[:, cols], send_sem=send.at[c],
                recv_sem=recv.at[c], device_id=tensor_peer(by), device_id_type=MESH,
            )

        @pl.when(is_first)
        def _():
            into[:, cols] = jnp.zeros((STATE, PAIR), F32)

        @pl.when(jnp.logical_not(is_first))
        def _():
            copy().wait_recv()
            into[:, cols] = incoming[:, cols].astype(F32)

        @pl.when(jnp.logical_not(is_last))
        def _():
            outgoing[:, cols] = (keep_row[0:1, cols] * into[:, cols] + add[:, cols]).astype(BF16)
            copy().start()

        return copy

    halves = [(slice(0, HALF), slice(0, HALF)), (slice(HALF, BLOCK), slice(0, BLOCK))]

    def decay_of(h, column, rows, cols):
        return jnp.exp2(column[rows] - cum_t[h, :, cols] + barred[rows, cols])

    def intra_forward(p):
        cols = pair_of(p)
        x = x_act[:, cols]
        x2 = [only(x, True), only(x, False)]
        columns = [head_column(cum2, 2 * p + k) for k in (0, 1)]
        for rows, js in halves:
            mix = [
                (scores[rows, js] * (decay_of(2 * p + k, columns[k], rows, js) * step_t[2 * p + k, :, js])).astype(BF16)
                for k in (0, 1)
            ]
            y[rows, cols] = dot(jnp.concatenate(mix, 1), jnp.concatenate([v[js] for v in x2], 0))

    lag = FORWARD_LAG * t

    @pl.loop(0, PAIRS + lag)
    def _(i):
        @pl.when(i < PAIRS)
        def _():
            intra_forward(i)

        @pl.when(i >= lag)
        def _():
            chain(True, i - lag, update, state, f_out, f_in, f_send, f_recv)

    row_acc[...] = jnp.zeros_like(row_acc)

    @pl.loop(0, TILES)
    def _(j):
        cols = tile_of(j)
        low = state[:, cols].astype(BF16)
        state_low[:, cols] = low
        carried = dot(bc[:, STATE:], low)
        value = y[:, cols] + carried * widen(enter_ref[...], j) + pmain[6:7, cols] * x_act[:, cols].astype(F32)
        y[:, cols] = value
        gated = value * silu(gate_in[:, cols])
        row_acc[...] += jnp.broadcast_to(jnp.sum(gated * gated, axis=1, keepdims=True), (BLOCK, LANES))

    gate_inv = lax.rsqrt(row_acc[:, :1] / DI + epsilon)
    row_acc[...] = jnp.zeros_like(row_acc)
    load.wait()

    @pl.loop(0, TILES)
    def _(j):
        cols = tile_of(j)
        gated = y[:, cols] * silu(gate_in[:, cols])
        hat = gated * gate_inv
        gain = pmain[5:6, cols]
        out = (hat * gain).astype(BF16)
        gate_out[:, cols] = out
        grad_out[:, cols] = dot(cot_t[...], out).astype(BF16)
        grad_gate = dot(cot[...], w_out[:, cols])
        vec_gate[:, cols] = jnp.broadcast_to(jnp.sum(grad_gate * hat, axis=0, keepdims=True), (8, TILE))
        dn = grad_gate * gain
        work[:, cols] = dn
        row_acc[...] += jnp.broadcast_to(jnp.sum(dn * gated, axis=1, keepdims=True), (BLOCK, LANES))

    inner = row_acc[:, :1] / DI * gate_inv * gate_inv * gate_inv
    acc_c[...] = jnp.zeros_like(acc_c)
    acc_heads[...] = jnp.zeros_like(acc_heads)

    @pl.loop(0, TILES)
    def _(j):
        cols = tile_of(j)
        gate, value = gate_in[:, cols], y[:, cols]
        s = sigmoid(gate)
        act = gate * s
        grad_gated = gate_inv * work[:, cols] - value * act * inner
        grad = (grad_gated * act).astype(BF16)
        dy[:, cols] = grad
        grad_gate_in[:, cols] = (grad_gated * value * (s * (1.0 + gate * (1.0 - s)))).astype(BF16)
        grad = grad.astype(F32)
        carried_grad = (grad * widen(enter_ref[...], j)).astype(BF16)
        low = state_low[:, cols]
        work_cols = dot(bc[:, STATE:], carried_grad, (0, 0))
        grad_add[:, cols] = work_cols
        acc_c[...] += dot(carried_grad, low, (1, 1))
        acc_heads[0] += by_head(grad * dot(bc[:, STATE:], low), j)

    rows_acc[...] = jnp.zeros_like(rows_acc)
    gs[...] = jnp.zeros_like(gs)

    def intra_backward(p):
        cols = pair_of(p)
        x, grad = x_act[:, cols], dy[:, cols]
        grad2 = [only(grad, True), only(grad, False)]
        columns = [head_column(cum2, 2 * p + k) for k in (0, 1)]
        lane = iota((HALF, LANES), 1)
        parts = []
        q_rows = [[], []]
        for rows, js in halves:
            mixes = []
            gs_sum = gs[rows, js]
            pulls = jnp.zeros((HALF, LANES), F32)
            for k in (0, 1):
                h = 2 * p + k
                decay = decay_of(h, columns[k], rows, js)
                decay_step = decay * step_t[h, :, js]
                mixes.append((scores[rows, js] * decay_step).astype(BF16))
                grad_mix = dot(grad2[k][rows], x[js], (1, 1))
                gs_sum = gs_sum + grad_mix * decay_step
                q = grad_mix * scores[rows, js] * decay
                q_rows[k].append(jnp.sum(q, axis=0, keepdims=True))
                pull = jnp.sum(q * step_t[h, :, js], axis=1, keepdims=True)
                pulls = jnp.where(lane == h, pull, pulls)
            gs[rows, js] = gs_sum
            rows_acc[rows] += pulls
            parts.append(dot(jnp.concatenate(mixes, 0), jnp.concatenate([v[rows] for v in grad2], 0), (0, 0)))
        grad_x[pl.ds(0, HALF), cols] = parts[0] + parts[1][:HALF]
        grad_x[pl.ds(HALF, HALF), cols] = parts[1][HALF:]
        for k in (0, 1):
            first, second = q_rows[k]
            q_t[2 * p + k, :, 0:HALF] = first + second[:, :HALF]
            q_t[2 * p + k, :, HALF:BLOCK] = second[:, HALF:]

    back_lag = BACKWARD_LAG * (7 - t)

    @pl.loop(0, PAIRS + back_lag)
    def _(i):
        @pl.when(i < PAIRS)
        def _():
            intra_backward(i)

        @pl.when(i >= back_lag)
        def _():
            chain(False, i - back_lag, grad_add, grad_state, b_out, b_in, b_send, b_recv)

    gs_low = gs[...].astype(BF16)
    grad_bc[:, STATE:] = acc_c[...] + dot(gs_low, bc[:, :STATE])
    acc_c[...] = dot(gs_low, bc[:, STATE:], (0, 0))

    @pl.loop(0, TILES)
    def _(j):
        cols = tile_of(j)
        wide = widen(weight_ref[...], j)
        grad_update = grad_state[:, cols].astype(BF16)
        spread_grad = dot(bc[:, :STATE], grad_update)
        x, grad = x_act[:, cols].astype(F32), dy[:, cols].astype(F32)
        grad_x[:, cols] += wide * spread_grad + pmain[6:7, cols] * grad
        acc_heads[1] += by_head(x * spread_grad, j)
        acc_c[...] += dot((x * wide).astype(BF16), grad_update, (1, 1))
        kept = jnp.sum(grad_state[:, cols] * state[:, cols], axis=0, keepdims=True)
        skip = jnp.sum(x * grad, axis=0, keepdims=True)
        row = iota((8, TILE), 0)
        both = jnp.where(row == 0, kept, jnp.where(row == 1, skip, 0.0))
        acc_heads[2, 0:8] += by_head(both, j)

    grad_bc[:, :STATE] = acc_c[...]
    grad_weight = acc_heads[1]
    q = jnp.concatenate([q_t[h] for h in range(HEADS)] + [jnp.zeros((LANES - HEADS, BLOCK), F32)], 0).T
    weight_pull = grad_weight * weight
    grad_end = jnp.sum(weight_pull, axis=0, keepdims=True) + acc_heads[2, 0:1] * keep
    grad_cum = rows_acc[...] - step * q + enter * acc_heads[0] - weight_pull
    grad_cum = grad_cum + jnp.where(iota((BLOCK, LANES), 0) == BLOCK - 1, grad_end, 0.0)
    upper = (iota((BLOCK, BLOCK), 0) <= iota((BLOCK, BLOCK), 1)).astype(F32)
    grad_log = dot(upper, grad_cum, precision=lax.Precision.HIGHEST)
    grad_step = q + grad_weight * tail + rate * grad_log
    grad_in = grad_step * sigmoid(steps[0])
    grad_step_in[...] = grad_in
    row = iota((8, LANES), 0)
    heads = jnp.where(row == 5, jnp.sum(grad_in, axis=0, keepdims=True), 0.0)
    heads = jnp.where(row == 6, rate * jnp.sum(grad_log * step, axis=0, keepdims=True), heads)
    vec_heads[...] = jnp.where(row == 7, acc_heads[2, 1:2], heads)

    @pl.loop(0, D // TILE)
    def _(j):
        cols = tile_of(j)
        part = dot(gate_out[...], w_out[cols, :], (1, 1))
        mixed[:, cols] = (hidden[:, cols].astype(F32) + part).astype(BF16)

    for by, ends, outgoing, incoming, send, recv in (
        (1, 7, f_out, f_in, f_send, f_recv),
        (7, 0, b_out, b_in, b_send, b_recv),
    ):

        @pl.when(t != ends)
        def _(by=by, outgoing=outgoing, incoming=incoming, send=send, recv=recv):
            @pl.loop(0, PAIRS)
            def _(c):
                pltpu.make_async_remote_copy(
                    src_ref=outgoing.at[:, pair_of(c)], dst_ref=incoming.at[:, pair_of(c)], send_sem=send.at[c],
                    recv_sem=recv.at[c], device_id=tensor_peer(by), device_id_type=MESH,
                ).wait_send()


def mid(x_act, gate_in, update, bc, steps, scores, doc_col, doc_row, pmain, phead, hidden, cot, full):
    vmem = pl.BlockSpec(memory_space=VMEM)
    shapes = [
        ((BLOCK, D), BF16), ((D, DI), BF16), ((BLOCK, DI), BF16), ((BLOCK, DI), F32), ((BLOCK, 256), F32),
        ((BLOCK, LANES), F32), ((8, DI), F32), ((8, LANES), F32),
    ]
    wide, heads, square = (BLOCK, DI), (BLOCK, LANES), (BLOCK, BLOCK)
    turned = (HEADS, 1, BLOCK)
    scratch = [
        ((D, DI), BF16), ((D, BLOCK), BF16), ((STATE, DI), F32), (wide, F32), (wide, F32), (wide, BF16), (wide, BF16),
        ((STATE, DI), F32), ((STATE, DI), BF16), ((STATE, DI), F32), ((8, DI), F32),
        ((STATE, DI), BF16), ((STATE, DI), BF16), ((STATE, DI), BF16), ((STATE, DI), BF16),
        (square, F32), (heads, F32), (turned, F32), (turned, F32), (heads, F32), (heads, F32),
        (heads, F32), (turned, F32), (square, F32), (heads, F32), ((3,) + heads, F32), (heads, F32),
    ]
    return pl.pallas_call(
        mid_kernel,
        name="scan_and_gate",
        out_shape=[jax.ShapeDtypeStruct(*s) for s in shapes],
        in_specs=[vmem] * 12 + [pl.BlockSpec(memory_space=pl.ANY)],
        out_specs=[vmem] * len(shapes),
        scratch_shapes=[VMEM(*s) for s in scratch]
        + [pltpu.SemaphoreType.DMA((1,))]
        + [pltpu.SemaphoreType.DMA((PAIRS,))] * 4,
        compiler_params=pltpu.CompilerParams(
            collective_id=1, has_side_effects=True, vmem_limit_bytes=60 * 2**20
        ),
    )(x_act, gate_in, update, bc, steps, scores, doc_col, doc_row, pmain, phead, hidden, cot, full)


def tail_kernel(
    normed, x_ext, x_pre, grad_x, after, raw_ext, state_pre, grad_bc, grad_gate_in, grad_step_in, w_small, pmain, phead,
    doc_col, hidden, cot, gain, vec_gate, vec_heads, full,
    grad_main, grad_small, grad_hidden, vec,
    w_x, w_gate, normed_t, acc, small_acc, staged, sems, out_sems,
):
    loads = []
    for m, w in ((0, w_x), (1, w_gate)):
        for j in range(TILES):
            cols = pl.ds(j * TILE, TILE)
            loads.append(pltpu.make_async_copy(full.at[m, :, cols], w.at[:, cols], sems.at[m, j]))
    for c in loads:
        c.start()
    normed_t[...] = normed[...].T
    docs = doc_col[...]
    links = [None] + [conv_links(docs, o, BLOCK + 8) for o in range(1, TAPS)]
    params = small_params(phead[...])
    vec[...] = jnp.zeros_like(vec)

    def conv_back(grad, grad_after, ext, taps):
        grad_ext = jnp.concatenate([grad, grad_after], 0)
        total = taps[TAPS - 1 : TAPS] * grad
        rows = [None] * TAPS
        rows[TAPS - 1] = jnp.sum(grad * ext[HALO:], axis=0, keepdims=True)
        for offset in range(1, TAPS):
            masked = grad_ext * links[offset]
            rows[TAPS - 1 - offset] = jnp.sum(masked[:BLOCK] * ext[HALO - offset : EXT - offset], axis=0, keepdims=True)
            total = total + taps[TAPS - 1 - offset : TAPS - offset] * masked[offset : offset + BLOCK]
        return total, rows + [jnp.sum(grad, axis=0, keepdims=True)]

    grad = grad_bc[...] * silu_slope(state_pre[...])
    total, rows = conv_back(grad, after[:, DI:], raw_ext[:, :256], params[:TAPS, :256])
    for i, row in enumerate(rows):
        vec[i : i + 1, DI : DI + 256] = row
    raw = jnp.concatenate([total.astype(BF16), grad_step_in[...].astype(BF16)], 1)
    acc[...] = dot(raw, w_small[...], (1, 1))
    small_acc[...] = dot(normed_t[...], raw).astype(BF16)
    packed = jnp.zeros((512, 8 * LANES), F32)
    for r in range(3):
        rows_r = jnp.concatenate([small_acc[pl.ds(d * 96 + r * 32, 32)] for d in range(16)], 0)
        packed = packed + dot(rows_r, small_map(r), (1, 1))
    grad_small[...] = packed.astype(BF16)

    def put(m, j, slot):
        return pltpu.make_async_copy(staged.at[slot], grad_main.at[m, :, tile_of(j)], out_sems.at[slot])

    def project(m, j, grad, w):
        slot = lax.rem(j, 2)

        @pl.when(j >= 2)
        def _():
            put(m, j, slot).wait()

        staged[slot] = dot(normed_t[...], grad).astype(BF16)
        put(m, j, slot).start()
        acc[...] += dot(grad, w[:, tile_of(j)], (1, 1))

    @pl.loop(0, TILES)
    def _(j):
        cols = tile_of(j)
        pltpu.make_async_copy(full.at[0, :, cols], w_x.at[:, cols], sems.at[0, j]).wait()
        grad = grad_x[:, cols] * silu_slope(x_pre[:, cols])
        total, rows = conv_back(grad, after[:, cols], x_ext[:, cols], pmain[0:TAPS, cols])
        for i, row in enumerate(rows):
            vec[i : i + 1, cols] = row
        project(0, j, total.astype(BF16), w_x)

    for slot in range(2):
        put(0, TILES - 2 + slot, slot).wait()

    @pl.loop(0, TILES)
    def _(j):
        cols = tile_of(j)
        pltpu.make_async_copy(full.at[1, :, cols], w_gate.at[:, cols], sems.at[1, j]).wait()
        project(1, j, grad_gate_in[:, cols], w_gate)

    for slot in range(2):
        put(1, TILES - 2 + slot, slot).wait()

    value = hidden[...].astype(F32)
    inv = lax.rsqrt(jnp.mean(value * value, axis=1, keepdims=True) + epsilon)
    rows = value * inv
    grad = acc[...]
    vec[5:6, 0:DI] = vec_gate[0:1, :]
    vec[6:7, 0:D] = jnp.sum(grad * rows, axis=0, keepdims=True)
    vec[5:8, DI + 256 :] = vec_heads[5:8, :]
    dn = grad * gain[...]
    mean = jnp.mean(dn * rows, axis=1, keepdims=True)
    grad_hidden[...] = cot[...].astype(F32) + inv * dn - rows * inv * mean


def tail(*args):
    vmem = pl.BlockSpec(memory_space=VMEM)
    anywhere = pl.BlockSpec(memory_space=pl.ANY)
    return pl.pallas_call(
        tail_kernel,
        name="project_back",
        out_shape=[
            jax.ShapeDtypeStruct((2, D, DI), BF16),
            jax.ShapeDtypeStruct((512, 8 * LANES), BF16),
            jax.ShapeDtypeStruct((BLOCK, D), F32),
            jax.ShapeDtypeStruct(VEC, F32),
        ],
        in_specs=[vmem] * 19 + [anywhere],
        out_specs=[anywhere, vmem, vmem, vmem],
        scratch_shapes=[
            VMEM((D, DI), BF16), VMEM((D, DI), BF16), VMEM((D, BLOCK), BF16), VMEM((BLOCK, D), F32),
            VMEM((D, SMALL), BF16), VMEM((2, D, TILE), BF16),
            pltpu.SemaphoreType.DMA((2, TILES)), pltpu.SemaphoreType.DMA((2,)),
        ],
        compiler_params=pltpu.CompilerParams(vmem_limit_bytes=60 * 2**20),
    )(*args)


def per_device(
    hidden,
    doc_ids,
    norm_gain,
    main_proj,
    step_proj,
    state_proj,
    conv_main,
    conv_main_bias,
    conv_state,
    conv_state_bias,
    step_bias,
    decay_log,
    skip_gain,
    gate_gain,
    out_proj,
    cotangent,
):
    t = lax.axis_index("tensor")
    shards = jnp.stack([main_proj[:, 1], main_proj[:, 0], out_proj])
    small = jnp.concatenate([state_proj, step_proj], axis=1).reshape(3, SMALL_ROWS, 38)
    small = jnp.pad(small.transpose(1, 0, 2).reshape(SMALL_ROWS, 114), ((0, 0), (0, 14)))[None]
    params = pack_params(
        conv_main, conv_main_bias, conv_state, conv_state_bias, step_bias, decay_log, skip_gain, gate_gain
    )
    full, packed, halo, pmain, phead = gather_weights(shards, small, hidden[BLOCK - HALO :], params)
    full, packed = full.reshape(3, D, DI), packed.reshape(512, 8 * LANES)
    gain = norm_gain[None]

    docs_all = jnp.concatenate([jnp.full((HALO,), -1, jnp.int32), doc_ids, jnp.full((16,), -2, jnp.int32)])
    docs = lax.dynamic_slice(docs_all, (t * BLOCK,), (EXT + 16,))
    doc_col, doc_row = docs[:, None], docs[None, HALO:EXT]

    normed, x_ext, x_pre, x_act, gate_in, update, raw, state_pre, bc, steps, scores, w_small = front(
        hidden, halo, gain, full, packed, pmain, phead, doc_col
    )
    mixed, grad_out, grad_gate_in, grad_x, grad_bc, grad_step_in, vec_gate, vec_heads = mid(
        x_act, gate_in, update, bc, steps, scores, doc_col, doc_row, pmain, phead, hidden, cotangent, full
    )
    first = jnp.concatenate(
        [grad_x[:8] * silu_slope(x_pre[:8]), grad_bc[:8] * silu_slope(state_pre[:8])], axis=1
    )
    after = lax.ppermute(first, "tensor", [(i, i - 1) for i in range(1, 8)])
    grad_main, grad_small, grad_hidden, vec = tail(
        normed, x_ext, x_pre, grad_x, after, raw, state_pre, grad_bc, grad_gate_in, grad_step_in, w_small, pmain,
        phead, doc_col, hidden, cotangent, gain, vec_gate, vec_heads, full,
    )
    own_main, own_small, vec = scatter_grads(
        grad_main.reshape(2, 2, 4, 2, ROWS, DI), grad_out.reshape(1, 2, 4, 2, ROWS, DI),
        grad_small.reshape(1, 2, 4, 2, SMALL_ROWS, 8 * LANES), vec,
    )
    own_small = own_small[0, :, :114].reshape(SMALL_ROWS, 3, 38).transpose(1, 0, 2).reshape(ROWS, 38)
    vec_main = lax.dynamic_slice(vec, (0, t * WIDTH), (8, WIDTH))
    vec_state = lax.dynamic_slice(vec, (0, DI + t * 32), (5, 32))
    vec_head = lax.dynamic_slice(vec, (5, DI + 256 + t * 6), (3, 6))
    return (
        mixed,
        grad_hidden,
        vec[6, :D],
        jnp.stack([own_main[1], own_main[0]], axis=1),
        own_small[:, 32:],
        own_small[:, :32],
        vec_main[:TAPS],
        vec_main[TAPS],
        vec_state[:TAPS],
        vec_state[TAPS],
        vec_head[0],
        vec_head[1],
        vec_head[2],
        vec_main[5],
        own_main[2],
    )


def solution(mesh):
    placed = (
        P(("dp", "tensor"), None),
        P("dp"),
        P(),
        P("dp", None, "tensor"),
        P("dp", "tensor"),
        P("dp", "tensor"),
        P(None, "tensor"),
        P("tensor"),
        P(None, "tensor"),
        P("tensor"),
        P("tensor"),
        P("tensor"),
        P("tensor"),
        P("tensor"),
        P("dp", "tensor"),
        P(("dp", "tensor"), None),
    )
    return jax.shard_map(
        per_device,
        mesh=mesh,
        in_specs=placed,
        out_specs=(
            P(("dp", "tensor"), None),
            P(("dp", "tensor"), None),
            P(),
            P("dp", None, "tensor"),
            P("dp", "tensor"),
            P("dp", "tensor"),
            P(None, "tensor"),
            P("tensor"),
            P(None, "tensor"),
            P("tensor"),
            P("tensor"),
            P("tensor"),
            P("tensor"),
            P("tensor"),
            P("dp", "tensor"),
        ),
        check_vma=False,
    )
```

time: 586 us -> 379 us (0.65)
  local copies, waits for them, and re-layouts: 140 us -> 24.3 us
  matrix products: 104 us -> 0 us
  Pallas kernels: 250 us -> 341 us
  other arithmetic: 81.2 us -> 5.49 us
    dot_general x26 -> x0, matrix products: 104 us -> none  [the longest x18 70.5 us: dot(): lax.dot_general(a, b, ((dims[:1], dims[1:]), ((), ())), preferred_element...]
    pallas_call x2 -> x3, Pallas kernels: 81.8 us -> 173 us  [the longest x1 117 us: mid(): pl.pallas_call(mid_kernel, name='scan_and_gate', out_shape=[jax.ShapeDtyp...]
    reshape x30 -> x0, local copies, waits for them, and re-layouts: 43.1 us -> none  [the longest x2 12.2 us: per_device(): grad_small.reshape(16, 3, SMALL_ROWS, 8, 38).transpose(0, 2, 3, 1, 4)]
    slice x23 -> x5, local copies, waits for them, and re-layouts: 31.8 us -> 5.38 us  [the longest x1 1.45 us: per_device(): vec_main[5]]
    another operation x8 -> x0, other arithmetic: 24.7 us -> none  [the longest x1 19.3 us: per_device(): main_grads = jnp.stack(grad_main + [grad_out]).reshape(3, 2, 4, 2, ROWS, DI)]
    reduce_sum x10 -> x0, other arithmetic: 21.5 us -> none  [the longest x2 5.71 us: conv_backward(): jnp.sum(masked[:BLOCK] * ext[HALO - offset:-offset], axis=0)]
    mul x11 -> x2, other arithmetic: 16.7 us -> 1.72 us  [the longest x1 0.99 us: per_device(): grad_x[:8] * silu_slope(x_pre[:8])]
    transpose x2 -> x0, local copies, waits for them, and re-layouts: 11.2 us -> none  [the longest x1 8.18 us: per_device(): grad_small.reshape(16, 3, SMALL_ROWS, 8, 38).transpose(0, 2, 3, 1, 4)]
  transfers between devices with their start and end apart: 1 -> 1, of which waited for: 0 -> 1; matrix products, arithmetic and copies ran while one was open for 12% -> 0% of each run, Pallas kernels for 0% -> 0%
where the time goes in v2:
time: 379 us; the launch traced here: 378 us
  Pallas kernels  341 us (90%)
  local copies, waits for them, and re-layouts  24.3 us (6%)
  other arithmetic  5.49 us (1%)
  waiting for transfers between devices  5.29 us (1%)
    pallas_call x1, Pallas kernels, mid(): pl.pallas_call(mid_kernel, name='scan_and_gate', out_shape=[jax.ShapeDtyp...  117 us
    pallas_call x1, Pallas kernels, scatter_grads(): pl.pallas_call(scatter_kernel, name='scatter_grads', out_shape=[jax.Shape...  88 us
    pallas_call x1, Pallas kernels, gather_weights(): pl.pallas_call(gather_kernel, name='gather_weights', out_shape=[jax.Shape...  80.1 us
    pallas_call x1, Pallas kernels, tail(): pl.pallas_call(tail_kernel, name='project_back', out_shape=[jax.ShapeDtyp...  33.5 us
    pallas_call x1, Pallas kernels, front(): pl.pallas_call(front_kernel, name='front', out_shape=[jax.ShapeDtypeStruc...  21.9 us
  transfers between devices with their start and end apart: 1, of which 1 were waited for; matrix products, arithmetic and copies ran while one was open for 0% of the time, Pallas kernels for 0%

profile of v2, /device:TPU:0, one launch (start us, length us, event | category | flops | bytes accessed | tf_op | source)
XLA Modules:
  0.0 378.0 jit_solution(10986577624152791100)
XLA Ops:
  0.7 0.8 concatenate.18
  1.4 0.1 dynamic_slice.12
  1.5 0.8 broadcast_in_dim.36.doc_col
  2.3 0.6 slice.72
  2.9 1.2 fusion.3
  4.2 0.7 pad_maximum_fusion.3
  4.9 0.1 copy.50
  5.0 0.1 reshape.55
  5.1 0.6 pad_bitcast_fusion.refs_1_
  5.7 1.4 slice.71.refs_2_
  7.2 0.7 broadcast_in_dim.30
  7.9 0.1 broadcast_in_dim_reshape.3
  8.0 0.7 broadcast_in_dim.28
  8.6 0.7 broadcast_in_dim.29
  9.3 1.3 broadcast_in_dim.33.gain
  10.6 1.6 pad_maximum_fusion.1.refs_0_
  12.2 1.3 concatenate.16.refs_3_
  13.5 1.4 fusion.refs_4_
  15.0 80.1 %gather_weights.1 = (bf16[3,2,4,2,96,3072]{5,4,3,2,1,0:T(8,128)(2,1)}, bf16[1,2,4,2,32,1024]{5,4,3,2,1,0:T(8,128)(2,1)}, bf16[16,1536]{1,0:T(8,128)(2,1)}, f32[8,3072]{1,0:T(8,128)}, f32[8,1024]{1,0:T(8,128)}) custom-call(bf16[3,96,384]{2,1,0:T(8,128)(2,1)} %pad_maximum_fusion.1.refs_0_, bf16[1,32,128]{2,1,0:T(8,128)(2,1)} %pad_bitcast_fusion.refs_1_, ...), custom_call_target="tpu_custom_call" | custom-call | tf_op jit(solution)/shard_map/gather_weights/pallas_call | solution.py:218
  95.1 21.9 %front.1 = (bf16[256,1536]{1,0:T(8,128)(2,1)}, f32[272,3072]{1,0:T(8,128)}, f32[256,3072]{1,0:T(8,128)}, bf16[256,3072]{1,0:T(8,128)(2,1)}, f32[256,3072]{1,0:T(...) custom-call(bf16[256,1536]{1,0:T(8,128)(2,1)} %hidden.5, ...), custom_call_target="tpu_custom_call" | custom-call | tf_op jit(solution)/shard_map/front/pallas_call | solution.py:667
  117.0 117.3 %scan_and_gate.1 = (bf16[256,1536]{1,0:T(8,128)(2,1)}, bf16[1536,3072]{1,0:T(8,128)(2,1)}, bf16[256,3072]{1,0:T(8,128)(2,1)}, f32[256,3072]{1,0:T(8,128)}, f32[2...) custom-call(bf16[256,3072]{1,0:T(8,128)(2,1)} %get-tuple-element.52.x_act, ...), custom_call_target="tpu_custom_call" | custom-call | tf_op jit(solution)/shard_map/scan_and_gate/pallas_call | solution.py:977
  234.4 1.0 multiply_multiply_fusion
  235.3 0.7 multiply_multiply_fusion.1
  236.1 1.3 collective-permute-start
  237.4 5.3 %collective-permute-done.after = f32[8,3328]{1,0:T(8,128)S(1)} collective-permute-done((f32[8,3328]{1,0:T(8,128)S(1)}, f32[8,3328]{1,0:T(8,128)S(1)}, u32[]{:S(2)}, u32[]{:S(2)}) %collective-permute-start) | collective-permute-done | bytes 106528 | tf_op jit(solution)/shard_map/ppermute | solution.py:1148
  242.7 0.0 copy-start.1
  242.7 0.6 copy-done.1
  243.3 33.5 %project_back.1 = (bf16[2,1536,3072]{2,1,0:T(8,128)(2,1)}, bf16[512,1024]{1,0:T(8,128)(2,1)}, f32[256,1536]{1,0:T(8,128)}, f32[8,3456]{1,0:T(8,128)}) custom-call(bf16[256,1536]{1,0:T(8,128)(2,1)} %get-tuple-element.59.normed, f32[272,3072]{1,0:T(8,128)} %get-tuple-element.60.x_ext, f32[256,3072]{1,0:T(8,128)} %get-tuple-element.61.x_pre, ...), custom_call_target="tpu_custom_call" | custom-call | tf_op jit(solution)/shard_map/project_back/pallas_call | solution.py:1086
  276.8 0.0 copy-start
  276.9 88.0 %scatter_grads.1 = (f32[3,96,384]{2,1,0:T(8,128)}, f32[1,32,128]{2,1,0:T(8,128)}, f32[8,3456]{1,0:T(8,128)}) custom-call(bf16[2,2,4,2,96,3072]{5,4,3,2,1,0:T(8,128)(2,1)} %bitcast.41, bf16[1,2,4,2,96,3072]{5,4,3,2,1,0:T(8,128)(2,1)} %bitcast.42, bf16[1,2,4,2,32,1024]{5,4,3,2,1,0:T(8,128)(2,1)} %bitcast.43, f32[8,3456]{1,0:T(8,128)} %get-tuple-element.75.refs_3_), custom_call_target="tpu_custom_call" | custom-call | tf_op jit(solution)/shard_map/scatter_grads/pallas_call | solution.py:477
  364.9 0.8 constant_dynamic-slice_fusion.2
  365.6 0.6 slice.85
  366.2 0.5 slice_bitcast_fusion.6
  366.7 1.4 slice_reduce_fusion
  368.2 1.7 slice_bitcast_fusion
  369.9 0.9 copy.56
  370.9 0.8 reshape_squeeze.3
  371.7 0.1 slice.92
  371.8 0.7 copy.57
  372.4 0.7 copy.58
  373.1 1.3 constant_dynamic-slice_fusion.1
  374.4 0.7 constant_dynamic-slice_fusion
  375.2 0.5 slice_bitcast_fusion.3
  375.7 1.5 dynamic-slice_reduce_fusion
  377.1 0.0 copy-done
  377.1 0.9 copy.64
  (8 shorter events, 0.1 us)
Async XLA Ops:
  236.1 6.6 %collective-permute-start = (f32[8,3328]{1,0:T(8,128)S(1)}, f32[8,3328]{1,0:T(8,128)S(1)}, u32[]{:S(2)}, u32[]{:S(2)}) collective-permute-start(f32[8,3328]{1,0:T(8,128)S(1)} %pad_maximum_fusion.2), channel_id=1, source_target_pairs={{1,0},{2,1},{3,2},{4,3},{5,4},{6,5},{7,6},{9,8},{10,9},{11,10},{12... | collective-permute-start | bytes 319496 | tf_op jit(solution)/shard_map/ppermute | solution.py:1148
  242.7 0.6 copy-start.1
  276.8 100.3 %copy-start = (bf16[256,1536]{1,0:T(8,128)(2,1)S(1)}, bf16[256,1536]{1,0:T(8,128)(2,1)}, u32[]{:S(2)}) copy-start(bf16[256,1536]{1,0:T(8,128)(2,1)} %get-tuple-element.151) | copy-start | bytes 2359300

commit v3 on v2

v3 whole, which is shorter than its diff:
```python
import functools

import jax
import jax.numpy as jnp
from jax import lax
from jax.experimental import pallas as pl
from jax.experimental.pallas import tpu as pltpu
from jax.sharding import PartitionSpec as P

BLOCK = 256
epsilon = 1e-05

MESH = pl.DeviceIdType.MESH
AXES = (0, 1, 2)
SIDE = 4


def coordinates():
    dp = lax.axis_index("dp")
    t = lax.axis_index("tensor")
    z = lax.div(t, 4) * 2 + lax.div(dp, 8)
    return (lax.rem(t, 4), lax.rem(lax.div(dp, 2), 4), z), lax.rem(dp, 2)


def device(at, core):
    x, y, z = at
    return (lax.rem(z, 2) * 8 + y * 2 + core, lax.div(z, 2) * 4 + x)


def moved(at, axis, by):
    return tuple(lax.rem(v + by + SIDE, SIDE) if i == axis else v for i, v in enumerate(at))


def pieces(at, whole, width):
    x, y, z = at
    lo = pl.ds(0, 2) if 2 in whole else pl.ds(lax.rem(z, 2), 1)
    row = pl.ds(0, 4) if 1 in whole else pl.ds(y, 1)
    hi = lax.div(z, 2)
    if 0 in whole and 2 in whole:
        cols = [pl.ds(0, 8 * width)]
    elif 0 in whole:
        cols = [pl.ds(pl.multiple_of(hi * 4 * width, 128), 4 * width)]
    elif 2 in whole:
        cols = [
            pl.ds(pl.multiple_of(x * width, 128), width),
            pl.ds(pl.multiple_of((4 + x) * width, 128), width),
        ]
    else:
        cols = [pl.ds(pl.multiple_of((hi * 4 + x) * width, 128), width)]
    return [(lo, row, c) for c in cols]


def greet(at, core, group):
    barrier = pltpu.get_barrier_semaphore()
    others = [device(moved(at, axis, by), core) for axis in AXES for by in (1, -1)]
    others.append(device(at, 1 - core))
    others += group
    for other in others:
        pl.semaphore_signal(barrier, inc=1, device_id=other, device_id_type=MESH)
    pl.semaphore_wait(barrier, len(others))


def tensor_peer(by):
    return (lax.axis_index("dp"), lax.rem(lax.axis_index("tensor") + by, 8))


ROWS, WIDTH, SMALL_ROWS, SMALL_WIDTH = 96, 384, 32, 128
UNITS = [(0, q * 32, q) for q in range(3)] + [(1, 0, 0)]
WIDTHS = [WIDTH, SMALL_WIDTH]
STACK = [3, 1]


def axes_of(u):
    return [(UNITS[u][2] + j) % 3 for j in range(3)]


def region(ref, u, core, mats, where, whole, half=None):
    which, first, rows = UNITS[u][0], UNITS[u][1], 32
    if half is not None:
        first, rows = first + half * 16, 16
    return [
        ref.at[mats, lo, row, core, pl.ds(first, rows), cols]
        for lo, row, cols in pieces(where, whole, WIDTHS[which])
    ]


def sized(ref, u, mats, blocks, halves=2):
    width = WIDTHS[UNITS[u][0]]
    cols = min(blocks, 8)
    rest = blocks // cols
    return ref.at[mats, pl.ds(0, max(rest // 4, 1)), pl.ds(0, min(rest, 4)), 0, pl.ds(0, 16 * halves), pl.ds(0, cols * width)]


def gather_kernel(*refs):
    shards, small, tail, params = refs[0], refs[1], refs[2], refs[3:5]
    full, halo, params_all = refs[5:7], refs[7], refs[8:10]
    own_sem, halo_sem, param_send, param_recv, send, recv, core_send, core_recv = refs[10:]
    at, core = coordinates()
    t = lax.axis_index("tensor")
    own = []
    for w, source in enumerate((shards, small)):
        for lo, row, cols in pieces(at, (), WIDTHS[w]):
            own.append(
                pltpu.make_async_copy(source, full[w].at[:, lo.start, row.start, core, :, cols], own_sem.at[w])
            )
    def columns(i, of):
        width = params[i].shape[-1]
        return params_all[i].at[:, pl.ds(pl.multiple_of(of * width, 128), width)]

    for i in range(2):
        own.append(pltpu.make_async_copy(params[i], columns(i, t), own_sem.at[2 + i]))
    for c in own:
        c.start()
    greet(at, core, [tensor_peer(by) for by in range(1, 8)])
    last = []

    def go(copy, wait=True):
        copy.start()
        if wait:
            last.append(copy)

    def tail_copy():
        return pltpu.make_async_remote_copy(
            src_ref=tail, dst_ref=halo, send_sem=halo_sem.at[0], recv_sem=halo_sem.at[1],
            device_id=tensor_peer(1), device_id_type=MESH,
        )

    def param_copy(by, i, of):
        return pltpu.make_async_remote_copy(
            src_ref=params[i], dst_ref=columns(i, of), send_sem=param_send.at[i, by - 1],
            recv_sem=param_recv.at[i, by - 1], device_id=tensor_peer(by), device_id_type=MESH,
        )

    go(tail_copy())
    for by in range(1, 8):
        for i in range(2):
            go(param_copy(by, i, t))
    for c in own:
        c.wait()

    def slot(u, phase, m):
        return (phase if phase < 2 else 2 + m), [u]

    def mats_of(u, phase, m):
        return pl.ds(0, STACK[UNITS[u][0]]) if phase < 2 else pl.ds(m, 1)

    def sends(u, phase, m, step):
        axes = axes_of(u)
        whole, axis = axes[:phase], axes[phase]
        index = phase if phase < 2 else 2 + m
        ref = full[UNITS[u][0]]
        for kind, by in ((0, 1), (1, -1)):
            where = at if step == 0 else moved(at, axis, -by)
            for part in region(ref, u, core, mats_of(u, phase, m), where, whole, kind if step else None):
                pltpu.make_async_remote_copy(
                    src_ref=part, dst_ref=part, send_sem=send.at[u, index, step],
                    recv_sem=recv.at[u, index, step],
                    device_id=device(moved(at, axis, by), core), device_id_type=MESH,
                ).start()

    def await_step(u, phase, m, step, sem):
        index = phase if phase < 2 else 2 + m
        part = sized(full[UNITS[u][0]], u, mats_of(u, phase, m), 2 * 4**phase // (1 + step))
        pltpu.make_async_copy(part, part, sem.at[u, index, step]).wait()

    def to_partner(u, m, where, whole):
        for part in region(full[UNITS[u][0]], u, core, mats_of(u, 2, m), where, whole):
            pltpu.make_async_remote_copy(
                src_ref=part, dst_ref=part, send_sem=core_send.at[u, m],
                recv_sem=core_recv.at[u, m], device_id=device(at, 1 - core), device_id_type=MESH,
            ).start()

    everything = range(len(UNITS))
    late = [(u, m) for m in range(3) for u in everything if m < STACK[UNITS[u][0]]]
    for phase in (0, 1):
        for u in everything:
            sends(u, phase, 0, 0)
        for u in everything:
            await_step(u, phase, 0, 0, recv)
            sends(u, phase, 0, 1)
        for u in everything:
            await_step(u, phase, 0, 1, recv)
    for u, m in late:
        sends(u, 2, m, 0)
    for u, m in late:
        to_partner(u, m, at, axes_of(u)[:2])
    for u, m in late:
        await_step(u, 2, m, 0, recv)
        sends(u, 2, m, 1)
        whole, axis = axes_of(u)[:2], axes_of(u)[2]
        for by in (-1, 1):
            to_partner(u, m, moved(at, axis, by), whole)
    for u, m in late:
        await_step(u, 2, m, 1, recv)
        whole, axis = axes_of(u)[:2], axes_of(u)[2]
        to_partner(u, m, moved(at, axis, 2), whole)
    for u, m in late:
        part = sized(full[UNITS[u][0]], u, mats_of(u, 2, m), 64)
        pltpu.make_async_copy(part, part, core_recv.at[u, m]).wait()
        pltpu.make_async_copy(part, part, core_send.at[u, m]).wait()
    tail_copy().wait_recv()
    for by in range(1, 8):
        for i in range(2):
            param_copy(by, i, lax.rem(t + 8 - by, 8)).wait_recv()
    for u in everything:
        for phase in (0, 1):
            for step in (0, 1):
                await_step(u, phase, 0, step, send)
    for u, m in late:
        for step in (0, 1):
            await_step(u, 2, m, step, send)
    for c in last:
        c.wait_send()


def gather_weights(shards, small, tail, params):
    units = len(UNITS)
    return pl.pallas_call(
        gather_kernel,
        name="gather_weights",
        out_shape=[
            jax.ShapeDtypeStruct((3, 2, 4, 2, ROWS, 8 * WIDTH), jnp.bfloat16),
            jax.ShapeDtypeStruct((1, 2, 4, 2, SMALL_ROWS, 8 * SMALL_WIDTH), jnp.bfloat16),
            jax.ShapeDtypeStruct(tail.shape, tail.dtype),
        ]
        + [jax.ShapeDtypeStruct((8, 8 * p.shape[1]), p.dtype) for p in params],
        in_specs=[pl.BlockSpec(memory_space=pl.ANY)] * 5,
        out_specs=[pl.BlockSpec(memory_space=pl.ANY)] * 5,
        scratch_shapes=[
            pltpu.SemaphoreType.DMA((4,)),
            pltpu.SemaphoreType.DMA((2,)),
            pltpu.SemaphoreType.DMA((2, 7)),
            pltpu.SemaphoreType.DMA((2, 7)),
            pltpu.SemaphoreType.DMA((units, 5, 2)),
            pltpu.SemaphoreType.DMA((units, 5, 2)),
            pltpu.SemaphoreType.DMA((units, 3)),
            pltpu.SemaphoreType.DMA((units, 3)),
        ],
        compiler_params=pltpu.CompilerParams(collective_id=0, has_side_effects=True),
    )(shards, small, tail, *params)


D, DI, HEADS, HEAD_DIM, STATE, TAPS, HALO = 1536, 3072, 48, 64, 128, 4, 16
BF16, F32 = jnp.bfloat16, jnp.float32
TILE, LANES, SMALL = 512, 128, 384
TILES = DI // TILE
LOG2E = 1.4426950408889634
EXT = HALO + BLOCK
VMEM = pltpu.VMEM


def dot(a, b, dims=(1, 0), precision=None):
    return lax.dot_general(
        a, b, ((dims[:1], dims[1:]), ((), ())), precision=precision, preferred_element_type=F32
    )


def iota(shape, dim):
    return lax.broadcasted_iota(jnp.int32, shape, dim)


def sigmoid(v):
    return 1.0 / (1.0 + jnp.exp(-v))


def silu(v):
    return v * sigmoid(v)


def silu_slope(v):
    s = sigmoid(v)
    return s * (1.0 + v * (1.0 - s))


def softplus(v):
    return jnp.maximum(v, 0.0) + jnp.log1p(jnp.exp(-jnp.abs(v)))


def split(v):
    high = v.astype(BF16)
    return high, (v - high.astype(F32)).astype(BF16)


def head_map(j):
    return (iota((LANES, TILE), 0) == j * (TILE // HEAD_DIM) + iota((LANES, TILE), 1) // HEAD_DIM).astype(BF16)


def widen(v, j):
    high, low = split(v)
    return dot(high, head_map(j)) + dot(low, head_map(j))


def by_head(v, j):
    high, low = split(v)
    return dot(high, head_map(j), (1, 1)) + dot(low, head_map(j), (1, 1))


def small_map(r):
    row, col = iota((8 * LANES, SMALL), 0), iota((8 * LANES, SMALL), 1)
    t, lane = row // LANES, row % LANES - 38 * r
    state = (lane >= 0) & (lane < 32) & (col == t * 32 + lane)
    step = (lane >= 32) & (lane < 38) & (col == 256 + t * 6 + lane - 32)
    return (state | step).astype(BF16)


def tile_of(j):
    return pl.ds(pl.multiple_of(j * TILE, TILE), TILE)


def conv_links(doc_col, offset, rows):
    return (doc_col[HALO : HALO + rows] == doc_col[HALO - offset : HALO - offset + rows]).astype(F32)


def conv(ext, taps, bias, links):
    total = bias + taps[TAPS - 1 : TAPS] * ext[HALO:]
    for offset in range(1, TAPS):
        total = total + taps[TAPS - 1 - offset : TAPS - offset] * ext[HALO - offset : EXT - offset] * links[offset]
    return total


def small_params(phead):
    return dot(phead, small_map(0).astype(F32), precision=lax.Precision.HIGHEST)


def decay_terms(step, cum, doc_col, doc_prev):
    block = doc_col[HALO:EXT]
    end = cum[BLOCK - 1 : BLOCK]
    tail = jnp.exp(end - cum) * (block == block[BLOCK - 1 : BLOCK]).astype(F32)
    enter = jnp.exp(cum) * (block == doc_prev).astype(F32)
    keep = jnp.exp(end) * (block[BLOCK - 1 : BLOCK] == doc_prev).astype(F32)
    return enter, tail, tail * step, keep


def pack_params(conv_main, conv_main_bias, conv_state, conv_state_bias, step_bias, decay_log, skip_gain, gate_gain):
    main = jnp.concatenate(
        [conv_main, conv_main_bias[None], gate_gain[None], jnp.repeat(skip_gain, HEAD_DIM)[None],
         jnp.zeros((1, WIDTH), F32)]
    )
    state = jnp.pad(jnp.concatenate([conv_state, conv_state_bias[None]]), ((0, 3), (0, 96)))
    heads = jnp.pad(jnp.stack([step_bias, decay_log, skip_gain]), ((5, 0), (32, 90)))
    return main, state + heads


PAIR = 2 * HEAD_DIM
PAIRS = DI // PAIR
HALF = BLOCK // 2
CHUNK = 256
CHUNKS = DI // CHUNK
FORWARD_LAG, BACKWARD_LAG = 4, 2


def pair_of(p):
    return pl.ds(pl.multiple_of(p * PAIR, PAIR), PAIR)


def chunk_of(c):
    return pl.ds(pl.multiple_of(c * CHUNK, CHUNK), CHUNK)


def only(value, first):
    lane = iota(value.shape, 1)
    return jnp.where((lane < HEAD_DIM) == first, value, jnp.zeros_like(value))


def head_column(ref, h):
    return pltpu.roll(ref[...], lax.rem(LANES - h, LANES), axis=1)[:, :1]


def mid_kernel(
    hidden, halo, gain, packed, pmain, phead, doc_col, doc_row, cot, full,
    mixed, normed_t, raw, state_pre, grad_bc, grad_step_in, w_small, acc, grad_x, vec_gate, vec_heads,
    x_ext, x_pre, grad_out, grad_gate,
    normed, w_in, ext_out, pre_out, staged, x_act, bc, scores, gate_in, work, y, gate_out, dy, gate_grad, update,
    grad_add, state, state_low, grad_state, keep_row, f_out, f_in, b_out, b_in, cot_t, mixed_acc,
    barred, cum2, cum_t, step_t, step_in, enter_ref, weight_ref, rows_acc, q_t, gs, acc_c, acc_heads, row_acc,
    w_sem, put_sem, x_sem, f_send, f_recv, b_send, b_recv,
):
    t = lax.axis_index("tensor")

    def load(m, j, slot):
        return pltpu.make_async_copy(full.at[m, :, tile_of(j)], w_in.at[slot], w_sem.at[slot])

    load(0, 0, 0).start()
    barrier = pltpu.get_barrier_semaphore()
    for other in (tensor_peer(1), tensor_peer(7)):
        pl.semaphore_signal(barrier, inc=1, device_id=other, device_id_type=MESH)
    pl.semaphore_wait(barrier, 2)

    for rows, part in ((pl.ds(0, HALO), halo), (pl.ds(HALO, BLOCK), hidden)):
        value = part[...].astype(F32)
        inv = lax.rsqrt(jnp.mean(value * value, axis=1, keepdims=True) + epsilon)
        normed[rows] = (value * inv * gain[...]).astype(BF16)
    normed_t[...] = normed[pl.ds(HALO, BLOCK)].T
    cot_t[...] = cot[...].T
    for r in range(3):
        rows = dot(packed[...], small_map(r)).astype(BF16)
        for d in range(16):
            w_small[pl.ds(d * 96 + r * 32, 32)] = rows[d * 32 : d * 32 + 32]
    raw[...] = dot(normed[...], w_small[...])
    params = small_params(phead[...])
    docs = doc_col[...]
    links = [None] + [conv_links(docs, o, BLOCK) for o in range(1, TAPS)]
    pre = conv(raw[:, :256], params[:TAPS, :256], params[TAPS : TAPS + 1, :256], links)
    state_pre[...] = pre
    act = silu(pre).astype(BF16)
    bc[...] = act
    scores[...] = dot(act[:, STATE:], act[:, :STATE], (1, 1))
    step_in[...] = raw[HALO:, 256:] + params[5:6, 256:]
    rate = -jnp.exp(params[6:7, 256:])
    step = softplus(step_in[...])
    lower = (iota((BLOCK, BLOCK), 0) >= iota((BLOCK, BLOCK), 1)).astype(F32)
    cum = dot(lower, step * rate, precision=lax.Precision.HIGHEST)
    enter, tail, weight, keep = decay_terms(step, cum, docs, docs[HALO - 1 : HALO])
    enter_ref[...] = enter
    weight_ref[...] = weight
    cum2[...] = cum * LOG2E
    for ref, turned in ((cum_t, (cum * LOG2E).T), (step_t, step.T)):
        for h in range(HEADS):
            ref[h] = turned[h : h + 1]
    linked = (docs[HALO:EXT] == doc_row[...]) & (iota((BLOCK, BLOCK), 0) >= iota((BLOCK, BLOCK), 1))
    barred[...] = jnp.where(linked, 0.0, -1e30)
    keep8 = jnp.broadcast_to(keep, (8, LANES))

    def chain(forward, c, add, into, outgoing, incoming, send, recv):
        cols = chunk_of(c)
        by = 1 if forward else 7
        is_first = t == (0 if forward else 7)
        is_last = t == (7 if forward else 0)

        def copy():
            return pltpu.make_async_remote_copy(
                src_ref=outgoing.at[:, cols], dst_ref=incoming.at[:, cols], send_sem=send.at[c],
                recv_sem=recv.at[c], device_id=tensor_peer(by), device_id_type=MESH,
            )

        @pl.when(is_first)
        def _():
            into[:, cols] = jnp.zeros((STATE, CHUNK), F32)

        @pl.when(jnp.logical_not(is_first))
        def _():
            copy().wait_recv()
            into[:, cols] = incoming[:, cols].astype(F32)

        @pl.when(jnp.logical_not(is_last))
        def _():
            outgoing[:, cols] = (keep_row[0:1, cols] * into[:, cols] + add[:, cols]).astype(BF16)
            copy().start()

    def forward_slot(s):
        c = s - FORWARD_LAG * t

        @pl.when((c >= 0) & (c < CHUNKS))
        def _():
            chain(True, c, update, state, f_out, f_in, f_send, f_recv)

    def backward_slot(s):
        c = s - BACKWARD_LAG * (7 - t)

        @pl.when((c >= 0) & (c < CHUNKS))
        def _():
            chain(False, c, grad_add, grad_state, b_out, b_in, b_send, b_recv)

    def x_puts(j, slot):
        return [
            pltpu.make_async_copy(src.at[slot], dst.at[:, tile_of(j)], x_sem.at[i, slot])
            for i, (src, dst) in enumerate(((ext_out, x_ext), (pre_out, x_pre)))
        ]

    @pl.loop(0, TILES)
    def _(j):
        cols = tile_of(j)
        slot = lax.rem(j, 2)

        @pl.when(j + 1 < TILES)
        def _():
            load(0, j + 1, 1 - slot).start()

        @pl.when(j + 1 == TILES)
        def _():
            load(1, 0, 0).start()

        @pl.when(j >= 2)
        def _():
            for c in x_puts(j, slot):
                c.wait()

        load(0, j, slot).wait()
        ext = dot(normed[...], w_in[slot])
        ext_out[slot] = ext
        pre = conv(ext, pmain[0:TAPS, cols], pmain[TAPS : TAPS + 1, cols], links)
        pre_out[slot] = pre
        for c in x_puts(j, slot):
            c.start()
        act = silu(pre).astype(BF16)
        x_act[:, cols] = act
        heavy = (act.astype(F32) * widen(weight_ref[...], j)).astype(BF16)
        update[:, cols] = dot(bc[:, :STATE], heavy, (0, 0))
        keep_row[:, cols] = widen(keep8, j)
        forward_slot(2 * j)
        forward_slot(2 * j + 1)

    load(2, 0, 1).start()
    for slot in range(2):
        for c in x_puts(TILES - 2 + slot, slot):
            c.wait()

    halves = [(slice(0, HALF), slice(0, HALF)), (slice(HALF, BLOCK), slice(0, BLOCK))]

    def decay_of(h, column, rows, cols):
        return jnp.exp2(column[rows] - cum_t[h, :, cols] + barred[rows, cols])

    def intra_forward(p):
        cols = pair_of(p)
        x = x_act[:, cols]
        x2 = [only(x, True), only(x, False)]
        columns = [head_column(cum2, 2 * p + k) for k in (0, 1)]
        for rows, js in halves:
            mix = [
                (scores[rows, js] * (decay_of(2 * p + k, columns[k], rows, js) * step_t[2 * p + k, :, js])).astype(BF16)
                for k in (0, 1)
            ]
            y[rows, cols] = dot(jnp.concatenate(mix, 1), jnp.concatenate([v[js] for v in x2], 0))

    @pl.loop(0, PAIRS)
    def _(i):
        intra_forward(i)
        j = lax.div(i, 4)

        @pl.when(lax.rem(i, 4) == 0)
        def _():
            load(1, j, 0).wait()
            gate_in[:, tile_of(j)] = dot(normed[pl.ds(HALO, BLOCK)], w_in[0])

            @pl.when(j + 1 < TILES)
            def _():
                load(1, j + 1, 0).start()

        @pl.when(lax.rem(i, 4) == 2)
        def _():
            load(2, j, 1).wait()
            work[:, tile_of(j)] = dot(cot[...], w_in[1])

            @pl.when(j + 1 < TILES)
            def _():
                load(2, j + 1, 1).start()

        forward_slot(2 * TILES + i)

    @pl.loop(2 * TILES + PAIRS, jnp.maximum(2 * TILES + PAIRS, FORWARD_LAG * t + CHUNKS))
    def _(s):
        forward_slot(s)

    load(2, 0, 1).start()
    load(1, 0, 0).start()
    row_acc[...] = jnp.zeros_like(row_acc)

    @pl.loop(0, TILES)
    def _(j):
        cols = tile_of(j)
        low = state[:, cols].astype(BF16)
        state_low[:, cols] = low
        carried = dot(bc[:, STATE:], low)
        value = y[:, cols] + carried * widen(enter_ref[...], j) + pmain[6:7, cols] * x_act[:, cols].astype(F32)
        y[:, cols] = value
        gated = value * silu(gate_in[:, cols])
        row_acc[...] += jnp.broadcast_to(jnp.sum(gated * gated, axis=1, keepdims=True), (BLOCK, LANES))

    gate_inv = lax.rsqrt(row_acc[:, :1] / DI + epsilon)
    row_acc[...] = jnp.zeros_like(row_acc)

    @pl.loop(0, TILES)
    def _(j):
        cols = tile_of(j)
        gated = y[:, cols] * silu(gate_in[:, cols])
        hat = gated * gate_inv
        gate_gain = pmain[5:6, cols]
        gate_out[:, cols] = (hat * gate_gain).astype(BF16)
        grad = work[:, cols]
        vec_gate[:, cols] = jnp.broadcast_to(jnp.sum(grad * hat, axis=0, keepdims=True), (8, TILE))
        dn = grad * gate_gain
        work[:, cols] = dn
        row_acc[...] += jnp.broadcast_to(jnp.sum(dn * gated, axis=1, keepdims=True), (BLOCK, LANES))

    inner = row_acc[:, :1] / DI * gate_inv * gate_inv * gate_inv
    acc_c[...] = jnp.zeros_like(acc_c)
    acc_heads[...] = jnp.zeros_like(acc_heads)

    @pl.loop(0, TILES)
    def _(j):
        cols = tile_of(j)
        gate, value = gate_in[:, cols], y[:, cols]
        s = sigmoid(gate)
        act = gate * s
        grad_gated = gate_inv * work[:, cols] - value * act * inner
        grad = (grad_gated * act).astype(BF16)
        dy[:, cols] = grad
        gate_grad[:, cols] = (grad_gated * value * (s * (1.0 + gate * (1.0 - s)))).astype(BF16)
        grad = grad.astype(F32)
        carried_grad = (grad * widen(enter_ref[...], j)).astype(BF16)
        low = state_low[:, cols]
        grad_add[:, cols] = dot(bc[:, STATE:], carried_grad, (0, 0))
        acc_c[...] += dot(carried_grad, low, (1, 1))
        acc_heads[0] += by_head(grad * dot(bc[:, STATE:], low), j)

    rows_acc[...] = jnp.zeros_like(rows_acc)
    gs[...] = jnp.zeros_like(gs)
    acc[...] = jnp.zeros_like(acc)
    mixed_acc[...] = jnp.zeros_like(mixed_acc)

    def intra_backward(p):
        cols = pair_of(p)
        x, grad = x_act[:, cols], dy[:, cols]
        grad2 = [only(grad, True), only(grad, False)]
        columns = [head_column(cum2, 2 * p + k) for k in (0, 1)]
        lane = iota((HALF, LANES), 1)
        parts = []
        q_rows = [[], []]
        for rows, js in halves:
            mixes = []
            gs_sum = gs[rows, js]
            pulls = jnp.zeros((HALF, LANES), F32)
            for k in (0, 1):
                h = 2 * p + k
                decay = decay_of(h, columns[k], rows, js)
                decay_step = decay * step_t[h, :, js]
                mixes.append((scores[rows, js] * decay_step).astype(BF16))
                grad_mix = dot(grad2[k][rows], x[js], (1, 1))
                gs_sum = gs_sum + grad_mix * decay_step
                q = grad_mix * scores[rows, js] * decay
                q_rows[k].append(jnp.sum(q, axis=0, keepdims=True))
                pull = jnp.sum(q * step_t[h, :, js], axis=1, keepdims=True)
                pulls = jnp.where(lane == h, pull, pulls)
            gs[rows, js] = gs_sum
            rows_acc[rows] += pulls
            parts.append(dot(jnp.concatenate(mixes, 0), jnp.concatenate([v[rows] for v in grad2], 0), (0, 0)))
        grad_x[pl.ds(0, HALF), cols] = parts[0] + parts[1][:HALF]
        grad_x[pl.ds(HALF, HALF), cols] = parts[1][HALF:]
        for k in (0, 1):
            first, second = q_rows[k]
            q_t[2 * p + k, :, 0:HALF] = first + second[:, :HALF]
            q_t[2 * p + k, :, HALF:BLOCK] = second[:, HALF:]

    def put(ref, j, slot):
        return [
            pltpu.make_async_copy(
                staged.at[slot, pl.ds(i * ROWS, ROWS)], ref.at[0, lo, y_, c, :, tile_of(j)], put_sem.at[slot, i]
            )
            for i, (lo, y_, c) in enumerate((lo, y_, c) for lo in range(2) for y_ in range(4) for c in range(2))
        ]

    def put_tile(ref, j, slot, lhs, grad):
        @pl.when(j >= 1)
        def _():
            for c in put(ref, j, slot):
                c.wait()

        staged[slot] = dot(lhs[...], grad).astype(BF16)
        for c in put(ref, j, slot):
            c.start()

    @pl.loop(0, PAIRS)
    def _(i):
        backward_slot(i)
        intra_backward(i)
        j = lax.div(i, 4)
        cols = tile_of(j)

        @pl.when(lax.rem(i, 4) == 0)
        def _():
            put_tile(grad_out, j, 0, cot_t, gate_out[:, cols])

        @pl.when(lax.rem(i, 4) == 1)
        def _():
            put_tile(grad_gate, j, 1, normed_t, gate_grad[:, cols])

        @pl.when(lax.rem(i, 4) == 2)
        def _():
            load(2, j, 1).wait()
            mixed_acc[...] += dot(gate_out[:, cols], w_in[1], (1, 1))

            @pl.when(j + 1 < TILES)
            def _():
                load(2, j + 1, 1).start()

        @pl.when(lax.rem(i, 4) == 3)
        def _():
            load(1, j, 0).wait()
            acc[...] += dot(gate_grad[:, cols], w_in[0], (1, 1))

            @pl.when(j + 1 < TILES)
            def _():
                load(1, j + 1, 0).start()

    @pl.loop(PAIRS, jnp.maximum(PAIRS, BACKWARD_LAG * (7 - t) + CHUNKS))
    def _(s):
        backward_slot(s)

    gs_low = gs[...].astype(BF16)
    grad_bc[:, STATE:] = acc_c[...] + dot(gs_low, bc[:, :STATE])
    acc_c[...] = dot(gs_low, bc[:, STATE:], (0, 0))

    @pl.loop(0, TILES)
    def _(j):
        cols = tile_of(j)
        wide = widen(weight_ref[...], j)
        grad_update = grad_state[:, cols].astype(BF16)
        spread_grad = dot(bc[:, :STATE], grad_update)
        x, grad = x_act[:, cols].astype(F32), dy[:, cols].astype(F32)
        grad_x[:, cols] += wide * spread_grad + pmain[6:7, cols] * grad
        acc_heads[1] += by_head(x * spread_grad, j)
        acc_c[...] += dot((x * wide).astype(BF16), grad_update, (1, 1))
        kept = jnp.sum(grad_state[:, cols] * state[:, cols], axis=0, keepdims=True)
        skip = jnp.sum(x * grad, axis=0, keepdims=True)
        row = iota((8, TILE), 0)
        both = jnp.where(row == 0, kept, jnp.where(row == 1, skip, 0.0))
        acc_heads[2, 0:8] += by_head(both, j)

    grad_bc[:, :STATE] = acc_c[...]
    grad_weight = acc_heads[1]
    none = jnp.zeros((LANES - HEADS, BLOCK), F32)
    step = jnp.concatenate([step_t[h] for h in range(HEADS)] + [none], 0).T
    q = jnp.concatenate([q_t[h] for h in range(HEADS)] + [none], 0).T
    weight_pull = grad_weight * weight_ref[...]
    grad_end = jnp.sum(weight_pull, axis=0, keepdims=True) + acc_heads[2, 0:1] * keep
    grad_cum = rows_acc[...] - step * q + enter_ref[...] * acc_heads[0] - weight_pull
    grad_cum = grad_cum + jnp.where(iota((BLOCK, LANES), 0) == BLOCK - 1, grad_end, 0.0)
    upper = (iota((BLOCK, BLOCK), 0) <= iota((BLOCK, BLOCK), 1)).astype(F32)
    grad_log = dot(upper, grad_cum, precision=lax.Precision.HIGHEST)
    grad_step = q + grad_weight * tail + rate * grad_log
    grad_in = grad_step * sigmoid(step_in[...])
    grad_step_in[...] = grad_in
    row = iota((8, LANES), 0)
    heads = jnp.where(row == 5, jnp.sum(grad_in, axis=0, keepdims=True), 0.0)
    heads = jnp.where(row == 6, rate * jnp.sum(grad_log * step, axis=0, keepdims=True), heads)
    vec_heads[...] = jnp.where(row == 7, acc_heads[2, 1:2], heads)
    mixed[...] = (hidden[...].astype(F32) + mixed_acc[...]).astype(BF16)

    for slot, ref in ((0, grad_out), (1, grad_gate)):
        for c in put(ref, TILES - 1, slot):
            c.wait()
    for by, ends, outgoing, incoming, send, recv in (
        (1, 7, f_out, f_in, f_send, f_recv),
        (7, 0, b_out, b_in, b_send, b_recv),
    ):

        @pl.when(t != ends)
        def _(by=by, outgoing=outgoing, incoming=incoming, send=send, recv=recv):
            @pl.loop(0, CHUNKS)
            def _(c):
                pltpu.make_async_remote_copy(
                    src_ref=outgoing.at[:, chunk_of(c)], dst_ref=incoming.at[:, chunk_of(c)], send_sem=send.at[c],
                    recv_sem=recv.at[c], device_id=tensor_peer(by), device_id_type=MESH,
                ).wait_send()


def mid(*args):
    vmem = pl.BlockSpec(memory_space=VMEM)
    anywhere = pl.BlockSpec(memory_space=pl.ANY)
    wide, heads, square = (BLOCK, DI), (BLOCK, LANES), (BLOCK, BLOCK)
    turned, own_state = (HEADS, 1, BLOCK), (STATE, DI)
    blocks = (1, 2, 4, 2, ROWS, DI)
    shapes = [
        ((BLOCK, D), BF16), ((D, BLOCK), BF16), ((EXT, SMALL), F32), (square, F32), (square, F32), (heads, F32),
        ((D, SMALL), BF16), ((BLOCK, D), F32), (wide, F32), ((8, DI), F32), ((8, LANES), F32),
        ((EXT, DI), F32), (wide, F32), (blocks, BF16), (blocks, BF16),
    ]
    scratch = [
        ((EXT, D), BF16), ((2, D, TILE), BF16), ((2, EXT, TILE), F32), ((2, BLOCK, TILE), F32), ((2, D, TILE), BF16),
        (wide, BF16), ((BLOCK, 2 * STATE), BF16), (square, F32), (wide, F32), (wide, F32), (wide, F32), (wide, BF16),
        (wide, BF16), (wide, BF16), (own_state, F32), (own_state, F32), (own_state, F32), (own_state, BF16),
        (own_state, F32), ((8, DI), F32), (own_state, BF16), (own_state, BF16), (own_state, BF16), (own_state, BF16),
        ((D, BLOCK), BF16), ((BLOCK, D), F32),
        (square, F32), (heads, F32), (turned, F32), (turned, F32), (heads, F32), (heads, F32), (heads, F32),
        (heads, F32), (turned, F32), (square, F32), (heads, F32), ((3,) + heads, F32), (heads, F32),
    ]
    return pl.pallas_call(
        mid_kernel,
        name="scan_and_gate",
        out_shape=[jax.ShapeDtypeStruct(*s) for s in shapes],
        in_specs=[vmem] * 9 + [anywhere],
        out_specs=[vmem] * 11 + [anywhere] * 4,
        scratch_shapes=[VMEM(*s) for s in scratch]
        + [pltpu.SemaphoreType.DMA((2,)), pltpu.SemaphoreType.DMA((2, 16)), pltpu.SemaphoreType.DMA((2, 2))]
        + [pltpu.SemaphoreType.DMA((CHUNKS,))] * 4,
        compiler_params=pltpu.CompilerParams(
            collective_id=1, has_side_effects=True, vmem_limit_bytes=60 * 2**20
        ),
    )(*args)


VEC = (8, 8 * WIDTH + 384)
VEC_STEPS = 7
MATS = (2, 1, 0)


def spread(whole):
    return (2 if 2 in whole else 1, 4 if 1 in whole else 1, (4 if 0 in whole else 1) * (2 if 2 in whole else 1))


def region_shape(u, phase, rows):
    lo, y, cols = spread(axes_of(u)[:phase])
    return (lo, y, rows, cols * WIDTHS[UNITS[u][0]])


def back_kernel(*refs):
    refs = list(refs)

    def take(n):
        got = refs[:n]
        del refs[:n]
        return got

    (normed_t, raw_ext, state_pre, grad_bc, grad_step_in, w_small, acc_in, pmain, phead, doc_col, hidden, cot, gain,
     vec_gate, vec_heads, x_ext, x_pre, grad_x, grad_gate, grad_out, full) = take(21)
    grad_main, grad_small, out_main, out_small, grad_hidden, vec_out = take(6)
    outs = (out_main, out_small)
    units = len(UNITS)
    other = take(2)
    half_buf = [take(3) for _ in range(units)]
    full_buf = [take(3) for _ in range(units)]
    own = take(units)
    (ext_in, pre_in, grad_in, first_grad, first_pre, first_out, after, w_in, staged, raw_x, acc, small_acc,
     small_out, vec_acc, vec_in) = take(15)
    (stream_sem, first_sem, halo_sem, w_sem, put_sem, small_sem, own_sem, vec_send, vec_recv, send, recv, core_send,
     core_recv) = take(13)
    at, core = coordinates()
    t = lax.axis_index("tensor")
    everything = range(units)

    def stream(j, slot):
        cols = tile_of(j)
        return [
            pltpu.make_async_copy(src.at[:, cols], dst.at[slot], stream_sem.at[i, slot])
            for i, (src, dst) in enumerate(((x_ext, ext_in), (x_pre, pre_in), (grad_x, grad_in)))
        ]

    firsts = [
        pltpu.make_async_copy(src.at[pl.ds(0, 8)], dst, first_sem.at[i])
        for i, (src, dst) in enumerate(((grad_x, first_grad), (x_pre, first_pre)))
    ]
    for c in firsts + stream(0, 0):
        c.start()
    greet(at, core, [device(moved(at, axis, 2), core) for axis in AXES] + [tensor_peer(1), tensor_peer(7)])

    def source_of(u, m):
        return grad_small if UNITS[u][0] else (grad_main, grad_gate, grad_out)[m]

    def units_of(m):
        return [u for u in everything if m == 0 or UNITS[u][0] == 0]

    def index_of(u, m):
        return 0 if UNITS[u][0] else m

    def part_of(ref, u, mats, where, whole, half=None):
        which, first, rows = UNITS[u][0], UNITS[u][1], 32
        if half is not None:
            first, rows = first + half * 16, 16
        return [ref.at[mats, lo, y, pl.ds(first, rows), cols] for lo, y, cols in pieces(where, whole, WIDTHS[which])]

    def place(u, by):
        return moved(at, axes_of(u)[2], by) if by else at

    groups = [[2], [1, -1], [0]]

    def to_partner(m):
        for g, group in enumerate(groups):
            for u in units_of(m):
                for by in group:
                    whole = axes_of(u)[:2]
                    for src, dst in zip(
                        region(source_of(u, m), u, 1 - core, pl.ds(0, 1), place(u, by), whole),
                        part_of(other[UNITS[u][0]], u, pl.ds(index_of(u, m), 1), place(u, by), whole),
                    ):
                        pltpu.make_async_remote_copy(
                            src_ref=src, dst_ref=dst, send_sem=core_send.at[u, m], recv_sem=core_recv.at[u, m, g],
                            device_id=device(at, 1 - core), device_id_type=MESH,
                        ).start()

    def await_partner(u, m, g):
        rows = 2 * len(groups[g])
        part = other[UNITS[u][0]].at[pl.ds(0, 1), pl.ds(0, 1), pl.ds(0, rows), pl.ds(0, 32)]
        pltpu.make_async_copy(part, part, core_recv.at[u, m, g]).wait()

    def own_loads(u, m, g):
        copies = []
        for slot, by in enumerate(groups[g]):
            parts = region(source_of(u, m), u, core, 0, place(u, by), axes_of(u)[:2])
            width = own[u].shape[-1] // len(parts)
            for i, src in enumerate(parts):
                copies.append(
                    pltpu.make_async_copy(src, own[u].at[slot, :, :, :, pl.ds(i * width, width)], own_sem.at[u, slot, i])
                )
        return copies

    def prefetch(m, g):
        for u in units_of(m):
            for c in own_loads(u, m, g):
                c.start()

    def add(u, phase, mats, where, half, terms, result=None):
        which, first, rows = UNITS[u][0], UNITS[u][1], 32
        if half is not None:
            first, rows = first + half * 16, 16
        whole = axes_of(u)[:phase]
        n_lo, n_y, _ = spread(whole)
        for i, (lo, y, cols) in enumerate(pieces(where, whole, WIDTHS[which])):

            @pl.loop(0, len(mats) * n_lo * n_y)
            def _(k, i=i, lo=lo, y=y, cols=cols):
                mat = mats[0] if len(mats) == 1 else lax.div(k, n_lo * n_y)
                a, b = lax.rem(lax.div(k, n_y), n_lo), lax.rem(k, n_y)
                here = (mat, lo.start + a, y.start + b, pl.ds(first, rows), cols)
                total = other[which][here].astype(F32)
                for term in terms:
                    total = total + term(mat, i, a, b).astype(F32)
                if result is None:
                    other[which][here] = total.astype(BF16)
                else:
                    result[mat, pl.ds(first, rows), :] = total

    def width_of(u, phase, ref):
        whole = axes_of(u)[:phase]
        return ref.shape[-1] // (2 if 2 in whole and 0 not in whole else 1)

    def from_own(u, slot, half=None):
        width = width_of(u, 2, own[u])
        rows = pl.ds(0, 32) if half is None else pl.ds(half * 16, 16)
        return lambda mat, i, a, b: own[u][slot, a, b, rows, pl.ds(i * width, width)]

    def from_buf(ref, side, u, phase):
        width = width_of(u, phase, ref)
        return lambda mat, i, a, b: ref[side, mat, a, b, :, pl.ds(i * width, width)]

    def mats_of(u, m):
        return pl.ds(0, STACK[UNITS[u][0]]) if m is None else pl.ds(index_of(u, m), 1)

    def send_step(u, phase, m, step):
        axes = axes_of(u)
        whole, axis = axes[:phase], axes[phase]
        index = phase if m is None else 2 + m
        buf = half_buf[u][phase] if step == 0 else full_buf[u][phase]
        for side, by in ((0, 1), (1, -1)):
            where = moved(at, axis, 2 if step == 0 else by)
            sources = part_of(other[UNITS[u][0]], u, mats_of(u, m), where, whole, side if step == 0 else None)
            width = buf.shape[-1] // len(sources)
            for i, src in enumerate(sources):
                pltpu.make_async_remote_copy(
                    src_ref=src, dst_ref=buf.at[side, mats_of(u, m), :, :, :, pl.ds(i * width, width)],
                    send_sem=send.at[u, index, step], recv_sem=recv.at[u, index, step],
                    device_id=device(moved(at, axis, by), core), device_id_type=MESH,
                ).start()

    def await_step(u, phase, m, step, sem):
        index = phase if m is None else 2 + m
        buf = half_buf[u][phase] if step == 0 else full_buf[u][phase]
        part = buf.at[:, mats_of(u, m)]
        pltpu.make_async_copy(part, part, sem.at[u, index, step]).wait()

    def stage(m, g):
        for u in units_of(m):
            for c in own_loads(u, m, g):
                c.wait()
            await_partner(u, m, g)
            mats = [index_of(u, m)]
            if g == 0:
                add(u, 2, mats, place(u, 2), None, [from_own(u, 0)])
                send_step(u, 2, m, 0)
            elif g == 1:
                await_step(u, 2, m, 0, recv)
                for side, by in ((0, 1), (1, -1)):
                    halves = [from_own(u, side, side), from_buf(half_buf[u][2], side, u, 2)]
                    add(u, 2, mats, place(u, by), side, halves)
                    add(u, 2, mats, place(u, by), 1 - side, [from_own(u, side, 1 - side)])
                send_step(u, 2, m, 1)
            else:
                await_step(u, 2, m, 1, recv)
                arrived = [from_buf(full_buf[u][2], side, u, 2) for side in (0, 1)]
                add(u, 2, mats, at, None, [from_own(u, 0)] + arrived)

    def vec_copy(k):
        (x, y, z) = at
        flip = lambda v: v + 1 - 2 * lax.rem(v, 2)
        to = [
            device(at, 1 - core),
            device((flip(x), y, z), core),
            device((x, flip(y), z), core),
            device((x, y, flip(z)), core),
            device(moved(at, 0, 2), core),
            device(moved(at, 1, 2), core),
            device(moved(at, 2, 2), core),
        ][k]
        return pltpu.make_async_remote_copy(
            src_ref=vec_acc.at[k], dst_ref=vec_in.at[k], send_sem=vec_send.at[k], recv_sem=vec_recv.at[k],
            device_id=to, device_id_type=MESH,
        )

    def vec_step(k):
        if k:
            vec_copy(k - 1).wait_recv()
            vec_acc[k] = vec_acc[k - 1] + vec_in[k - 1]
        if k < VEC_STEPS:
            vec_copy(k).start()
        else:
            vec_out[...] = vec_acc[VEC_STEPS]

    prefetch(2, 0)
    to_partner(2)
    to_partner(1)
    for c in firsts:
        c.wait()
    first_out[:, :DI] = first_grad[...] * silu_slope(first_pre[...])
    first_out[:, DI:] = grad_bc[:8] * silu_slope(state_pre[:8])

    def halo_copy():
        return pltpu.make_async_remote_copy(
            src_ref=first_out, dst_ref=after, send_sem=halo_sem.at[0], recv_sem=halo_sem.at[1],
            device_id=tensor_peer(7), device_id_type=MESH,
        )

    @pl.when(t > 0)
    def _():
        halo_copy().start()

    docs = doc_col[...]
    links = [None] + [conv_links(docs, o, BLOCK + 8) for o in range(1, TAPS)]
    params = small_params(phead[...])
    vec = vec_acc.at[0]
    vec[...] = jnp.zeros(VEC, F32)

    @pl.when(t < 7)
    def _():
        halo_copy().wait_recv()

    @pl.when(t == 7)
    def _():
        after[...] = jnp.zeros_like(after)

    def conv_back(grad, grad_after, ext, taps):
        grad_ext = jnp.concatenate([grad, grad_after], 0)
        total = taps[TAPS - 1 : TAPS] * grad
        rows = [None] * TAPS
        rows[TAPS - 1] = jnp.sum(grad * ext[HALO:], axis=0, keepdims=True)
        for offset in range(1, TAPS):
            masked = grad_ext * links[offset]
            rows[TAPS - 1 - offset] = jnp.sum(masked[:BLOCK] * ext[HALO - offset : EXT - offset], axis=0, keepdims=True)
            total = total + taps[TAPS - 1 - offset : TAPS - offset] * masked[offset : offset + BLOCK]
        return total, rows + [jnp.sum(grad, axis=0, keepdims=True)]

    flat_main = [(lo, y, c) for lo in range(2) for y in range(4) for c in range(2)]

    def put(j, slot):
        cols = tile_of(j)
        return [
            pltpu.make_async_copy(
                staged.at[slot, pl.ds(i * ROWS, ROWS)], grad_main.at[0, lo, y, c, :, cols], put_sem.at[slot, i]
            )
            for i, (lo, y, c) in enumerate(flat_main)
        ]

    def x_tiles(first, last):
        @pl.loop(first, last)
        def _(j):
            slot = lax.rem(j, 2)
            cols = tile_of(j)

            @pl.when(j + 1 < TILES)
            def _():
                for c in stream(j + 1, 1 - slot):
                    c.start()

            for c in stream(j, slot):
                c.wait()
            grad = grad_in[slot] * silu_slope(pre_in[slot])
            total, rows = conv_back(grad, after[:, cols], ext_in[slot], pmain[0:TAPS, cols])
            for i, row in enumerate(rows):
                vec[i : i + 1, cols] = row
            total = total.astype(BF16)
            raw_x[:, cols] = total

            @pl.when(j >= 2)
            def _():
                for c in put(j, slot):
                    c.wait()

            staged[slot] = dot(normed_t[...], total).astype(BF16)
            for c in put(j, slot):
                c.start()

    def small_part():
        grad = grad_bc[...] * silu_slope(state_pre[...])
        total, rows = conv_back(grad, after[:, DI:], raw_ext[:, :256], params[:TAPS, :256])
        for i, row in enumerate(rows):
            vec[i : i + 1, DI : DI + 256] = row
        raw = jnp.concatenate([total.astype(BF16), grad_step_in[...].astype(BF16)], 1)
        acc[...] = acc_in[...] + dot(raw, w_small[...], (1, 1))
        small_acc[...] = dot(normed_t[...], raw).astype(BF16)
        packed = jnp.zeros((512, 8 * LANES), F32)
        for r in range(3):
            rows_r = jnp.concatenate([small_acc[pl.ds(d * 96 + r * 32, 32)] for d in range(16)], 0)
            packed = packed + dot(rows_r, small_map(r), (1, 1))
        small_out[...] = packed.astype(BF16)
        for c in small_puts:
            c.start()

    small_puts = [
        pltpu.make_async_copy(small_out.at[pl.ds(i * 32, 32)], grad_small.at[0, lo, y, c], small_sem.at[i])
        for i, (lo, y, c) in enumerate(flat_main)
    ]

    def input_tiles(first, last):
        @pl.loop(first, last)
        def _(k):
            slot = lax.rem(k, 2)

            def load(n, into):
                return pltpu.make_async_copy(full.at[0, :, tile_of(n)], w_in.at[into], w_sem.at[into])

            @pl.when(k + 1 < TILES)
            def _():
                load(k + 1, 1 - slot).start()

            load(k, slot).wait()
            acc[...] += dot(raw_x[:, tile_of(k)], w_in[slot], (1, 1))

    def input_grad():
        value = hidden[...].astype(F32)
        inv = lax.rsqrt(jnp.mean(value * value, axis=1, keepdims=True) + epsilon)
        rows = value * inv
        grad = acc[...]
        vec[5:6, 0:DI] = vec_gate[0:1, :]
        vec[6:7, 0:D] = jnp.sum(grad * rows, axis=0, keepdims=True)
        vec[5:8, DI + 256 :] = vec_heads[5:8, :]
        dn = grad * gain[...]
        mean = jnp.mean(dn * rows, axis=1, keepdims=True)
        grad_hidden[...] = cot[...].astype(F32) + inv * dn - rows * inv * mean

    stage(2, 0)
    prefetch(1, 0)
    small_part()
    x_tiles(0, 1)
    stage(1, 0)
    prefetch(2, 1)
    x_tiles(1, 3)
    stage(2, 1)
    prefetch(1, 1)
    x_tiles(3, 5)
    stage(1, 1)
    prefetch(2, 2)
    x_tiles(5, 6)
    pltpu.make_async_copy(full.at[0, :, tile_of(0)], w_in.at[0], w_sem.at[0]).start()
    for slot in range(2):
        for c in put(TILES - 2 + slot, slot):
            c.wait()
    for c in small_puts:
        c.wait()
    to_partner(0)
    input_tiles(0, 3)
    stage(2, 2)
    prefetch(1, 2)
    input_tiles(3, 6)
    stage(1, 2)
    prefetch(0, 0)
    input_grad()
    vec_step(0)
    stage(0, 0)
    prefetch(0, 1)
    vec_step(1)
    stage(0, 1)
    prefetch(0, 2)
    vec_step(2)
    stage(0, 2)
    vec_step(3)
    for phase in (1, 0):
        for u in everything:
            send_step(u, phase, None, 0)
        vec_step(4 if phase else 6)
        for u in everything:
            axis = axes_of(u)[phase]
            mats = list(range(STACK[UNITS[u][0]]))
            await_step(u, phase, None, 0, recv)
            for side, by in ((0, 1), (1, -1)):
                add(u, phase, mats, moved(at, axis, by), side, [from_buf(half_buf[u][phase], side, u, phase)])
            send_step(u, phase, None, 1)
        vec_step(5 if phase else 7)
        for u in everything:
            mats = list(range(STACK[UNITS[u][0]]))
            await_step(u, phase, None, 1, recv)
            arrived = [from_buf(full_buf[u][phase], side, u, phase) for side in (0, 1)]
            add(u, phase, mats, at, None, arrived, None if phase else outs[UNITS[u][0]])
    for m in MATS:
        for u in units_of(m):
            part = other[UNITS[u][0]].at[pl.ds(0, 1), :, :, pl.ds(0, 32)]
            pltpu.make_async_copy(part, part, core_send.at[u, m]).wait()
            for step in (0, 1):
                await_step(u, 2, m, step, send)
    for u in everything:
        for phase in (0, 1):
            for step in (0, 1):
                await_step(u, phase, None, step, send)
    for k in range(VEC_STEPS):
        vec_copy(k).wait_send()

    @pl.when(t > 0)
    def _():
        halo_copy().wait_send()


def back(*args):
    vmem = pl.BlockSpec(memory_space=VMEM)
    anywhere = pl.BlockSpec(memory_space=pl.ANY)
    units = range(len(UNITS))
    n = len(UNITS)
    held = [(3, 2, 4, ROWS, 8 * WIDTH), (1, 2, 4, SMALL_ROWS, 8 * SMALL_WIDTH)]
    landing = [(2, STACK[UNITS[u][0]]) + region_shape(u, p, rows) for rows in (16, 32) for u in units for p in range(3)]
    return pl.pallas_call(
        back_kernel,
        name="project_back",
        out_shape=[
            jax.ShapeDtypeStruct((1, 2, 4, 2, ROWS, DI), BF16),
            jax.ShapeDtypeStruct((1, 2, 4, 2, SMALL_ROWS, 8 * LANES), BF16),
            jax.ShapeDtypeStruct((3, ROWS, WIDTH), F32),
            jax.ShapeDtypeStruct((1, SMALL_ROWS, SMALL_WIDTH), F32),
            jax.ShapeDtypeStruct((BLOCK, D), F32),
            jax.ShapeDtypeStruct(VEC, F32),
        ],
        in_specs=[vmem] * 15 + [anywhere] * 6,
        out_specs=[anywhere, anywhere, vmem, vmem, vmem, vmem],
        scratch_shapes=[VMEM(s, BF16) for s in held + landing]
        + [VMEM((2,) + region_shape(u, 2, 32), BF16) for u in units]
        + [
            VMEM((2, EXT, TILE), F32), VMEM((2, BLOCK, TILE), F32), VMEM((2, BLOCK, TILE), F32),
            VMEM((8, DI), F32), VMEM((8, DI), F32), VMEM((8, DI + 256), F32), VMEM((8, DI + 256), F32),
            VMEM((2, D, TILE), BF16), VMEM((2, D, TILE), BF16), VMEM((BLOCK, DI), BF16),
            VMEM((BLOCK, D), F32), VMEM((D, SMALL), BF16), VMEM((512, 8 * LANES), BF16),
            VMEM((VEC_STEPS + 1,) + VEC, F32), VMEM((VEC_STEPS,) + VEC, F32),
        ]
        + [
            pltpu.SemaphoreType.DMA(s)
            for s in (
                (3, 2), (2,), (2,), (2,), (2, 16), (16,), (n, 2, 2), (VEC_STEPS,), (VEC_STEPS,), (n, 5, 2), (n, 5, 2),
                (n, 3), (n, 3, 3),
            )
        ],
        compiler_params=pltpu.CompilerParams(collective_id=3, has_side_effects=True, vmem_limit_bytes=62 * 2**20),
    )(*args)


def per_device(
    hidden,
    doc_ids,
    norm_gain,
    main_proj,
    step_proj,
    state_proj,
    conv_main,
    conv_main_bias,
    conv_state,
    conv_state_bias,
    step_bias,
    decay_log,
    skip_gain,
    gate_gain,
    out_proj,
    cotangent,
):
    t = lax.axis_index("tensor")
    shards = jnp.stack([main_proj[:, 1], main_proj[:, 0], out_proj])
    small = jnp.concatenate([state_proj, step_proj], axis=1).reshape(3, SMALL_ROWS, 38)
    small = jnp.pad(small.transpose(1, 0, 2).reshape(SMALL_ROWS, 114), ((0, 0), (0, 14)))[None]
    params = pack_params(
        conv_main, conv_main_bias, conv_state, conv_state_bias, step_bias, decay_log, skip_gain, gate_gain
    )
    full, packed, halo, pmain, phead = gather_weights(shards, small, hidden[BLOCK - HALO :], params)
    full, packed = full.reshape(3, D, DI), packed.reshape(512, 8 * LANES)
    gain = norm_gain[None]

    docs_all = jnp.concatenate([jnp.full((HALO,), -1, jnp.int32), doc_ids, jnp.full((16,), -2, jnp.int32)])
    docs = lax.dynamic_slice(docs_all, (t * BLOCK,), (EXT + 16,))
    doc_col, doc_row = docs[:, None], docs[None, HALO:EXT]

    (mixed, normed_t, raw, state_pre, grad_bc, grad_step_in, w_small, acc, grad_x, vec_gate, vec_heads, x_ext, x_pre,
     grad_out, grad_gate) = mid(
        hidden, halo, gain, packed, pmain, phead, doc_col, doc_row, cotangent, full
    )
    _, _, own_main, own_small, grad_hidden, vec = back(
        normed_t, raw, state_pre, grad_bc, grad_step_in, w_small, acc, pmain, phead, doc_col, hidden, cotangent,
        gain, vec_gate, vec_heads, x_ext, x_pre, grad_x, grad_gate, grad_out, full,
    )
    own_small = own_small[0, :, :114].reshape(SMALL_ROWS, 3, 38).transpose(1, 0, 2).reshape(ROWS, 38)
    vec_main = lax.dynamic_slice(vec, (0, t * WIDTH), (8, WIDTH))
    vec_state = lax.dynamic_slice(vec, (0, DI + t * 32), (5, 32))
    vec_head = lax.dynamic_slice(vec, (5, DI + 256 + t * 6), (3, 6))
    return (
        mixed,
        grad_hidden,
        vec[6, :D],
        jnp.stack([own_main[1], own_main[0]], axis=1),
        own_small[:, 32:],
        own_small[:, :32],
        vec_main[:TAPS],
        vec_main[TAPS],
        vec_state[:TAPS],
        vec_state[TAPS],
        vec_head[0],
        vec_head[1],
        vec_head[2],
        vec_main[5],
        own_main[2],
    )


def solution(mesh):
    placed = (
        P(("dp", "tensor"), None),
        P("dp"),
        P(),
        P("dp", None, "tensor"),
        P("dp", "tensor"),
        P("dp", "tensor"),
        P(None, "tensor"),
        P("tensor"),
        P(None, "tensor"),
        P("tensor"),
        P("tensor"),
        P("tensor"),
        P("tensor"),
        P("tensor"),
        P("dp", "tensor"),
        P(("dp", "tensor"), None),
    )
    return jax.shard_map(
        per_device,
        mesh=mesh,
        in_specs=placed,
        out_specs=(
            P(("dp", "tensor"), None),
            P(("dp", "tensor"), None),
            P(),
            P("dp", None, "tensor"),
            P("dp", "tensor"),
            P("dp", "tensor"),
            P(None, "tensor"),
            P("tensor"),
            P(None, "tensor"),
            P("tensor"),
            P("tensor"),
            P("tensor"),
            P("tensor"),
            P("tensor"),
            P("dp", "tensor"),
        ),
        check_vma=False,
    )
```

time: 379 us -> 312 us (0.82)
  Pallas kernels: 341 us -> 282 us
  waiting for transfers between devices: 5.29 us -> 0 us
    pallas_call x3 -> x1, Pallas kernels: 143 us -> 87.3 us  [back(): pl.pallas_call(back_kernel, name='project_back', out_shape=[jax.ShapeDtyp...]
    ppermute x1 -> x0, waiting for transfers between devices: 5.29 us -> none  [per_device(): after = lax.ppermute(first, 'tensor', [(i, i - 1) for i in range(1, 8)])]
  transfers between devices with their start and end apart: 1 -> 0, of which waited for: 1 -> 0; matrix products, arithmetic and copies ran while one was open for 0% -> 0% of each run, Pallas kernels for 0% -> 0%
where the time goes in v3:
time: 312 us; the launch traced here: 311 us
  Pallas kernels  282 us (90%)
  local copies, waits for them, and re-layouts  24.9 us (8%)
  other arithmetic  3.76 us (1%)
    pallas_call x1, Pallas kernels, mid(): pl.pallas_call(mid_kernel, name='scan_and_gate', out_shape=[jax.ShapeDtyp...  114 us
    pallas_call x1, Pallas kernels, back(): pl.pallas_call(back_kernel, name='project_back', out_shape=[jax.ShapeDtyp...  87.3 us
    pallas_call x1, Pallas kernels, gather_weights(): pl.pallas_call(gather_kernel, name='gather_weights', out_shape=[jax.Shape...  80.1 us

profile of v3, /device:TPU:0, one launch (start us, length us, event | category | flops | bytes accessed | tf_op | source)
XLA Modules:
  0.0 311.4 jit_solution(18401781169127804645)
XLA Ops:
  0.6 1.2 fusion.3
  1.9 1.6 pad_maximum_fusion.1.refs_0_
  3.5 0.7 pad_maximum_fusion.2
  4.2 0.1 copy.49
  4.4 0.1 reshape.46
  4.5 0.6 pad_bitcast_fusion.refs_1_
  5.1 1.4 slice.59.refs_2_
  6.5 0.7 broadcast_in_dim.28
  7.2 0.7 broadcast_in_dim.29
  7.9 0.7 broadcast_in_dim.30
  8.6 0.1 broadcast_in_dim_reshape.3
  8.7 1.3 concatenate.13.refs_3_
  10.0 1.4 fusion.refs_4_
  11.4 80.1 %gather_weights.1 = (bf16[3,2,4,2,96,3072]{5,4,3,2,1,0:T(8,128)(2,1)}, bf16[1,2,4,2,32,1024]{5,4,3,2,1,0:T(8,128)(2,1)}, bf16[16,1536]{1,0:T(8,128)(2,1)}, f32[8,3072]{1,0:T(8,128)}, f32[8,1024]{1,0:T(8,128)}) custom-call(bf16[3,96,384]{2,1,0:T(8,128)(2,1)} %pad_maximum_fusion.1.refs_0_, bf16[1,32,128]{2,1,0:T(8,128)(2,1)} %pad_bitcast_fusion.refs_1_, ...), custom_call_target="tpu_custom_call" | custom-call | tf_op jit(solution)/shard_map/gather_weights/pallas_call | solution.py:218
  91.6 1.3 broadcast_in_dim.33.gain.refs_12_
  92.9 0.8 concatenate.15
  93.6 0.1 dynamic_slice.12
  93.7 0.8 broadcast_in_dim.36.doc_col.refs_9_
  94.5 0.6 slice.60
  95.1 114.5 %scan_and_gate.1 = (bf16[256,1536]{1,0:T(8,128)(2,1)}, bf16[1536,256]{1,0:T(8,128)(2,1)}, f32[272,384]{1,0:T(8,128)}, f32[256,256]{1,0:T(8,128)}, f32[256,256]{1...) custom-call(bf16[256,1536]{1,0:T(8,128)(2,1)} %refs_10_.1, ...), custom_call_target="tpu_custom_call" | custom-call | tf_op jit(solution)/shard_map/scan_and_gate/pallas_call | solution.py:777
  209.6 0.0 copy-start.1
  209.6 87.3 %project_back.1 = (bf16[1,2,4,2,96,3072]{5,4,3,2,1,0:T(8,128)(2,1)}, bf16[1,2,4,2,32,1024]{5,4,3,2,1,0:T(8,128)(2,1)}, f32[3,96,384]{2,1,0:T(8,128)}, f32[1,32,1...) custom-call(bf16[1536,256]{1,0:T(8,128)(2,1)} %get-tuple-element.45.refs_0_, ...), custom_call_target="tpu_custom_call" | custom-call | tf_op jit(solution)/shard_map/project_back/pallas_call | solution.py:1216
  296.9 0.0 copy-start
  297.0 1.5 slice_reduce_fusion
  298.5 1.7 slice_bitcast_fusion
  300.3 0.9 copy.54
  301.2 0.8 reshape_squeeze.3
  302.0 0.1 slice.76
  302.1 0.7 copy.55
  302.8 0.7 copy.56
  303.5 1.3 constant_dynamic-slice_fusion.1
  304.8 1.5 dynamic-slice_reduce_fusion
  306.2 0.7 constant_dynamic-slice_fusion.2
  307.0 0.6 slice.69
  307.5 0.5 slice_bitcast_fusion.6
  308.1 0.8 constant_dynamic-slice_fusion
  308.8 0.5 slice_bitcast_fusion.3
  309.3 0.0 copy-done.1
  309.3 0.9 copy.63
  310.2 0.0 copy-done
  310.2 1.1 copy.64
  (7 shorter events, 0.1 us)
Async XLA Ops:
  209.6 99.7 %copy-start.1 = (bf16[256,1536]{1,0:T(8,128)(2,1)S(1)}, bf16[256,1536]{1,0:T(8,128)(2,1)}, u32[]{:S(2)}) copy-start(bf16[256,1536]{1,0:T(8,128)(2,1)} %get-tuple-element.135) | copy-start | bytes 2359300
  296.9 13.3 %copy-start = (f32[256,1536]{1,0:T(8,128)S(1)}, f32[256,1536]{1,0:T(8,128)}, u32[]{:S(2)}) copy-start(f32[256,1536]{1,0:T(8,128)} %get-tuple-element.136) | copy-start | bytes 4718596

commit v4 on v3

--- a/solution.py
+++ b/solution.py
@@ -91,153 +91,43 @@
     return ref.at[mats, pl.ds(0, max(rest // 4, 1)), pl.ds(0, min(rest, 4)), 0, pl.ds(0, 16 * halves), pl.ds(0, cols * width)]
 
 
-def gather_kernel(*refs):
-    shards, small, tail, params = refs[0], refs[1], refs[2], refs[3:5]
-    full, halo, params_all = refs[5:7], refs[7], refs[8:10]
-    own_sem, halo_sem, param_send, param_recv, send, recv, core_send, core_recv = refs[10:]
+def gather_ops(full, send, recv, core_send, core_recv):
     at, core = coordinates()
-    t = lax.axis_index("tensor")
-    own = []
-    for w, source in enumerate((shards, small)):
-        for lo, row, cols in pieces(at, (), WIDTHS[w]):
-            own.append(
-                pltpu.make_async_copy(source, full[w].at[:, lo.start, row.start, core, :, cols], own_sem.at[w])
-            )
-    def columns(i, of):
-        width = params[i].shape[-1]
-        return params_all[i].at[:, pl.ds(pl.multiple_of(of * width, 128), width)]
-
-    for i in range(2):
-        own.append(pltpu.make_async_copy(params[i], columns(i, t), own_sem.at[2 + i]))
-    for c in own:
-        c.start()
-    greet(at, core, [tensor_peer(by) for by in range(1, 8)])
-    last = []
-
-    def go(copy, wait=True):
-        copy.start()
-        if wait:
-            last.append(copy)
-
-    def tail_copy():
-        return pltpu.make_async_remote_copy(
-            src_ref=tail, dst_ref=halo, send_sem=halo_sem.at[0], recv_sem=halo_sem.at[1],
-            device_id=tensor_peer(1), device_id_type=MESH,
-        )
-
-    def param_copy(by, i, of):
-        return pltpu.make_async_remote_copy(
-            src_ref=params[i], dst_ref=columns(i, of), send_sem=param_send.at[i, by - 1],
-            recv_sem=param_recv.at[i, by - 1], device_id=tensor_peer(by), device_id_type=MESH,
-        )
-
-    go(tail_copy())
-    for by in range(1, 8):
-        for i in range(2):
-            go(param_copy(by, i, t))
-    for c in own:
-        c.wait()
-
-    def slot(u, phase, m):
-        return (phase if phase < 2 else 2 + m), [u]
-
-    def mats_of(u, phase, m):
-        return pl.ds(0, STACK[UNITS[u][0]]) if phase < 2 else pl.ds(m, 1)
-
-    def sends(u, phase, m, step):
+
+    def sends(u, phase, mats, step, key):
         axes = axes_of(u)
         whole, axis = axes[:phase], axes[phase]
-        index = phase if phase < 2 else 2 + m
-        ref = full[UNITS[u][0]]
         for kind, by in ((0, 1), (1, -1)):
             where = at if step == 0 else moved(at, axis, -by)
-            for part in region(ref, u, core, mats_of(u, phase, m), where, whole, kind if step else None):
+            for part in region(full[UNITS[u][0]], u, core, mats, where, whole, kind if step else None):
                 pltpu.make_async_remote_copy(
-                    src_ref=part, dst_ref=part, send_sem=send.at[u, index, step],
-                    recv_sem=recv.at[u, index, step],
+                    src_ref=part, dst_ref=part, send_sem=send.at[u, key, step], recv_sem=recv.at[u, key, step],
                     device_id=device(moved(at, axis, by), core), device_id_type=MESH,
                 ).start()
 
-    def await_step(u, phase, m, step, sem):
-        index = phase if phase < 2 else 2 + m
-        part = sized(full[UNITS[u][0]], u, mats_of(u, phase, m), 2 * 4**phase // (1 + step))
-        pltpu.make_async_copy(part, part, sem.at[u, index, step]).wait()
-
-    def to_partner(u, m, where, whole):
-        for part in region(full[UNITS[u][0]], u, core, mats_of(u, 2, m), where, whole):
-            pltpu.make_async_remote_copy(
-                src_ref=part, dst_ref=part, send_sem=core_send.at[u, m],
-                recv_sem=core_recv.at[u, m], device_id=device(at, 1 - core), device_id_type=MESH,
-            ).start()
-
-    everything = range(len(UNITS))
-    late = [(u, m) for m in range(3) for u in everything if m < STACK[UNITS[u][0]]]
-    for phase in (0, 1):
-        for u in everything:
-            sends(u, phase, 0, 0)
-        for u in everything:
-            await_step(u, phase, 0, 0, recv)
-            sends(u, phase, 0, 1)
-        for u in everything:
-            await_step(u, phase, 0, 1, recv)
-    for u, m in late:
-        sends(u, 2, m, 0)
-    for u, m in late:
-        to_partner(u, m, at, axes_of(u)[:2])
-    for u, m in late:
-        await_step(u, 2, m, 0, recv)
-        sends(u, 2, m, 1)
-        whole, axis = axes_of(u)[:2], axes_of(u)[2]
-        for by in (-1, 1):
-            to_partner(u, m, moved(at, axis, by), whole)
-    for u, m in late:
-        await_step(u, 2, m, 1, recv)
-        whole, axis = axes_of(u)[:2], axes_of(u)[2]
-        to_partner(u, m, moved(at, axis, 2), whole)
-    for u, m in late:
-        part = sized(full[UNITS[u][0]], u, mats_of(u, 2, m), 64)
-        pltpu.make_async_copy(part, part, core_recv.at[u, m]).wait()
-        pltpu.make_async_copy(part, part, core_send.at[u, m]).wait()
-    tail_copy().wait_recv()
-    for by in range(1, 8):
-        for i in range(2):
-            param_copy(by, i, lax.rem(t + 8 - by, 8)).wait_recv()
-    for u in everything:
-        for phase in (0, 1):
-            for step in (0, 1):
-                await_step(u, phase, 0, step, send)
-    for u, m in late:
-        for step in (0, 1):
-            await_step(u, 2, m, step, send)
-    for c in last:
-        c.wait_send()
-
-
-def gather_weights(shards, small, tail, params):
-    units = len(UNITS)
-    return pl.pallas_call(
-        gather_kernel,
-        name="gather_weights",
-        out_shape=[
-            jax.ShapeDtypeStruct((3, 2, 4, 2, ROWS, 8 * WIDTH), jnp.bfloat16),
-            jax.ShapeDtypeStruct((1, 2, 4, 2, SMALL_ROWS, 8 * SMALL_WIDTH), jnp.bfloat16),
-            jax.ShapeDtypeStruct(tail.shape, tail.dtype),
-        ]
-        + [jax.ShapeDtypeStruct((8, 8 * p.shape[1]), p.dtype) for p in params],
-        in_specs=[pl.BlockSpec(memory_space=pl.ANY)] * 5,
-        out_specs=[pl.BlockSpec(memory_space=pl.ANY)] * 5,
-        scratch_shapes=[
-            pltpu.SemaphoreType.DMA((4,)),
-            pltpu.SemaphoreType.DMA((2,)),
-            pltpu.SemaphoreType.DMA((2, 7)),
-            pltpu.SemaphoreType.DMA((2, 7)),
-            pltpu.SemaphoreType.DMA((units, 5, 2)),
-            pltpu.SemaphoreType.DMA((units, 5, 2)),
-            pltpu.SemaphoreType.DMA((units, 3)),
-            pltpu.SemaphoreType.DMA((units, 3)),
-        ],
-        compiler_params=pltpu.CompilerParams(collective_id=0, has_side_effects=True),
-    )(shards, small, tail, *params)
+    def await_step(u, phase, mats, step, key, sem):
+        part = sized(full[UNITS[u][0]], u, mats, 2 * 4**phase // (1 + step))
+        pltpu.make_async_copy(part, part, sem.at[u, key, step]).wait()
+
+    def to_partner(u, mats, bys, key):
+        axes = axes_of(u)
+        for by in bys:
+            where = moved(at, axes[2], by) if by else at
+            for part in region(full[UNITS[u][0]], u, core, mats, where, axes[:2]):
+                pltpu.make_async_remote_copy(
+                    src_ref=part, dst_ref=part, send_sem=core_send.at[u, key], recv_sem=core_recv.at[u, key],
+                    device_id=device(at, 1 - core), device_id_type=MESH,
+                ).start()
+
+    def await_partner(u, mats, key, sem):
+        part = sized(full[UNITS[u][0]], u, mats, 64)
+        pltpu.make_async_copy(part, part, sem.at[u, key]).wait()
+
+    return sends, await_step, to_partner, await_partner
+
+
+MAIN_UNITS = range(3)
+ALL = pl.ds(0, 3)
 
 
 D, DI, HEADS, HEAD_DIM, STATE, TAPS, HALO = 1536, 3072, 48, 64, 128, 4, 16
@@ -331,22 +221,104 @@
     return enter, tail, tail * step, keep
 
 
-def pack_params(conv_main, conv_main_bias, conv_state, conv_state_bias, step_bias, decay_log, skip_gain, gate_gain):
-    main = jnp.concatenate(
-        [conv_main, conv_main_bias[None], gate_gain[None], jnp.repeat(skip_gain, HEAD_DIM)[None],
-         jnp.zeros((1, WIDTH), F32)]
-    )
-    state = jnp.pad(jnp.concatenate([conv_state, conv_state_bias[None]]), ((0, 3), (0, 96)))
-    heads = jnp.pad(jnp.stack([step_bias, decay_log, skip_gain]), ((5, 0), (32, 90)))
-    return main, state + heads
+def pack_kernel(
+    main_proj, out_proj, state_proj, step_proj, conv_main, conv_main_bias, conv_state, conv_state_bias, step_bias,
+    decay_log, skip_gain, gate_gain, norm_gain, doc_ids,
+    shards, small, pmain, phead, doc_col, doc_row, gain, docs,
+):
+    t = lax.axis_index("tensor")
+    shards[0] = main_proj[:, 1, :]
+    shards[1] = main_proj[:, 0, :]
+    shards[2] = out_proj[...]
+    lanes = [jnp.concatenate([state_proj[...], step_proj[...]], 1)[r * 32 : r * 32 + 32] for r in range(3)]
+    small[0] = jnp.concatenate(lanes + [jnp.zeros((SMALL_ROWS, 14), BF16)], 1)
+    pmain[0:TAPS] = conv_main[...]
+    pmain[TAPS : TAPS + 1] = conv_main_bias[...].reshape(1, WIDTH)
+    pmain[5:6] = gate_gain[...].reshape(1, WIDTH)
+    own_skip = skip_gain[...].reshape(1, 6)
+    pmain[6:7] = jnp.concatenate([jnp.broadcast_to(own_skip[:, h : h + 1], (1, HEAD_DIM)) for h in range(6)], 1)
+    pmain[7:8] = jnp.zeros((1, WIDTH), F32)
+    phead[...] = jnp.zeros_like(phead)
+    phead[0:TAPS, 0:32] = conv_state[...]
+    phead[TAPS : TAPS + 1, 0:32] = conv_state_bias[...].reshape(1, 32)
+    phead[5:6, 32:38] = step_bias[...].reshape(1, 6)
+    phead[6:7, 32:38] = decay_log[...].reshape(1, 6)
+    phead[7:8, 32:38] = own_skip
+    gain[...] = norm_gain[...].reshape(1, D)
+    docs[:, 0:LANES] = jnp.full((8, LANES), -1, jnp.int32)
+    docs[:, LANES : LANES + 2048] = jnp.broadcast_to(doc_ids[...].reshape(1, 2048), (8, 2048))
+    docs[:, LANES + 2048 :] = jnp.full((8, LANES), -2, jnp.int32)
+    window = docs[:, pl.ds(pl.multiple_of(t * BLOCK, LANES), 2 * BLOCK)]
+    doc_row[...] = window[0:1, LANES : LANES + BLOCK]
+    doc_col[...] = window.T[LANES - HALO : LANES + BLOCK + 16, 0:1]
+
+
+def pack(*args):
+    vmem = pl.BlockSpec(memory_space=VMEM)
+    shapes = [
+        ((3, ROWS, WIDTH), BF16), ((1, SMALL_ROWS, SMALL_WIDTH), BF16), ((8, WIDTH), F32), ((8, LANES), F32),
+        ((EXT + 16, 1), jnp.int32), ((1, BLOCK), jnp.int32), ((1, D), F32),
+    ]
+    return pl.pallas_call(
+        pack_kernel,
+        name="pack",
+        out_shape=[jax.ShapeDtypeStruct(*s) for s in shapes],
+        in_specs=[vmem] * 14,
+        out_specs=[vmem] * len(shapes),
+        scratch_shapes=[VMEM((8, 2048 + 2 * LANES), jnp.int32)],
+    )(*args)
+
+
+def finish_kernel(
+    own_main, own_small, vec,
+    norm_gain, main_proj, step_proj, state_proj, conv_main, conv_main_bias, conv_state, conv_state_bias, step_bias,
+    decay_log, skip_gain, gate_gain, out_proj,
+):
+    t = lax.axis_index("tensor")
+    main_proj[:, 0, :] = own_main[1]
+    main_proj[:, 1, :] = own_main[0]
+    out_proj[...] = own_main[2]
+    packed = own_small[0]
+    for r in range(3):
+        rows = pl.ds(r * 32, 32)
+        state_proj[rows] = packed[:, r * 38 : r * 38 + 32]
+        step_proj[rows] = packed[:, r * 38 + 32 : r * 38 + 38]
+    own = vec[:, pl.ds(pl.multiple_of(t * WIDTH, LANES), WIDTH)]
+    conv_main[...] = own[:TAPS]
+    conv_main_bias[...] = own[TAPS : TAPS + 1]
+    gate_gain[...] = own[5:6]
+    state = pltpu.roll(vec[:, DI : DI + 256], lax.rem(256 - 32 * t, 256), axis=1)
+    conv_state[...] = state[:TAPS, :32]
+    conv_state_bias[...] = state[TAPS : TAPS + 1, :32]
+    heads = pltpu.roll(vec[:, DI + 256 :], lax.rem(LANES - 6 * t, LANES), axis=1)
+    step_bias[...] = heads[5:6, :6]
+    decay_log[...] = heads[6:7, :6]
+    skip_gain[...] = heads[7:8, :6]
+    norm_gain[...] = vec[6:7, 0:D]
+
+
+def finish(*args):
+    vmem = pl.BlockSpec(memory_space=VMEM)
+    shapes = [
+        (1, D), (ROWS, 2, WIDTH), (ROWS, 6), (ROWS, 32), (TAPS, WIDTH), (1, WIDTH), (TAPS, 32), (1, 32), (1, 6), (1, 6),
+        (1, 6), (1, WIDTH), (ROWS, WIDTH),
+    ]
+    outs = pl.pallas_call(
+        finish_kernel,
+        name="finish",
+        out_shape=[jax.ShapeDtypeStruct(s, F32) for s in shapes],
+        in_specs=[vmem] * 3,
+        out_specs=[vmem] * len(shapes),
+    )(*args)
+    return [v[0] if v.shape[0] == 1 else v for v in outs]
 
 
 PAIR = 2 * HEAD_DIM
 PAIRS = DI // PAIR
 HALF = BLOCK // 2
-CHUNK = 256
+CHUNK = 128
 CHUNKS = DI // CHUNK
-FORWARD_LAG, BACKWARD_LAG = 4, 2
+FORWARD_LAG, BACKWARD_LAG = 7, 4
 
 
 def pair_of(p):
@@ -367,33 +339,137 @@
 
 
 def mid_kernel(
-    hidden, halo, gain, packed, pmain, phead, doc_col, doc_row, cot, full,
-    mixed, normed_t, raw, state_pre, grad_bc, grad_step_in, w_small, acc, grad_x, vec_gate, vec_heads,
-    x_ext, x_pre, grad_out, grad_gate,
-    normed, w_in, ext_out, pre_out, staged, x_act, bc, scores, gate_in, work, y, gate_out, dy, gate_grad, update,
+    hidden, gain, doc_col, doc_row, cot, shards, small, pmain_own, phead_own,
+    mixed, pmain, phead, normed_t, raw, state_pre, grad_bc, grad_step_in, w_small, acc, grad_x, vec_gate, vec_heads,
+    x_ext, x_pre, grad_out, grad_gate, full,
+    packed, halo, normed, w_in, ext_out, pre_out, staged, x_act, bc, scores, gate_in, work, y, gate_out, dy, gate_grad, update,
     grad_add, state, state_low, grad_state, keep_row, f_out, f_in, b_out, b_in, cot_t, mixed_acc,
     barred, cum2, cum_t, step_t, step_in, enter_ref, weight_ref, rows_acc, q_t, gs, acc_c, acc_heads, row_acc,
-    w_sem, put_sem, x_sem, f_send, f_recv, b_send, b_recv,
+    w_sem, put_sem, x_sem, f_send, f_recv, b_send, b_recv, g_send, g_recv, core_send, core_recv, own_sem, halo_sem,
+    param_send, param_recv,
 ):
     t = lax.axis_index("tensor")
 
     def load(m, j, slot):
-        return pltpu.make_async_copy(full.at[m, :, tile_of(j)], w_in.at[slot], w_sem.at[slot])
-
-    load(0, 0, 0).start()
-    barrier = pltpu.get_barrier_semaphore()
-    for other in (tensor_peer(1), tensor_peer(7)):
-        pl.semaphore_signal(barrier, inc=1, device_id=other, device_id_type=MESH)
-    pl.semaphore_wait(barrier, 2)
-
-    for rows, part in ((pl.ds(0, HALO), halo), (pl.ds(HALO, BLOCK), hidden)):
+        return pltpu.make_async_copy(full.at[m, :, :, :, :, tile_of(j)], w_in.at[slot], w_sem.at[slot])
+
+    def held(slot):
+        return w_in[slot].reshape(D, TILE)
+
+    at, core = coordinates()
+    both = [full, packed]
+    own = []
+    for w, source in enumerate((shards, small)):
+        for lo, row, cols in pieces(at, (), WIDTHS[w]):
+            own.append(
+                pltpu.make_async_copy(source, both[w].at[:, lo.start, row.start, core, :, cols], own_sem.at[w])
+            )
+    params_own, params_all = (pmain_own, phead_own), (pmain, phead)
+
+    def columns(i, of):
+        width = params_own[i].shape[-1]
+        return params_all[i].at[:, pl.ds(pl.multiple_of(of * width, 128), width)]
+
+    for i in range(2):
+        own.append(pltpu.make_async_copy(params_own[i], columns(i, t), own_sem.at[2 + i]))
+    for c in own:
+        c.start()
+    greet(at, core, [tensor_peer(by) for by in range(1, 8)])
+    sends, await_step, to_partner, await_partner = gather_ops(both, g_send, g_recv, core_send, core_recv)
+
+    def halo_copy():
+        return pltpu.make_async_remote_copy(
+            src_ref=hidden.at[pl.ds(BLOCK - HALO, HALO)], dst_ref=halo, send_sem=halo_sem.at[0],
+            recv_sem=halo_sem.at[1], device_id=tensor_peer(1), device_id_type=MESH,
+        )
+
+    def param_copy(by, i, of):
+        return pltpu.make_async_remote_copy(
+            src_ref=params_own[i], dst_ref=columns(i, of), send_sem=param_send.at[i, by - 1],
+            recv_sem=param_recv.at[i, by - 1], device_id=tensor_peer(by), device_id_type=MESH,
+        )
+
+    everything = [3, 0, 1, 2]
+
+    def early(u):
+        return pl.ds(0, STACK[UNITS[u][0]])
+
+    def rms(rows, part):
         value = part[...].astype(F32)
         inv = lax.rsqrt(jnp.mean(value * value, axis=1, keepdims=True) + epsilon)
         normed[rows] = (value * inv * gain[...]).astype(BF16)
-    normed_t[...] = normed[pl.ds(HALO, BLOCK)].T
-    cot_t[...] = cot[...].T
+
+    for c in own:
+        c.wait()
+    for u in everything:
+        sends(u, 0, early(u), 0, 0)
+    halo_copy().start()
+    for by in range(1, 8):
+        for i in range(2):
+            param_copy(by, i, t).start()
+    rms(pl.ds(HALO, BLOCK), hidden)
+    for phase in (0, 1):
+        for u in everything:
+            await_step(u, phase, early(u), 0, phase, g_recv)
+            sends(u, phase, early(u), 1, phase)
+        if phase == 0:
+            cot_t[...] = cot[...].T
+        else:
+            normed_t[...] = normed[pl.ds(HALO, BLOCK)].T
+        for u in everything:
+            await_step(u, phase, early(u), 1, phase, g_recv)
+            if phase == 0:
+                sends(u, 1, early(u), 0, 1)
+
+    def units_with(m):
+        return [3] if m == 3 else MAIN_UNITS
+
+    def gather_first(m):
+        for u in units_with(m):
+            sends(u, 2, pl.ds(m % 3, 1), 0, 2 + m % 3)
+
+    def gather_near(m):
+        for u in units_with(m):
+            to_partner(u, pl.ds(m % 3, 1), [0], m % 3)
+
+    def gather_forward(m):
+        for u in units_with(m):
+            await_step(u, 2, pl.ds(m % 3, 1), 0, 2 + m % 3, g_recv)
+            sends(u, 2, pl.ds(m % 3, 1), 1, 2 + m % 3)
+
+    def gather_second(m):
+        for u in units_with(m):
+            to_partner(u, pl.ds(m % 3, 1), [-1, 1], m % 3)
+
+    def gather_last(m):
+        for u in units_with(m):
+            await_step(u, 2, pl.ds(m % 3, 1), 1, 2 + m % 3, g_recv)
+            to_partner(u, pl.ds(m % 3, 1), [2], m % 3)
+
+    def gather_done(m):
+        for u in units_with(m):
+            await_partner(u, pl.ds(m % 3, 1), m % 3, core_recv)
+
+    gather_first(3)
+    gather_first(0)
+    gather_near(3)
+    gather_near(0)
+    halo_copy().wait()
+    rms(pl.ds(0, HALO), halo)
+    for by in range(1, 8):
+        for i in range(2):
+            param_copy(by, i, lax.rem(t + 8 - by, 8)).wait()
+    gather_forward(3)
+    gather_second(3)
+    gather_last(3)
+    gather_forward(0)
+    gather_first(1)
+    gather_first(2)
+    gather_second(0)
+    gather_done(3)
+
     for r in range(3):
-        rows = dot(packed[...], small_map(r)).astype(BF16)
+        rows = dot(packed[...].reshape(512, 8 * LANES), small_map(r)).astype(BF16)
         for d in range(16):
             w_small[pl.ds(d * 96 + r * 32, 32)] = rows[d * 32 : d * 32 + 32]
     raw[...] = dot(normed[...], w_small[...])
@@ -421,6 +497,12 @@
     barred[...] = jnp.where(linked, 0.0, -1e30)
     keep8 = jnp.broadcast_to(keep, (8, LANES))
 
+    gather_last(0)
+    gather_near(1)
+    gather_near(2)
+    gather_done(0)
+    load(0, 0, 0).start()
+
     def chain(forward, c, add, into, outgoing, incoming, send, recv):
         cols = chunk_of(c)
         by = 1 if forward else 7
@@ -467,18 +549,13 @@
             for i, (src, dst) in enumerate(((ext_out, x_ext), (pre_out, x_pre)))
         ]
 
-    @pl.loop(0, TILES)
-    def _(j):
+    def x_tile(j):
         cols = tile_of(j)
         slot = lax.rem(j, 2)
 
         @pl.when(j + 1 < TILES)
         def _():
             load(0, j + 1, 1 - slot).start()
-
-        @pl.when(j + 1 == TILES)
-        def _():
-            load(1, 0, 0).start()
 
         @pl.when(j >= 2)
         def _():
@@ -486,7 +563,7 @@
                 c.wait()
 
         load(0, j, slot).wait()
-        ext = dot(normed[...], w_in[slot])
+        ext = dot(normed[...], held(slot))
         ext_out[slot] = ext
         pre = conv(ext, pmain[0:TAPS, cols], pmain[TAPS : TAPS + 1, cols], links)
         pre_out[slot] = pre
@@ -497,10 +574,15 @@
         heavy = (act.astype(F32) * widen(weight_ref[...], j)).astype(BF16)
         update[:, cols] = dot(bc[:, :STATE], heavy, (0, 0))
         keep_row[:, cols] = widen(keep8, j)
-        forward_slot(2 * j)
-        forward_slot(2 * j + 1)
-
-    load(2, 0, 1).start()
+        for k in range(4):
+            forward_slot(4 * j + k)
+
+    gather_forward(1)
+    gather_second(1)
+    pl.loop(0, 3)(x_tile)
+    gather_forward(2)
+    gather_second(2)
+    pl.loop(3, TILES)(x_tile)
     for slot in range(2):
         for c in x_puts(TILES - 2 + slot, slot):
             c.wait()
@@ -522,34 +604,55 @@
             ]
             y[rows, cols] = dot(jnp.concatenate(mix, 1), jnp.concatenate([v[js] for v in x2], 0))
 
-    @pl.loop(0, PAIRS)
-    def _(i):
-        intra_forward(i)
-        j = lax.div(i, 4)
-
-        @pl.when(lax.rem(i, 4) == 0)
+    def scan_pairs(first, last):
+        @pl.loop(first, last)
+        def _(i):
+            forward_slot(4 * TILES + 2 * i)
+            intra_forward(i)
+            forward_slot(4 * TILES + 2 * i + 1)
+
+    def gate_tile(j, slot):
+        gate_in[:, tile_of(j)] = dot(normed[pl.ds(HALO, BLOCK)], held(slot))
+
+    def out_tile(j, slot):
+        work[:, tile_of(j)] = dot(cot[...], held(slot))
+
+    def tile_step(m, j, use):
+        slot = lax.rem(j, 2)
+
+        @pl.when(j + 1 < TILES)
         def _():
-            load(1, j, 0).wait()
-            gate_in[:, tile_of(j)] = dot(normed[pl.ds(HALO, BLOCK)], w_in[0])
-
-            @pl.when(j + 1 < TILES)
-            def _():
-                load(1, j + 1, 0).start()
-
-        @pl.when(lax.rem(i, 4) == 2)
-        def _():
-            load(2, j, 1).wait()
-            work[:, tile_of(j)] = dot(cot[...], w_in[1])
-
-            @pl.when(j + 1 < TILES)
-            def _():
-                load(2, j + 1, 1).start()
-
-        forward_slot(2 * TILES + i)
-
-    @pl.loop(2 * TILES + PAIRS, jnp.maximum(2 * TILES + PAIRS, FORWARD_LAG * t + CHUNKS))
-    def _(s):
-        forward_slot(s)
+            load(m, j + 1, 1 - slot).start()
+
+        load(m, j, slot).wait()
+        use(j, slot)
+
+    scan_pairs(0, 8)
+    gather_last(1)
+    scan_pairs(8, 12)
+    gather_last(2)
+    gather_done(1)
+    load(1, 0, 0).start()
+
+    @pl.loop(0, TILES)
+    def _(j):
+        for k in range(2):
+            i = 12 + 2 * j + k
+            forward_slot(4 * TILES + 2 * i)
+            intra_forward(i)
+            forward_slot(4 * TILES + 2 * i + 1)
+        tile_step(1, j, gate_tile)
+
+    base = 4 * TILES + 2 * PAIRS
+    gather_done(2)
+    load(2, 0, 0).start()
+
+    @pl.loop(0, TILES)
+    def _(j):
+        forward_slot(base + j)
+        tile_step(2, j, out_tile)
+
+    base = base + TILES
 
     load(2, 0, 1).start()
     load(1, 0, 0).start()
@@ -557,6 +660,14 @@
 
     @pl.loop(0, TILES)
     def _(j):
+        @pl.loop(0, TILE // CHUNK)
+        def _(k):
+            c = j * (TILE // CHUNK) + k
+
+            @pl.when(c + FORWARD_LAG * t >= base)
+            def _():
+                chain(True, c, update, state, f_out, f_in, f_send, f_recv)
+
         cols = tile_of(j)
         low = state[:, cols].astype(BF16)
         state_low[:, cols] = low
@@ -661,8 +772,9 @@
 
     @pl.loop(0, PAIRS)
     def _(i):
-        backward_slot(i)
+        backward_slot(2 * i)
         intra_backward(i)
+        backward_slot(2 * i + 1)
         j = lax.div(i, 4)
         cols = tile_of(j)
 
@@ -677,7 +789,7 @@
         @pl.when(lax.rem(i, 4) == 2)
         def _():
             load(2, j, 1).wait()
-            mixed_acc[...] += dot(gate_out[:, cols], w_in[1], (1, 1))
+            mixed_acc[...] += dot(gate_out[:, cols], held(1), (1, 1))
 
             @pl.when(j + 1 < TILES)
             def _():
@@ -686,22 +798,26 @@
         @pl.when(lax.rem(i, 4) == 3)
         def _():
             load(1, j, 0).wait()
-            acc[...] += dot(gate_grad[:, cols], w_in[0], (1, 1))
+            acc[...] += dot(gate_grad[:, cols], held(0), (1, 1))
 
             @pl.when(j + 1 < TILES)
             def _():
                 load(1, j + 1, 0).start()
 
-    @pl.loop(PAIRS, jnp.maximum(PAIRS, BACKWARD_LAG * (7 - t) + CHUNKS))
-    def _(s):
-        backward_slot(s)
-
     gs_low = gs[...].astype(BF16)
     grad_bc[:, STATE:] = acc_c[...] + dot(gs_low, bc[:, :STATE])
     acc_c[...] = dot(gs_low, bc[:, STATE:], (0, 0))
 
     @pl.loop(0, TILES)
     def _(j):
+        @pl.loop(0, TILE // CHUNK)
+        def _(k):
+            c = j * (TILE // CHUNK) + k
+
+            @pl.when(c + BACKWARD_LAG * (7 - t) >= 2 * PAIRS)
+            def _():
+                chain(False, c, grad_add, grad_state, b_out, b_in, b_send, b_recv)
+
         cols = tile_of(j)
         wide = widen(weight_ref[...], j)
         grad_update = grad_state[:, cols].astype(BF16)
@@ -736,6 +852,15 @@
     vec_heads[...] = jnp.where(row == 7, acc_heads[2, 1:2], heads)
     mixed[...] = (hidden[...].astype(F32) + mixed_acc[...]).astype(BF16)
 
+    for u in everything:
+        for step in (0, 1):
+            for phase in (0, 1):
+                await_step(u, phase, early(u), step, phase, g_send)
+    for m in range(4):
+        for u in units_with(m):
+            await_partner(u, pl.ds(m % 3, 1), m % 3, core_send)
+            for step in (0, 1):
+                await_step(u, 2, pl.ds(m % 3, 1), step, 2 + m % 3, g_send)
     for slot, ref in ((0, grad_out), (1, grad_gate)):
         for c in put(ref, TILES - 1, slot):
             c.wait()
@@ -761,12 +886,12 @@
     turned, own_state = (HEADS, 1, BLOCK), (STATE, DI)
     blocks = (1, 2, 4, 2, ROWS, DI)
     shapes = [
-        ((BLOCK, D), BF16), ((D, BLOCK), BF16), ((EXT, SMALL), F32), (square, F32), (square, F32), (heads, F32),
+        ((BLOCK, D), BF16), ((8, DI), F32), ((8, 8 * LANES), F32), ((D, BLOCK), BF16), ((EXT, SMALL), F32), (square, F32), (square, F32), (heads, F32),
         ((D, SMALL), BF16), ((BLOCK, D), F32), (wide, F32), ((8, DI), F32), ((8, LANES), F32),
-        ((EXT, DI), F32), (wide, F32), (blocks, BF16), (blocks, BF16),
+        ((EXT, DI), F32), (wide, F32), (blocks, BF16), (blocks, BF16), ((3,) + blocks[1:], BF16),
     ]
     scratch = [
-        ((EXT, D), BF16), ((2, D, TILE), BF16), ((2, EXT, TILE), F32), ((2, BLOCK, TILE), F32), ((2, D, TILE), BF16),
+        ((1, 2, 4, 2, SMALL_ROWS, 8 * LANES), BF16), ((HALO, D), BF16), ((EXT, D), BF16), ((2, 2, 4, 2, ROWS, TILE), BF16), ((2, EXT, TILE), F32), ((2, BLOCK, TILE), F32), ((2, D, TILE), BF16),
         (wide, BF16), ((BLOCK, 2 * STATE), BF16), (square, F32), (wide, F32), (wide, F32), (wide, F32), (wide, BF16),
         (wide, BF16), (wide, BF16), (own_state, F32), (own_state, F32), (own_state, F32), (own_state, BF16),
         (own_state, F32), ((8, DI), F32), (own_state, BF16), (own_state, BF16), (own_state, BF16), (own_state, BF16),
@@ -778,11 +903,14 @@
         mid_kernel,
         name="scan_and_gate",
         out_shape=[jax.ShapeDtypeStruct(*s) for s in shapes],
-        in_specs=[vmem] * 9 + [anywhere],
-        out_specs=[vmem] * 11 + [anywhere] * 4,
+        in_specs=[vmem] * 5 + [anywhere] * 4,
+        out_specs=[vmem] * 13 + [anywhere] * 5,
         scratch_shapes=[VMEM(*s) for s in scratch]
         + [pltpu.SemaphoreType.DMA((2,)), pltpu.SemaphoreType.DMA((2, 16)), pltpu.SemaphoreType.DMA((2, 2))]
-        + [pltpu.SemaphoreType.DMA((CHUNKS,))] * 4,
+        + [pltpu.SemaphoreType.DMA((CHUNKS,))] * 4
+        + [pltpu.SemaphoreType.DMA((len(UNITS), 5, 2))] * 2
+        + [pltpu.SemaphoreType.DMA((len(UNITS), 3))] * 2
+        + [pltpu.SemaphoreType.DMA(s) for s in ((4,), (2,), (2, 7), (2, 7))],
         compiler_params=pltpu.CompilerParams(
             collective_id=1, has_side_effects=True, vmem_limit_bytes=60 * 2**20
         ),
@@ -933,12 +1061,12 @@
         return lambda mat, i, a, b: ref[side, mat, a, b, :, pl.ds(i * width, width)]
 
     def mats_of(u, m):
-        return pl.ds(0, STACK[UNITS[u][0]]) if m is None else pl.ds(index_of(u, m), 1)
+        return pl.ds(index_of(u, m), 1)
 
     def send_step(u, phase, m, step):
         axes = axes_of(u)
         whole, axis = axes[:phase], axes[phase]
-        index = phase if m is None else 2 + m
+        index = 3 * index_of(u, m) + phase
         buf = half_buf[u][phase] if step == 0 else full_buf[u][phase]
         for side, by in ((0, 1), (1, -1)):
             where = moved(at, axis, 2 if step == 0 else by)
@@ -952,7 +1080,7 @@
                 ).start()
 
     def await_step(u, phase, m, step, sem):
-        index = phase if m is None else 2 + m
+        index = 3 * index_of(u, m) + phase
         buf = half_buf[u][phase] if step == 0 else full_buf[u][phase]
         part = buf.at[:, mats_of(u, m)]
         pltpu.make_async_copy(part, part, sem.at[u, index, step]).wait()
@@ -978,6 +1106,20 @@
                 arrived = [from_buf(full_buf[u][2], side, u, 2) for side in (0, 1)]
                 add(u, 2, mats, at, None, [from_own(u, 0)] + arrived)
 
+    def later(m, phase, step):
+        for u in units_of(m):
+            axis, mats = axes_of(u)[phase], [index_of(u, m)]
+            if step == 1:
+                await_step(u, phase, m, 0, recv)
+                for side, by in ((0, 1), (1, -1)):
+                    add(u, phase, mats, moved(at, axis, by), side, [from_buf(half_buf[u][phase], side, u, phase)])
+            elif step == 2:
+                await_step(u, phase, m, 1, recv)
+                arrived = [from_buf(full_buf[u][phase], side, u, phase) for side in (0, 1)]
+                add(u, phase, mats, at, None, arrived, None if phase else outs[UNITS[u][0]])
+            if step < 2:
+                send_step(u, phase, m, step)
+
     def vec_copy(k):
         (x, y, z) = at
         flip = lambda v: v + 1 - 2 * lax.rem(v, 2)
@@ -1028,6 +1170,9 @@
     vec = vec_acc.at[0]
     vec[...] = jnp.zeros(VEC, F32)
 
+    stage(2, 0)
+    prefetch(1, 0)
+
     @pl.when(t < 7)
     def _():
         halo_copy().wait_recv()
@@ -1135,8 +1280,6 @@
         mean = jnp.mean(dn * rows, axis=1, keepdims=True)
         grad_hidden[...] = cot[...].astype(F32) + inv * dn - rows * inv * mean
 
-    stage(2, 0)
-    prefetch(1, 0)
     small_part()
     x_tiles(0, 1)
     stage(1, 0)
@@ -1157,47 +1300,49 @@
     to_partner(0)
     input_tiles(0, 3)
     stage(2, 2)
+    prefetch(0, 0)
+    later(2, 1, 0)
+    input_tiles(3, 6)
+    stage(0, 0)
     prefetch(1, 2)
-    input_tiles(3, 6)
-    stage(1, 2)
-    prefetch(0, 0)
+    later(2, 1, 1)
     input_grad()
     vec_step(0)
-    stage(0, 0)
+    stage(1, 2)
     prefetch(0, 1)
+    later(1, 1, 0)
+    later(2, 1, 2)
+    later(2, 0, 0)
     vec_step(1)
     stage(0, 1)
     prefetch(0, 2)
+    later(1, 1, 1)
+    later(2, 0, 1)
     vec_step(2)
+    later(1, 1, 2)
+    later(1, 0, 0)
+    later(2, 0, 2)
+    vec_step(3)
+    later(1, 0, 1)
     stage(0, 2)
-    vec_step(3)
-    for phase in (1, 0):
-        for u in everything:
-            send_step(u, phase, None, 0)
-        vec_step(4 if phase else 6)
-        for u in everything:
-            axis = axes_of(u)[phase]
-            mats = list(range(STACK[UNITS[u][0]]))
-            await_step(u, phase, None, 0, recv)
-            for side, by in ((0, 1), (1, -1)):
-                add(u, phase, mats, moved(at, axis, by), side, [from_buf(half_buf[u][phase], side, u, phase)])
-            send_step(u, phase, None, 1)
-        vec_step(5 if phase else 7)
-        for u in everything:
-            mats = list(range(STACK[UNITS[u][0]]))
-            await_step(u, phase, None, 1, recv)
-            arrived = [from_buf(full_buf[u][phase], side, u, phase) for side in (0, 1)]
-            add(u, phase, mats, at, None, arrived, None if phase else outs[UNITS[u][0]])
+    later(0, 1, 0)
+    vec_step(4)
+    later(1, 0, 2)
+    later(0, 1, 1)
+    vec_step(5)
+    later(0, 1, 2)
+    later(0, 0, 0)
+    vec_step(6)
+    later(0, 0, 1)
+    vec_step(7)
+    later(0, 0, 2)
     for m in MATS:
         for u in units_of(m):
             part = other[UNITS[u][0]].at[pl.ds(0, 1), :, :, pl.ds(0, 32)]
             pltpu.make_async_copy(part, part, core_send.at[u, m]).wait()
-            for step in (0, 1):
-                await_step(u, 2, m, step, send)
-    for u in everything:
-        for phase in (0, 1):
-            for step in (0, 1):
-                await_step(u, phase, None, step, send)
+            for phase in range(3):
+                for step in (0, 1):
+                    await_step(u, phase, m, step, send)
     for k in range(VEC_STEPS):
         vec_copy(k).wait_send()
 
@@ -1238,7 +1383,7 @@
         + [
             pltpu.SemaphoreType.DMA(s)
             for s in (
-                (3, 2), (2,), (2,), (2,), (2, 16), (16,), (n, 2, 2), (VEC_STEPS,), (VEC_STEPS,), (n, 5, 2), (n, 5, 2),
+                (3, 2), (2,), (2,), (2,), (2, 16), (16,), (n, 2, 2), (VEC_STEPS,), (VEC_STEPS,), (n, 9, 2), (n, 9, 2),
                 (n, 3), (n, 3, 3),
             )
         ],
@@ -1264,50 +1409,19 @@
     out_proj,
     cotangent,
 ):
-    t = lax.axis_index("tensor")
-    shards = jnp.stack([main_proj[:, 1], main_proj[:, 0], out_proj])
-    small = jnp.concatenate([state_proj, step_proj], axis=1).reshape(3, SMALL_ROWS, 38)
-    small = jnp.pad(small.transpose(1, 0, 2).reshape(SMALL_ROWS, 114), ((0, 0), (0, 14)))[None]
-    params = pack_params(
-        conv_main, conv_main_bias, conv_state, conv_state_bias, step_bias, decay_log, skip_gain, gate_gain
+    shards, small, pmain, phead, doc_col, doc_row, gain = pack(
+        main_proj, out_proj, state_proj, step_proj, conv_main, conv_main_bias, conv_state, conv_state_bias, step_bias,
+        decay_log, skip_gain, gate_gain, norm_gain, doc_ids,
     )
-    full, packed, halo, pmain, phead = gather_weights(shards, small, hidden[BLOCK - HALO :], params)
-    full, packed = full.reshape(3, D, DI), packed.reshape(512, 8 * LANES)
-    gain = norm_gain[None]
-
-    docs_all = jnp.concatenate([jnp.full((HALO,), -1, jnp.int32), doc_ids, jnp.full((16,), -2, jnp.int32)])
-    docs = lax.dynamic_slice(docs_all, (t * BLOCK,), (EXT + 16,))
-    doc_col, doc_row = docs[:, None], docs[None, HALO:EXT]
-
-    (mixed, normed_t, raw, state_pre, grad_bc, grad_step_in, w_small, acc, grad_x, vec_gate, vec_heads, x_ext, x_pre,
-     grad_out, grad_gate) = mid(
-        hidden, halo, gain, packed, pmain, phead, doc_col, doc_row, cotangent, full
+    (mixed, pmain, phead, normed_t, raw, state_pre, grad_bc, grad_step_in, w_small, acc, grad_x, vec_gate, vec_heads,
+     x_ext, x_pre, grad_out, grad_gate, full) = mid(
+        hidden, gain, doc_col, doc_row, cotangent, shards, small, pmain, phead
     )
     _, _, own_main, own_small, grad_hidden, vec = back(
         normed_t, raw, state_pre, grad_bc, grad_step_in, w_small, acc, pmain, phead, doc_col, hidden, cotangent,
-        gain, vec_gate, vec_heads, x_ext, x_pre, grad_x, grad_gate, grad_out, full,
+        gain, vec_gate, vec_heads, x_ext, x_pre, grad_x, grad_gate, grad_out, full.reshape(3, D, DI),
     )
-    own_small = own_small[0, :, :114].reshape(SMALL_ROWS, 3, 38).transpose(1, 0, 2).reshape(ROWS, 38)
-    vec_main = lax.dynamic_slice(vec, (0, t * WIDTH), (8, WIDTH))
-    vec_state = lax.dynamic_slice(vec, (0, DI + t * 32), (5, 32))
-    vec_head = lax.dynamic_slice(vec, (5, DI + 256 + t * 6), (3, 6))
-    return (
-        mixed,
-        grad_hidden,
-        vec[6, :D],
-        jnp.stack([own_main[1], own_main[0]], axis=1),
-        own_small[:, 32:],
-        own_small[:, :32],
-        vec_main[:TAPS],
-        vec_main[TAPS],
-        vec_state[:TAPS],
-        vec_state[TAPS],
-        vec_head[0],
-        vec_head[1],
-        vec_head[2],
-        vec_main[5],
-        own_main[2],
-    )
+    return (mixed, grad_hidden, *finish(own_main, own_small, vec))
 
 
 def solution(mesh):

time: 312 us -> 290 us (0.929)
  local copies, waits for them, and re-layouts: 24.9 us -> 7.76 us
  Pallas kernels: 282 us -> 276 us
    pallas_call x1 -> x2, Pallas kernels: 80.1 us -> 4.39 us  [the longest x1 2.32 us: pack(): pl.pallas_call(pack_kernel, name='pack', out_shape=[jax.ShapeDtypeStruct(...]
    pallas_call x1, Pallas kernels: 114 us -> 183 us  [mid(): pl.pallas_call(mid_kernel, name='scan_and_gate', out_shape=[jax.ShapeDtyp...]
    slice x8 -> x0, local copies, waits for them, and re-layouts: 8.24 us -> none  [the longest x1 1.54 us: per_device(): vec[6, :D]]
    broadcast_in_dim x7 -> x0, local copies, waits for them, and re-layouts: 4.76 us -> none  [the longest x1 1.3 us: per_device(): gain = norm_gain[None]]
    pallas_call x0 -> x3, other arithmetic: none -> 3.86 us  [finish(): pl.pallas_call(finish_kernel, name='finish', out_shape=[jax.ShapeDtypeStr...]
    unnamed x9 -> x10, local copies, waits for them, and re-layouts: 4.33 us -> 7.76 us
where the time goes in v4:
time: 290 us; the launch traced here: 289 us
  Pallas kernels  276 us (95%)
  local copies, waits for them, and re-layouts  7.76 us (3%)
  other arithmetic  3.86 us (1%)
    pallas_call x1, Pallas kernels, mid(): pl.pallas_call(mid_kernel, name='scan_and_gate', out_shape=[jax.ShapeDtyp...  183 us
    pallas_call x1, Pallas kernels, back(): pl.pallas_call(back_kernel, name='project_back', out_shape=[jax.ShapeDtyp...  89.1 us
    unnamed x10, local copies, waits for them, and re-layouts  7.76 us

profile of v4, /device:TPU:0, one launch (start us, length us, event | category | flops | bytes accessed | tf_op | source)
XLA Modules:
  0.0 288.7 jit_solution(5562319864798327096)
XLA Ops:
  0.6 1.4 copy.32.step_proj
  2.0 1.4 copy.31.state_proj
  3.4 2.3 pack.1
  5.8 182.9 %scan_and_gate.1 = (bf16[256,1536]{1,0:T(8,128)(2,1)}, f32[8,3072]{1,0:T(8,128)}, f32[8,1024]{1,0:T(8,128)}, bf16[1536,256]{1,0:T(8,128)(2,1)}, f32[272,384]{1,0...) custom-call(bf16[256,1536]{1,0:T(8,128)(2,1)} %refs_10_.1, ...), custom_call_target="tpu_custom_call" | custom-call | tf_op jit(solution)/shard_map/scan_and_gate/pallas_call | solution.py:902
  188.6 0.0 copy-start.1
  188.6 89.1 %project_back.1 = (bf16[1,2,4,2,96,3072]{5,4,3,2,1,0:T(8,128)(2,1)}, bf16[1,2,4,2,32,1024]{5,4,3,2,1,0:T(8,128)(2,1)}, f32[3,96,384]{2,1,0:T(8,128)}, f32[1,32,1...) custom-call(bf16[1536,256]{1,0:T(8,128)(2,1)} %get-tuple-element.65.refs_0_, ...), custom_call_target="tpu_custom_call" | custom-call | tf_op jit(solution)/shard_map/project_back/pallas_call | solution.py:1361
  277.8 0.0 copy-start
  277.8 2.1 finish.1
  279.9 1.3 reduce
  281.2 1.3 reduce.1
  282.5 1.3 reduce.2
  283.7 1.5 copy.33
  285.2 1.5 copy.34
  286.7 0.0 copy-done.1
  286.7 0.9 copy.37
  287.6 0.0 copy-done
  287.6 1.1 copy.38
Async XLA Ops:
  188.6 98.1 %copy-start.1 = (bf16[256,1536]{1,0:T(8,128)(2,1)S(1)}, bf16[256,1536]{1,0:T(8,128)(2,1)}, u32[]{:S(2)}) copy-start(bf16[256,1536]{1,0:T(8,128)(2,1)} %get-tuple-element.129) | copy-start | bytes 2359300
  277.8 9.8 %copy-start = (f32[256,1536]{1,0:T(8,128)S(1)}, f32[256,1536]{1,0:T(8,128)}, u32[]{:S(2)}) copy-start(f32[256,1536]{1,0:T(8,128)} %get-tuple-element.130) | copy-start | bytes 4718596

commit v5 on v4

--- a/solution.py
+++ b/solution.py
@@ -66,6 +66,7 @@
 
 ROWS, WIDTH, SMALL_ROWS, SMALL_WIDTH = 96, 384, 32, 128
 UNITS = [(0, q * 32, q) for q in range(3)] + [(1, 0, 0)]
+SUMMED = len(UNITS)
 WIDTHS = [WIDTH, SMALL_WIDTH]
 STACK = [3, 1]
 
@@ -230,7 +231,8 @@
     shards[0] = main_proj[:, 1, :]
     shards[1] = main_proj[:, 0, :]
     shards[2] = out_proj[...]
-    lanes = [jnp.concatenate([state_proj[...], step_proj[...]], 1)[r * 32 : r * 32 + 32] for r in range(3)]
+    both = jnp.concatenate([state_proj[...].T, step_proj[...].T], 1)
+    lanes = [both[r * 32 : r * 32 + 32] for r in range(3)]
     small[0] = jnp.concatenate(lanes + [jnp.zeros((SMALL_ROWS, 14), BF16)], 1)
     pmain[0:TAPS] = conv_main[...]
     pmain[TAPS : TAPS + 1] = conv_main_bias[...].reshape(1, WIDTH)
@@ -280,28 +282,28 @@
     out_proj[...] = own_main[2]
     packed = own_small[0]
     for r in range(3):
-        rows = pl.ds(r * 32, 32)
-        state_proj[rows] = packed[:, r * 38 : r * 38 + 32]
-        step_proj[rows] = packed[:, r * 38 + 32 : r * 38 + 38]
+        rows_t = packed[:, r * 38 : r * 38 + 38].T
+        state_proj[:, r * 32 : r * 32 + 32] = rows_t[:32]
+        step_proj[:, r * 32 : r * 32 + 32] = rows_t[32:]
     own = vec[:, pl.ds(pl.multiple_of(t * WIDTH, LANES), WIDTH)]
     conv_main[...] = own[:TAPS]
-    conv_main_bias[...] = own[TAPS : TAPS + 1]
-    gate_gain[...] = own[5:6]
+    conv_main_bias[...] = own[TAPS : TAPS + 1].reshape(WIDTH)
+    gate_gain[...] = own[5:6].reshape(WIDTH)
     state = pltpu.roll(vec[:, DI : DI + 256], lax.rem(256 - 32 * t, 256), axis=1)
     conv_state[...] = state[:TAPS, :32]
-    conv_state_bias[...] = state[TAPS : TAPS + 1, :32]
+    conv_state_bias[...] = state[TAPS : TAPS + 1, :32].reshape(32)
     heads = pltpu.roll(vec[:, DI + 256 :], lax.rem(LANES - 6 * t, LANES), axis=1)
-    step_bias[...] = heads[5:6, :6]
-    decay_log[...] = heads[6:7, :6]
-    skip_gain[...] = heads[7:8, :6]
-    norm_gain[...] = vec[6:7, 0:D]
+    step_bias[...] = heads[5:6, :6].reshape(6)
+    decay_log[...] = heads[6:7, :6].reshape(6)
+    skip_gain[...] = heads[7:8, :6].reshape(6)
+    norm_gain[...] = vec[6:7, 0:D].reshape(D)
 
 
 def finish(*args):
     vmem = pl.BlockSpec(memory_space=VMEM)
     shapes = [
-        (1, D), (ROWS, 2, WIDTH), (ROWS, 6), (ROWS, 32), (TAPS, WIDTH), (1, WIDTH), (TAPS, 32), (1, 32), (1, 6), (1, 6),
-        (1, 6), (1, WIDTH), (ROWS, WIDTH),
+        (D,), (ROWS, 2, WIDTH), (6, ROWS), (32, ROWS), (TAPS, WIDTH), (WIDTH,), (TAPS, 32), (32,), (6,), (6,), (6,),
+        (WIDTH,), (ROWS, WIDTH),
     ]
     outs = pl.pallas_call(
         finish_kernel,
@@ -310,7 +312,7 @@
         in_specs=[vmem] * 3,
         out_specs=[vmem] * len(shapes),
     )(*args)
-    return [v[0] if v.shape[0] == 1 else v for v in outs]
+    return [v.T if i in (2, 3) else v for i, v in enumerate(outs)]
 
 
 PAIR = 2 * HEAD_DIM
@@ -318,7 +320,7 @@
 HALF = BLOCK // 2
 CHUNK = 128
 CHUNKS = DI // CHUNK
-FORWARD_LAG, BACKWARD_LAG = 7, 4
+FORWARD_LAG, BACKWARD_LAG = 10, 4
 
 
 def pair_of(p):
@@ -340,13 +342,13 @@
 
 def mid_kernel(
     hidden, gain, doc_col, doc_row, cot, shards, small, pmain_own, phead_own,
-    mixed, pmain, phead, normed_t, raw, state_pre, grad_bc, grad_step_in, w_small, acc, grad_x, vec_gate, vec_heads,
-    x_ext, x_pre, grad_out, grad_gate, full,
-    packed, halo, normed, w_in, ext_out, pre_out, staged, x_act, bc, scores, gate_in, work, y, gate_out, dy, gate_grad, update,
+    pmain, phead, raw, state_pre, grad_bc, grad_step_in, vec_gate, vec_heads,
+    mixed_out, normed_out, w_small_out, acc_out, grad_x_out, x_ext, x_pre, grad_out, grad_gate, full,
+    mixed, normed_t, w_small, acc, grad_x, packed, halo, normed, w_in, ext_out, pre_out, staged, x_act, bc, scores, gate_in, work, y, gate_out, dy, gate_grad, update,
     grad_add, state, state_low, grad_state, keep_row, f_out, f_in, b_out, b_in, cot_t, mixed_acc,
     barred, cum2, cum_t, step_t, step_in, enter_ref, weight_ref, rows_acc, q_t, gs, acc_c, acc_heads, row_acc,
     w_sem, put_sem, x_sem, f_send, f_recv, b_send, b_recv, g_send, g_recv, core_send, core_recv, own_sem, halo_sem,
-    param_send, param_recv,
+    param_send, param_recv, out_sem,
 ):
     t = lax.axis_index("tensor")
 
@@ -391,69 +393,85 @@
 
     everything = [3, 0, 1, 2]
 
-    def early(u):
-        return pl.ds(0, STACK[UNITS[u][0]])
-
     def rms(rows, part):
         value = part[...].astype(F32)
         inv = lax.rsqrt(jnp.mean(value * value, axis=1, keepdims=True) + epsilon)
         normed[rows] = (value * inv * gain[...]).astype(BF16)
 
+    def units_with(m):
+        return [3] if m == 3 else MAIN_UNITS
+
+    def gather_first(m):
+        for u in units_with(m):
+            sends(u, 2, pl.ds(m % 3, 1), 0, 2 + m % 3)
+
+    def gather_near(m):
+        for u in units_with(m):
+            to_partner(u, pl.ds(m % 3, 1), [0], m % 3)
+
+    def gather_forward(m):
+        for u in units_with(m):
+            await_step(u, 2, pl.ds(m % 3, 1), 0, 2 + m % 3, g_recv)
+            sends(u, 2, pl.ds(m % 3, 1), 1, 2 + m % 3)
+
+    def gather_second(m):
+        for u in units_with(m):
+            to_partner(u, pl.ds(m % 3, 1), [-1, 1], m % 3)
+
+    def gather_last(m):
+        for u in units_with(m):
+            await_step(u, 2, pl.ds(m % 3, 1), 1, 2 + m % 3, g_recv)
+            to_partner(u, pl.ds(m % 3, 1), [2], m % 3)
+
+    def gather_done(m):
+        for u in units_with(m):
+            await_partner(u, pl.ds(m % 3, 1), m % 3, core_recv)
+
+    one, others = pl.ds(0, 1), pl.ds(1, 2)
     for c in own:
         c.wait()
     for u in everything:
-        sends(u, 0, early(u), 0, 0)
+        sends(u, 0, one, 0, 0)
     halo_copy().start()
     for by in range(1, 8):
         for i in range(2):
             param_copy(by, i, t).start()
+    for u in MAIN_UNITS:
+        sends(u, 0, others, 0, 5)
     rms(pl.ds(HALO, BLOCK), hidden)
-    for phase in (0, 1):
-        for u in everything:
-            await_step(u, phase, early(u), 0, phase, g_recv)
-            sends(u, phase, early(u), 1, phase)
-        if phase == 0:
-            cot_t[...] = cot[...].T
-        else:
-            normed_t[...] = normed[pl.ds(HALO, BLOCK)].T
-        for u in everything:
-            await_step(u, phase, early(u), 1, phase, g_recv)
-            if phase == 0:
-                sends(u, 1, early(u), 0, 1)
-
-    def units_with(m):
-        return [3] if m == 3 else MAIN_UNITS
-
-    def gather_first(m):
-        for u in units_with(m):
-            sends(u, 2, pl.ds(m % 3, 1), 0, 2 + m % 3)
-
-    def gather_near(m):
-        for u in units_with(m):
-            to_partner(u, pl.ds(m % 3, 1), [0], m % 3)
-
-    def gather_forward(m):
-        for u in units_with(m):
-            await_step(u, 2, pl.ds(m % 3, 1), 0, 2 + m % 3, g_recv)
-            sends(u, 2, pl.ds(m % 3, 1), 1, 2 + m % 3)
-
-    def gather_second(m):
-        for u in units_with(m):
-            to_partner(u, pl.ds(m % 3, 1), [-1, 1], m % 3)
-
-    def gather_last(m):
-        for u in units_with(m):
-            await_step(u, 2, pl.ds(m % 3, 1), 1, 2 + m % 3, g_recv)
-            to_partner(u, pl.ds(m % 3, 1), [2], m % 3)
-
-    def gather_done(m):
-        for u in units_with(m):
-            await_partner(u, pl.ds(m % 3, 1), m % 3, core_recv)
-
-    gather_first(3)
-    gather_first(0)
+    for u in everything:
+        await_step(u, 0, one, 0, 0, g_recv)
+        sends(u, 0, one, 1, 0)
+    for u in everything:
+        await_step(u, 0, one, 1, 0, g_recv)
+        sends(u, 1, one, 0, 1)
+    for u in MAIN_UNITS:
+        await_step(u, 0, others, 0, 5, g_recv)
+        sends(u, 0, others, 1, 5)
+    cot_t[...] = cot[...].T
+    for u in everything:
+        await_step(u, 1, one, 0, 1, g_recv)
+        sends(u, 1, one, 1, 1)
+    normed_t[...] = normed[pl.ds(HALO, BLOCK)].T
+    leaving = [
+        pltpu.make_async_copy(src, dst, out_sem.at[i])
+        for i, (src, dst) in enumerate(
+            ((normed_t, normed_out), (w_small, w_small_out), (acc, acc_out), (mixed, mixed_out))
+        )
+    ]
+    leaving[0].start()
+
+    def grad_x_put(j):
+        return pltpu.make_async_copy(grad_x.at[:, tile_of(j)], grad_x_out.at[:, tile_of(j)], out_sem.at[4 + j])
+
+    for u in everything:
+        await_step(u, 1, one, 1, 1, g_recv)
+        sends(u, 2, one, 0, 2)
     gather_near(3)
     gather_near(0)
+    for u in MAIN_UNITS:
+        await_step(u, 0, others, 1, 5, g_recv)
+        sends(u, 1, others, 0, 6)
     halo_copy().wait()
     rms(pl.ds(0, HALO), halo)
     for by in range(1, 8):
@@ -461,11 +479,12 @@
             param_copy(by, i, lax.rem(t + 8 - by, 8)).wait()
     gather_forward(3)
     gather_second(3)
+    gather_forward(0)
+    gather_second(0)
+    for u in MAIN_UNITS:
+        await_step(u, 1, others, 0, 6, g_recv)
+        sends(u, 1, others, 1, 6)
     gather_last(3)
-    gather_forward(0)
-    gather_first(1)
-    gather_first(2)
-    gather_second(0)
     gather_done(3)
 
     for r in range(3):
@@ -473,6 +492,11 @@
         for d in range(16):
             w_small[pl.ds(d * 96 + r * 32, 32)] = rows[d * 32 : d * 32 + 32]
     raw[...] = dot(normed[...], w_small[...])
+    leaving[1].start()
+    for u in MAIN_UNITS:
+        await_step(u, 1, others, 1, 6, g_recv)
+        sends(u, 2, pl.ds(1, 1), 0, 3)
+    gather_first(2)
     params = small_params(phead[...])
     docs = doc_col[...]
     links = [None] + [conv_links(docs, o, BLOCK) for o in range(1, TAPS)]
@@ -804,6 +828,9 @@
             def _():
                 load(1, j + 1, 0).start()
 
+    leaving[2].start()
+    mixed[...] = (hidden[...].astype(F32) + mixed_acc[...]).astype(BF16)
+    leaving[3].start()
     gs_low = gs[...].astype(BF16)
     grad_bc[:, STATE:] = acc_c[...] + dot(gs_low, bc[:, :STATE])
     acc_c[...] = dot(gs_low, bc[:, STATE:], (0, 0))
@@ -824,6 +851,7 @@
         spread_grad = dot(bc[:, :STATE], grad_update)
         x, grad = x_act[:, cols].astype(F32), dy[:, cols].astype(F32)
         grad_x[:, cols] += wide * spread_grad + pmain[6:7, cols] * grad
+        grad_x_put(j).start()
         acc_heads[1] += by_head(x * spread_grad, j)
         acc_c[...] += dot((x * wide).astype(BF16), grad_update, (1, 1))
         kept = jnp.sum(grad_state[:, cols] * state[:, cols], axis=0, keepdims=True)
@@ -850,12 +878,17 @@
     heads = jnp.where(row == 5, jnp.sum(grad_in, axis=0, keepdims=True), 0.0)
     heads = jnp.where(row == 6, rate * jnp.sum(grad_log * step, axis=0, keepdims=True), heads)
     vec_heads[...] = jnp.where(row == 7, acc_heads[2, 1:2], heads)
-    mixed[...] = (hidden[...].astype(F32) + mixed_acc[...]).astype(BF16)
-
+
+    for c in leaving:
+        c.wait()
+    for j in range(TILES):
+        grad_x_put(j).wait()
     for u in everything:
         for step in (0, 1):
             for phase in (0, 1):
-                await_step(u, phase, early(u), step, phase, g_send)
+                await_step(u, phase, one, step, phase, g_send)
+                if u in MAIN_UNITS:
+                    await_step(u, phase, others, step, 5 + phase, g_send)
     for m in range(4):
         for u in units_with(m):
             await_partner(u, pl.ds(m % 3, 1), m % 3, core_send)
@@ -886,10 +919,11 @@
     turned, own_state = (HEADS, 1, BLOCK), (STATE, DI)
     blocks = (1, 2, 4, 2, ROWS, DI)
     shapes = [
-        ((BLOCK, D), BF16), ((8, DI), F32), ((8, 8 * LANES), F32), ((D, BLOCK), BF16), ((EXT, SMALL), F32), (square, F32), (square, F32), (heads, F32),
-        ((D, SMALL), BF16), ((BLOCK, D), F32), (wide, F32), ((8, DI), F32), ((8, LANES), F32),
-        ((EXT, DI), F32), (wide, F32), (blocks, BF16), (blocks, BF16), ((3,) + blocks[1:], BF16),
+        ((8, DI), F32), ((8, 8 * LANES), F32), ((EXT, SMALL), F32), (square, F32), (square, F32), (heads, F32),
+        ((8, DI), F32), ((8, LANES), F32),
     ]
+    moved_out = [((BLOCK, D), BF16), ((D, BLOCK), BF16), ((D, SMALL), BF16), ((BLOCK, D), F32), (wide, F32)]
+    in_hbm = [((EXT, DI), F32), (wide, F32), (blocks, BF16), (blocks, BF16), ((3,) + blocks[1:], BF16)]
     scratch = [
         ((1, 2, 4, 2, SMALL_ROWS, 8 * LANES), BF16), ((HALO, D), BF16), ((EXT, D), BF16), ((2, 2, 4, 2, ROWS, TILE), BF16), ((2, EXT, TILE), F32), ((2, BLOCK, TILE), F32), ((2, D, TILE), BF16),
         (wide, BF16), ((BLOCK, 2 * STATE), BF16), (square, F32), (wide, F32), (wide, F32), (wide, F32), (wide, BF16),
@@ -902,15 +936,15 @@
     return pl.pallas_call(
         mid_kernel,
         name="scan_and_gate",
-        out_shape=[jax.ShapeDtypeStruct(*s) for s in shapes],
+        out_shape=[jax.ShapeDtypeStruct(*s) for s in shapes + moved_out + in_hbm],
         in_specs=[vmem] * 5 + [anywhere] * 4,
-        out_specs=[vmem] * 13 + [anywhere] * 5,
-        scratch_shapes=[VMEM(*s) for s in scratch]
+        out_specs=[vmem] * 8 + [anywhere] * 10,
+        scratch_shapes=[VMEM(*s) for s in moved_out + scratch]
         + [pltpu.SemaphoreType.DMA((2,)), pltpu.SemaphoreType.DMA((2, 16)), pltpu.SemaphoreType.DMA((2, 2))]
         + [pltpu.SemaphoreType.DMA((CHUNKS,))] * 4
-        + [pltpu.SemaphoreType.DMA((len(UNITS), 5, 2))] * 2
+        + [pltpu.SemaphoreType.DMA((len(UNITS), 7, 2))] * 2
         + [pltpu.SemaphoreType.DMA((len(UNITS), 3))] * 2
-        + [pltpu.SemaphoreType.DMA(s) for s in ((4,), (2,), (2, 7), (2, 7))],
+        + [pltpu.SemaphoreType.DMA(s) for s in ((4,), (2,), (2, 7), (2, 7), (4 + TILES,))],
         compiler_params=pltpu.CompilerParams(
             collective_id=1, has_side_effects=True, vmem_limit_bytes=60 * 2**20
         ),
@@ -939,19 +973,19 @@
         del refs[:n]
         return got
 
-    (normed_t, raw_ext, state_pre, grad_bc, grad_step_in, w_small, acc_in, pmain, phead, doc_col, hidden, cot, gain,
-     vec_gate, vec_heads, x_ext, x_pre, grad_x, grad_gate, grad_out, full) = take(21)
+    (raw_ext, state_pre, grad_bc, grad_step_in, pmain, phead, doc_col, gain, vec_gate, vec_heads,
+     normed_in, w_small_in, acc_in, hidden_in, cot_in, x_ext, x_pre, grad_x, grad_gate, grad_out, full) = take(21)
     grad_main, grad_small, out_main, out_small, grad_hidden, vec_out = take(6)
     outs = (out_main, out_small)
-    units = len(UNITS)
+    units = SUMMED
     other = take(2)
     half_buf = [take(3) for _ in range(units)]
     full_buf = [take(3) for _ in range(units)]
     own = take(units)
     (ext_in, pre_in, grad_in, first_grad, first_pre, first_out, after, w_in, staged, raw_x, acc, small_acc,
-     small_out, vec_acc, vec_in) = take(15)
+     small_out, vec_acc, vec_in, normed_t, w_small, hidden, cot) = take(19)
     (stream_sem, first_sem, halo_sem, w_sem, put_sem, small_sem, own_sem, vec_send, vec_recv, send, recv, core_send,
-     core_recv) = take(13)
+     core_recv, entry_sem) = take(14)
     at, core = coordinates()
     t = lax.axis_index("tensor")
     everything = range(units)
@@ -967,7 +1001,13 @@
         pltpu.make_async_copy(src.at[pl.ds(0, 8)], dst, first_sem.at[i])
         for i, (src, dst) in enumerate(((grad_x, first_grad), (x_pre, first_pre)))
     ]
-    for c in firsts + stream(0, 0):
+    entering = [
+        pltpu.make_async_copy(src, dst, entry_sem.at[i])
+        for i, (src, dst) in enumerate(
+            ((normed_in, normed_t), (w_small_in, w_small), (acc_in, acc), (hidden_in, hidden), (cot_in, cot))
+        )
+    ]
+    for c in firsts + stream(0, 0) + entering:
         c.start()
     greet(at, core, [device(moved(at, axis, 2), core) for axis in AXES] + [tensor_peer(1), tensor_peer(7)])
 
@@ -1238,7 +1278,7 @@
         for i, row in enumerate(rows):
             vec[i : i + 1, DI : DI + 256] = row
         raw = jnp.concatenate([total.astype(BF16), grad_step_in[...].astype(BF16)], 1)
-        acc[...] = acc_in[...] + dot(raw, w_small[...], (1, 1))
+        acc[...] += dot(raw, w_small[...], (1, 1))
         small_acc[...] = dot(normed_t[...], raw).astype(BF16)
         packed = jnp.zeros((512, 8 * LANES), F32)
         for r in range(3):
@@ -1280,6 +1320,8 @@
         mean = jnp.mean(dn * rows, axis=1, keepdims=True)
         grad_hidden[...] = cot[...].astype(F32) + inv * dn - rows * inv * mean
 
+    for c in entering:
+        c.wait()
     small_part()
     x_tiles(0, 1)
     stage(1, 0)
@@ -1354,8 +1396,8 @@
 def back(*args):
     vmem = pl.BlockSpec(memory_space=VMEM)
     anywhere = pl.BlockSpec(memory_space=pl.ANY)
-    units = range(len(UNITS))
-    n = len(UNITS)
+    units = range(SUMMED)
+    n = SUMMED
     held = [(3, 2, 4, ROWS, 8 * WIDTH), (1, 2, 4, SMALL_ROWS, 8 * SMALL_WIDTH)]
     landing = [(2, STACK[UNITS[u][0]]) + region_shape(u, p, rows) for rows in (16, 32) for u in units for p in range(3)]
     return pl.pallas_call(
@@ -1369,7 +1411,7 @@
             jax.ShapeDtypeStruct((BLOCK, D), F32),
             jax.ShapeDtypeStruct(VEC, F32),
         ],
-        in_specs=[vmem] * 15 + [anywhere] * 6,
+        in_specs=[vmem] * 10 + [anywhere] * 11,
         out_specs=[anywhere, anywhere, vmem, vmem, vmem, vmem],
         scratch_shapes=[VMEM(s, BF16) for s in held + landing]
         + [VMEM((2,) + region_shape(u, 2, 32), BF16) for u in units]
@@ -1379,12 +1421,13 @@
             VMEM((2, D, TILE), BF16), VMEM((2, D, TILE), BF16), VMEM((BLOCK, DI), BF16),
             VMEM((BLOCK, D), F32), VMEM((D, SMALL), BF16), VMEM((512, 8 * LANES), BF16),
             VMEM((VEC_STEPS + 1,) + VEC, F32), VMEM((VEC_STEPS,) + VEC, F32),
+            VMEM((D, BLOCK), BF16), VMEM((D, SMALL), BF16), VMEM((BLOCK, D), BF16), VMEM((BLOCK, D), BF16),
         ]
         + [
             pltpu.SemaphoreType.DMA(s)
             for s in (
                 (3, 2), (2,), (2,), (2,), (2, 16), (16,), (n, 2, 2), (VEC_STEPS,), (VEC_STEPS,), (n, 9, 2), (n, 9, 2),
-                (n, 3), (n, 3, 3),
+                (n, 3), (n, 3, 3), (5,),
             )
         ],
         compiler_params=pltpu.CompilerParams(collective_id=3, has_side_effects=True, vmem_limit_bytes=62 * 2**20),
@@ -1410,16 +1453,16 @@
     cotangent,
 ):
     shards, small, pmain, phead, doc_col, doc_row, gain = pack(
-        main_proj, out_proj, state_proj, step_proj, conv_main, conv_main_bias, conv_state, conv_state_bias, step_bias,
+        main_proj, out_proj, state_proj.T, step_proj.T, conv_main, conv_main_bias, conv_state, conv_state_bias, step_bias,
         decay_log, skip_gain, gate_gain, norm_gain, doc_ids,
     )
-    (mixed, pmain, phead, normed_t, raw, state_pre, grad_bc, grad_step_in, w_small, acc, grad_x, vec_gate, vec_heads,
+    (pmain, phead, raw, state_pre, grad_bc, grad_step_in, vec_gate, vec_heads, mixed, normed_t, w_small, acc, grad_x,
      x_ext, x_pre, grad_out, grad_gate, full) = mid(
         hidden, gain, doc_col, doc_row, cotangent, shards, small, pmain, phead
     )
     _, _, own_main, own_small, grad_hidden, vec = back(
-        normed_t, raw, state_pre, grad_bc, grad_step_in, w_small, acc, pmain, phead, doc_col, hidden, cotangent,
-        gain, vec_gate, vec_heads, x_ext, x_pre, grad_x, grad_gate, grad_out, full.reshape(3, D, DI),
+        raw, state_pre, grad_bc, grad_step_in, pmain, phead, doc_col, gain, vec_gate, vec_heads,
+        normed_t, w_small, acc, hidden, cotangent, x_ext, x_pre, grad_x, grad_gate, grad_out, full.reshape(3, D, DI),
     )
     return (mixed, grad_hidden, *finish(own_main, own_small, vec))
 

time: 290 us -> 272 us (0.938)
  Pallas kernels: 276 us -> 269 us
  local copies, waits for them, and re-layouts: 7.76 us -> 2.03 us
  other arithmetic: 3.86 us -> 0 us
    pallas_call x1, Pallas kernels: 183 us -> 177 us  [mid(): pl.pallas_call(mid_kernel, name='scan_and_gate', out_shape=[jax.ShapeDtyp...]
    unnamed x10 -> x6, local copies, waits for them, and re-layouts: 7.76 us -> 2.03 us
    pallas_call x3 -> x0, other arithmetic: 3.86 us -> none  [finish(): pl.pallas_call(finish_kernel, name='finish', out_shape=[jax.ShapeDtypeStr...]
where the time goes in v5:
time: 272 us; the launch traced here: 271 us
  Pallas kernels  269 us (99%)
    pallas_call x1, Pallas kernels, mid(): pl.pallas_call(mid_kernel, name='scan_and_gate', out_shape=[jax.ShapeDtyp...  177 us
    pallas_call x1, Pallas kernels, back(): pl.pallas_call(back_kernel, name='project_back', out_shape=[jax.ShapeDtyp...  87.5 us

profile of v5, /device:TPU:0, one launch (start us, length us, event | category | flops | bytes accessed | tf_op | source)
XLA Modules:
  0.0 271.4 jit_solution(4530500317208579309)
XLA Ops:
  0.7 2.4 pack.1
  3.0 176.6 %scan_and_gate.1 = (f32[8,3072]{1,0:T(8,128)}, f32[8,1024]{1,0:T(8,128)}, f32[272,384]{1,0:T(8,128)}, f32[256,256]{1,0:T(8,128)}, f32[256,256]{1,0:T(8,128)}, /*...) custom-call(bf16[256,1536]{1,0:T(8,128)(2,1)} %refs_13_.1, ...), custom_call_target="tpu_custom_call" | custom-call | tf_op jit(solution)/shard_map/scan_and_gate/pallas_call | solution.py:936
  179.6 0.0 copy-start.1
  179.7 87.5 %project_back.1 = (bf16[1,2,4,2,96,3072]{5,4,3,2,1,0:T(8,128)(2,1)}, bf16[1,2,4,2,32,1024]{5,4,3,2,1,0:T(8,128)(2,1)}, f32[3,96,384]{2,1,0:T(8,128)}, f32[1,32,1...) custom-call(f32[272,384]{1,0:T(8,128)} %get-tuple-element.65.refs_0_, f32[256,256]{1,0:T(8,128)} %get-tuple-element.66.refs_1_, ...), custom_call_target="tpu_custom_call" | custom-call | tf_op jit(solution)/shard_map/project_back/pallas_call | solution.py:1403
  267.2 0.0 copy-start
  267.2 2.1 finish.1
  269.3 0.0 copy-done.1
  269.3 0.9 copy.33
  270.2 0.0 copy-done
  270.2 1.1 copy.34
Async XLA Ops:
  179.6 89.7 %copy-start.1 = (bf16[256,1536]{1,0:T(8,128)(2,1)S(1)}, bf16[256,1536]{1,0:T(8,128)(2,1)}, u32[]{:S(2)}) copy-start(bf16[256,1536]{1,0:T(8,128)(2,1)} %get-tuple-element.114) | copy-start | bytes 2359300
  267.2 3.1 %copy-start = (f32[256,1536]{1,0:T(8,128)S(1)}, f32[256,1536]{1,0:T(8,128)}, u32[]{:S(2)}) copy-start(f32[256,1536]{1,0:T(8,128)} %get-tuple-element.115) | copy-start | bytes 4718596

commit v6 on v5

--- a/solution.py
+++ b/solution.py
@@ -1331,7 +1331,6 @@
     prefetch(1, 1)
     x_tiles(3, 5)
     stage(1, 1)
-    prefetch(2, 2)
     x_tiles(5, 6)
     pltpu.make_async_copy(full.at[0, :, tile_of(0)], w_in.at[0], w_sem.at[0]).start()
     for slot in range(2):
@@ -1340,38 +1339,39 @@
     for c in small_puts:
         c.wait()
     to_partner(0)
+    prefetch(0, 0)
     input_tiles(0, 3)
+    stage(0, 0)
+    prefetch(2, 2)
+    input_tiles(3, 6)
     stage(2, 2)
-    prefetch(0, 0)
+    prefetch(0, 1)
     later(2, 1, 0)
-    input_tiles(3, 6)
-    stage(0, 0)
-    prefetch(1, 2)
-    later(2, 1, 1)
     input_grad()
     vec_step(0)
+    stage(0, 1)
+    prefetch(1, 2)
+    vec_step(1)
     stage(1, 2)
-    prefetch(0, 1)
+    prefetch(0, 2)
     later(1, 1, 0)
+    later(2, 1, 1)
+    vec_step(2)
+    later(1, 1, 1)
     later(2, 1, 2)
     later(2, 0, 0)
-    vec_step(1)
-    stage(0, 1)
-    prefetch(0, 2)
-    later(1, 1, 1)
-    later(2, 0, 1)
-    vec_step(2)
+    vec_step(3)
     later(1, 1, 2)
     later(1, 0, 0)
-    later(2, 0, 2)
-    vec_step(3)
-    later(1, 0, 1)
     stage(0, 2)
     later(0, 1, 0)
     vec_step(4)
-    later(1, 0, 2)
+    later(2, 0, 1)
+    later(1, 0, 1)
     later(0, 1, 1)
     vec_step(5)
+    later(2, 0, 2)
+    later(1, 0, 2)
     later(0, 1, 2)
     later(0, 0, 0)
     vec_step(6)

time: 272 us -> 269 us (0.989)
  Pallas kernels: 269 us -> 266 us
where the time goes in v6:
time: 269 us
  Pallas kernels  266 us (99%)
    pallas_call x1, Pallas kernels, mid(): pl.pallas_call(mid_kernel, name='scan_and_gate', out_shape=[jax.ShapeDtyp...  177 us
    pallas_call x1, Pallas kernels, back(): pl.pallas_call(back_kernel, name='project_back', out_shape=[jax.ShapeDtyp...  85 us

profile of v6, /device:TPU:0, one launch (start us, length us, event | category | flops | bytes accessed | tf_op | source)
XLA Modules:
  0.0 268.8 jit_solution(306733492645615680)
XLA Ops:
  0.7 2.4 pack.1
  3.0 176.6 %scan_and_gate.1 = (f32[8,3072]{1,0:T(8,128)}, f32[8,1024]{1,0:T(8,128)}, f32[272,384]{1,0:T(8,128)}, f32[256,256]{1,0:T(8,128)}, f32[256,256]{1,0:T(8,128)}, /*...) custom-call(bf16[256,1536]{1,0:T(8,128)(2,1)} %refs_13_.1, ...), custom_call_target="tpu_custom_call" | custom-call | tf_op jit(solution)/shard_map/scan_and_gate/pallas_call | solution.py:936
  179.6 0.0 copy-start.1
  179.7 85.0 %project_back.1 = (bf16[1,2,4,2,96,3072]{5,4,3,2,1,0:T(8,128)(2,1)}, bf16[1,2,4,2,32,1024]{5,4,3,2,1,0:T(8,128)(2,1)}, f32[3,96,384]{2,1,0:T(8,128)}, f32[1,32,1...) custom-call(f32[272,384]{1,0:T(8,128)} %get-tuple-element.65.refs_0_, f32[256,256]{1,0:T(8,128)} %get-tuple-element.66.refs_1_, ...), custom_call_target="tpu_custom_call" | custom-call | tf_op jit(solution)/shard_map/project_back/pallas_call | solution.py:1403
  264.6 0.0 copy-start
  264.7 2.1 finish.1
  266.8 0.0 copy-done.1
  266.8 0.9 copy.33
  267.7 0.0 copy-done
  267.7 1.1 copy.34
Async XLA Ops:
  179.6 87.2 %copy-start.1 = (bf16[256,1536]{1,0:T(8,128)(2,1)S(1)}, bf16[256,1536]{1,0:T(8,128)(2,1)}, u32[]{:S(2)}) copy-start(bf16[256,1536]{1,0:T(8,128)(2,1)} %get-tuple-element.114) | copy-start | bytes 2359300
  264.6 3.1 %copy-start = (f32[256,1536]{1,0:T(8,128)S(1)}, f32[256,1536]{1,0:T(8,128)}, u32[]{:S(2)}) copy-start(f32[256,1536]{1,0:T(8,128)} %get-tuple-element.115) | copy-start | bytes 4718596
